TPU v7x, 512 devices: a whole 4x4x16 slice. The times are simulated.
512 devices in a mesh: sector: 64 (over y_lo, z, core), dof: 8 (over x, y_hi).
Axes of the slice: x: 4, y: 4 (y_hi: 2, y_lo: 2; y = y_hi * 2 + y_lo), z: 16, core: 2. Of those that a mesh axis runs over, the one named last changes fastest.
Arguments:
- wake_field: bfloat16 [64, 8, 14336], P('sector', None, 'dof'), may hold values from -6 to 6
- sector_basis: bfloat16 [64, 128, 14336], P('sector', None, 'dof'), may hold values from -0.046875 to 0.046875
- block_index: int32 [64, 256], P('sector'), may hold values from 0 to 63
- phase_index: int32 [64, 256], P('sector'), may hold values from 0 to 7
- mode_shapes: bfloat16 [64, 40, 128], P('sector'), may hold values from -0.5 to 0.5
- residual_flex: bfloat16 [64, 128, 128], P('sector'), may hold values from -0.5 to 0.5
- mode_omega: float32 [64, 40], P('sector'), may hold values from 0.2 to 2
- mode_zeta: float32 [64, 40], P('sector'), may hold values from 0.01 to 0.2
- stress_map: bfloat16 [64, 16384, 128], P('sector', 'dof'), may hold values from -0.5 to 0.5
Outputs:
- stress: bfloat16 [64, 16384, 256], P('sector', 'dof')
All inputs are finite; a program needn't handle non-finite values.
Results may differ from a plain program's by a relative error of at most 0.027.
Values may be sent and summed in bfloat16 or wider, within the bound.
No kernel may reach another device: no remote copies, remote signals or barrier semaphores. Data moves between devices by JAX's collectives and lax.ppermute only.
A program may use at most 64 MiB of HBM per device.

v0:
```python
import jax
import jax.numpy as jnp
from jax import lax
from jax.sharding import PartitionSpec as P


def fourier(count):
    row_ids = jnp.arange(count)[:, None]
    col_ids = jnp.arange(count)[None, :]
    freqs = (row_ids + 1) // 2
    angle = 2.0 * jnp.pi * (freqs * col_ids % count).astype(jnp.float32) / count
    table = jnp.where(row_ids % 2 == 1, jnp.cos(angle), jnp.sin(angle))
    table = jnp.where(row_ids == 0, jnp.ones_like(table), table)
    edges = (row_ids == 0) | (row_ids == count - 1)
    scale = jnp.where(edges, jnp.sqrt(1.0 / count), jnp.sqrt(2.0 / count)).astype(jnp.float32)
    return table * scale


def respond(force, omega, zeta):
    steps = force.shape[1]
    lag = (jnp.arange(steps)[:, None] - jnp.arange(steps)[None, :]).astype(jnp.float32)
    later = lag >= 0.0
    lag_pos = jnp.maximum(lag, 0.0)
    decay = (omega * zeta)[:, None, None]
    damped = (omega * jnp.sqrt(1.0 - zeta * zeta))[:, None, None]
    kernel = jnp.where(later[None], jnp.exp(-decay * lag_pos) * jnp.sin(damped * lag_pos), 0.0)
    return jnp.einsum("mts,ms->mt", kernel, force, precision=lax.Precision.HIGHEST)


def to_harmonics(forcing):
    table_f = fourier(lax.axis_size("sector"))
    mixed = jnp.einsum(
        "hs,snt->hnt",
        table_f,
        lax.all_to_all(forcing[None], "sector", split_axis=2, concat_axis=0, tiled=True).astype(
            jnp.float32
        ),
        precision=lax.Precision.HIGHEST,
    )
    return lax.all_to_all(
        mixed.astype(jnp.bfloat16), "sector", split_axis=0, concat_axis=2, tiled=True
    )[0]


def to_sectors(physical):
    table_f = fourier(lax.axis_size("sector"))
    mixed = jnp.einsum(
        "hs,hnt->snt",
        table_f,
        lax.all_to_all(physical[None], "sector", split_axis=2, concat_axis=0, tiled=True).astype(
            jnp.float32
        ),
        precision=lax.Precision.HIGHEST,
    )
    return lax.all_to_all(
        mixed.astype(jnp.bfloat16), "sector", split_axis=0, concat_axis=2, tiled=True
    )[0]


def local(
    wake_field,
    sector_basis,
    block_index,
    phase_index,
    mode_shapes,
    residual_flex,
    mode_omega,
    mode_zeta,
    stress_map,
):
    basis = sector_basis[0]
    partial_proj = jnp.einsum(
        "bpr,nr->bpn",
        lax.all_gather(wake_field, "sector", axis=0, tiled=True),
        basis,
        preferred_element_type=jnp.float32,
    )
    blocks, phases, width = partial_proj.shape
    partial_proj = partial_proj.reshape(blocks * phases, width)
    table = lax.psum(partial_proj.astype(jnp.bfloat16), "dof").astype(jnp.float32)
    table = table.astype(jnp.bfloat16)
    pairs = block_index[0] * phases + phase_index[0]
    onehot = (pairs[:, None] == jnp.arange(blocks * phases, dtype=jnp.int32)[None, :]).astype(
        jnp.bfloat16
    )
    forcing = jnp.einsum("pn,tp->nt", table, onehot, preferred_element_type=jnp.float32).astype(
        jnp.bfloat16
    )
    harmonic = to_harmonics(forcing)
    shapes = mode_shapes[0]
    modal_force = jnp.dot(shapes, harmonic, preferred_element_type=jnp.float32)
    omega = mode_omega[0]
    zeta = mode_zeta[0]
    group_parts = []
    for first in range(0, shapes.shape[0], 8):
        group_parts.append(
            respond(
                modal_force[first : first + 8], omega[first : first + 8], zeta[first : first + 8]
            )
        )
    amplitude = jnp.concatenate(group_parts, axis=0)
    physical = jnp.einsum(
        "mn,mt->nt", shapes.astype(jnp.float32), amplitude, precision=lax.Precision.HIGHEST
    )
    physical = (
        physical + jnp.dot(residual_flex[0], harmonic, preferred_element_type=jnp.float32)
    ).astype(jnp.bfloat16)
    sectoral = to_sectors(physical)
    stress = jnp.dot(stress_map[0], sectoral, preferred_element_type=jnp.float32).astype(
        jnp.bfloat16
    )
    return stress[None]


def solution(mesh):
    return jax.shard_map(
        local,
        mesh=mesh,
        in_specs=(
            P("sector", None, "dof"),
            P("sector", None, "dof"),
            P("sector", None),
            P("sector", None),
            P("sector", None, None),
            P("sector", None, None),
            P("sector", None),
            P("sector", None),
            P("sector", "dof", None),
        ),
        out_specs=P("sector", "dof", None),
        check_vma=False,
    )
```

profile of v0, /device:TPU:1, one launch (start us, length us, event | category | flops | bytes accessed | tf_op | source)
XLA Modules:
  0.0 381.1 jit_solution(5524477384957100548)
XLA Ops:
  6.5 0.0 copy-start
  6.5 0.0 all-gather.2.cloned.1.call-start
  6.5 0.7 all-gather.2.cloned.1.call-update
  7.3 0.0 all-reduce.2.cloned.1.call-start
  7.3 0.7 multiply_add_fusion
  8.0 0.0 copy-start.3
  8.0 0.0 copy-start.4
  8.0 0.0 copy-start.1
  8.0 129.2 %all-gather.2.cloned.1.call-done = bf16[64,8,1792]{2,1,0:T(8,128)(2,1)} async-done(((bf16[1,8,1792]{2,1,0:T(8,128)(2,1)}), bf16[64,8,1792]{2,1,0:T(8,128)(2,1)}) %all-gather.2.cloned.1.call-update) | async-done | bytes 1835024 | tf_op jit(solution)/shard_map/all_gather | solution.py:74
  137.2 2.9 fusion.38
  140.1 0.0 copy-start.2
  140.1 0.0 all-reduce.2.cloned.1.call-update
  140.1 89.6 %all-reduce.2.cloned.1.call-done = bf16[512,128]{1,0:T(8,128)(2,1)} async-done(((bf16[512,128]{1,0:T(8,128)(2,1)}), bf16[512,128]{1,0:T(8,128)(2,1)}) %all-reduce.2.cloned.1.call-update) | async-done | bytes 131088 | tf_op jit(solution)/shard_map/psum | solution.py:80
  229.8 1.2 fusion.42
  231.0 0.1 copy.28
  231.1 0.6 broadcast.204
  231.7 1.0 reduce
  232.7 0.7 reshape.247
  233.4 18.8 %all-to-all-start = ((bf16[64,2,256]{2,1,0:T(2,128)(2,1)}), bf16[64,2,256]{2,1,0:T(2,128)(2,1)S(1)}, u32[]{:S(2)}, u32[]{:S(2)}) async-start(bf16[64,2,256]{2,1,0:T(2,128)(2,1)} %reshape.247), calls=%async_computation | async-start | bytes 131072 | tf_op jit(solution)/shard_map/all_to_all | solution.py:35
  252.2 0.0 copy-done.3
  252.2 0.0 copy-done.4
  252.2 0.1 fusion.98
  252.3 14.5 %all-to-all-done = bf16[64,2,256]{2,1,0:T(2,128)(2,1)S(1)} async-done(((bf16[64,2,256]{2,1,0:T(2,128)(2,1)}), bf16[64,2,256]{2,1,0:T(2,128)(2,1)S(1)}, u32[]{:S(2)}, u32[]{:S(2)}) %all-to-all-start) | async-done | bytes 65568 | tf_op jit(solution)/shard_map/all_to_all | solution.py:35
  266.8 0.1 reshape.248
  266.8 0.4 convolution_convert_fusion.2
  267.2 0.7 copy.31
  267.9 4.6 %all-to-all-start.1 = ((bf16[64,128,4]{1,2,0:T(4,128)(2,1)}), bf16[64,128,4]{1,2,0:T(4,128)(2,1)S(1)}, u32[]{:S(2)}, u32[]{:S(2)}) async-start(bf16[64,128,4]{1,2,0:T(4,128)(2,1)} %copy.31), calls=%async_computation.1 | async-start | bytes 131072 | tf_op jit(solution)/shard_map/all_to_all | solution.py:40
  272.6 0.1 convert_compare_fusion
  272.6 0.1 fusion.94
  272.7 14.4 %all-to-all-done.1 = bf16[64,128,4]{1,2,0:T(4,128)(2,1)S(1)} async-done(((bf16[64,128,4]{1,2,0:T(4,128)(2,1)}), bf16[64,128,4]{1,2,0:T(4,128)(2,1)S(1)}, u32[]{:S(2)}, u32[]{:S(2)}) %all-to-all-start.1) | async-done | bytes 65568 | tf_op jit(solution)/shard_map/all_to_all | solution.py:40
  287.1 0.0 copy-done.1
  287.1 0.2 convolution_bitcast_fusion
  287.3 0.0 copy-done.2
  287.3 0.2 fusion.79
  287.5 9.1 %fusion.29 = f32[8,1,256]{2,1,0:T(1,128)S(1)} fusion(f32[8]{0:T(128)S(1)} %get-tuple-element.11, f32[256,256]{1,0:T(8,128)S(1)} %convert_maximum_fusion, f32[8]{0:T(128)S(1)} %get-tuple-element.18, pred[256,256]{1,0:T(8,128)(4,1)S(1)} %convert_compare_fusion, f32[8,256,1]{1,0,2:T(8,128)S(1)} %get-tuple-element.9), kind=kOutput, calls=%fused_computation.30 | convolution fusion | flops 8388608 | bytes 344128 | tf_op jit(solution)/shard_map/mts,ms->mt/dot_general | solution.py:27
  296.5 9.3 %fusion.22 = f32[8,1,256]{2,1,0:T(1,128)S(1)} fusion(f32[8]{0:T(128)S(1)} %get-tuple-element.12, f32[8]{0:T(128)S(1)} %get-tuple-element.17, f32[256,256]{1,0:T(8,128)S(1)} %convert_maximum_fusion, pred[256,256]{1,0:T(8,128)(4,1)S(1)} %convert_compare_fusion, f32[8,256,1]{1,0,2:T(8,128)S(1)} %get-tuple-element.8), kind=kOutput, calls=%fused_computation.23 | convolution fusion | flops 8388608 | bytes 344128 | tf_op jit(solution)/shard_map/mts,ms->mt/dot_general | solution.py:27
  305.8 9.5 %fusion.15 = f32[8,1,256]{2,1,0:T(1,128)S(1)} fusion(f32[8]{0:T(128)S(1)} %get-tuple-element.13, f32[8]{0:T(128)S(1)} %get-tuple-element.16, f32[256,256]{1,0:T(8,128)S(1)} %convert_maximum_fusion, pred[256,256]{1,0:T(8,128)(4,1)S(1)} %convert_compare_fusion, f32[8,256,1]{1,0,2:T(8,128)S(1)} %get-tuple-element.7), kind=kOutput, calls=%fused_computation.16 | convolution fusion | flops 8388608 | bytes 344128 | tf_op jit(solution)/shard_map/mts,ms->mt/dot_general | solution.py:27
  315.4 9.3 %fusion.8 = f32[8,1,256]{2,1,0:T(1,128)S(1)} fusion(f32[8]{0:T(128)S(1)} %get-tuple-element.14, f32[8]{0:T(128)S(1)} %fusion.98, f32[256,256]{1,0:T(8,128)S(1)} %convert_maximum_fusion, pred[256,256]{1,0:T(8,128)(4,1)S(1)} %convert_compare_fusion, f32[8,256,1]{1,0,2:T(8,128)S(1)} %get-tuple-element.6), kind=kOutput, calls=%fused_computation.9 | convolution fusion | flops 8388608 | bytes 344128 | tf_op jit(solution)/shard_map/mts,ms->mt/dot_general | solution.py:27
  324.6 9.1 %fusion.1 = f32[8,1,256]{2,1,0:T(1,128)S(1)} fusion(f32[8]{0:T(128)S(1)} %get-tuple-element.15, f32[8]{0:T(128)S(1)} %get-tuple-element.10, f32[256,256]{1,0:T(8,128)S(1)} %convert_maximum_fusion, pred[256,256]{1,0:T(8,128)(4,1)S(1)} %convert_compare_fusion, f32[8,256,1]{1,0,2:T(8,128)S(1)} %get-tuple-element.5), kind=kOutput, calls=%fused_computation.2 | convolution fusion | flops 8388608 | bytes 344128 | tf_op jit(solution)/shard_map/mts,ms->mt/dot_general | solution.py:27
  333.7 0.3 fusion.43
  334.1 0.1 copy.74
  334.2 1.0 reduce.1
  335.2 18.3 %all_to_all.66 = bf16[64,2,256]{2,1,0:T(2,128)(2,1)S(1)} all-to-all(bf16[64,2,256]{2,1,0:T(2,128)(2,1)S(1)} %reshape.249), channel_id=1, replica_groups=mesh['sector'=64,'dof'=8] {'sector'}, dimensions={0} | all-to-all | bytes 131072 | tf_op jit(solution)/shard_map/all_to_all | solution.py:50
  353.5 0.1 reshape.250
  353.6 0.3 convolution_convert_fusion.1
  354.0 0.1 copy.34
  354.0 18.3 %all_to_all.67 = bf16[64,128,4]{1,2,0:T(4,128)(2,1)S(1)} all-to-all(bf16[64,128,4]{1,2,0:T(4,128)(2,1)S(1)} %copy.34), channel_id=1, replica_groups=mesh['sector'=64,'dof'=8] {'sector'}, dimensions={0} | all-to-all | bytes 131072 | tf_op jit(solution)/shard_map/all_to_all | solution.py:55
  372.3 0.0 copy-done
  372.3 0.4 fusion
  372.8 1.3 copy.35
  (13 shorter events, 0.2 us)
Async XLA Ops:
  6.5 365.8 %copy-start = (bf16[1,2048,128]{2,1,0:T(8,128)(2,1)S(1)}, bf16[1,2048,128]{2,1,0:T(8,128)(2,1)}, u32[]{:S(2)}) copy-start(bf16[1,2048,128]{2,1,0:T(8,128)(2,1)} %param.17) | copy-start | bytes 1572868
  6.5 130.7 %all-gather.2.cloned.1.call-start = ((), (), s32[]{:S(2)}) async-start(), calls=%async_computation.4 | async-start | bytes 1863680 | tf_op jit(solution)/shard_map/all_gather | solution.py:74
  7.3 222.5 %all-reduce.2.cloned.1.call-start = ((), (), s32[]{:S(2)}) async-start(), calls=%async_computation.5 | async-start | bytes 262144 | tf_op jit(solution)/shard_map/psum | solution.py:80
  8.0 244.2 %copy-start.3 = (f32[1,40]{1,0:T(1,128)S(1)}, f32[1,40]{1,0:T(1,128)}, u32[]{:S(2)}) copy-start(f32[1,40]{1,0:T(1,128)} %param.16) | copy-start | bytes 484
  8.0 244.2 %copy-start.4 = (f32[1,40]{1,0:T(1,128)S(1)}, f32[1,40]{1,0:T(1,128)}, u32[]{:S(2)}) copy-start(f32[1,40]{1,0:T(1,128)} %param.15) | copy-start | bytes 484
  8.0 279.1 %copy-start.1 = (bf16[1,40,128]{2,1,0:T(8,128)(2,1)S(1)}, bf16[1,40,128]{2,1,0:T(8,128)(2,1)}, u32[]{:S(2)}) copy-start(bf16[1,40,128]{2,1,0:T(8,128)(2,1)} %param.13) | copy-start | bytes 30724
  140.1 147.2 %copy-start.2 = (bf16[1,128,128]{2,1,0:T(8,128)(2,1)S(1)}, bf16[1,128,128]{2,1,0:T(8,128)(2,1)}, u32[]{:S(2)}) copy-start(bf16[1,128,128]{2,1,0:T(8,128)(2,1)} %param.14) | copy-start | bytes 98308
  233.4 33.4 %all-to-all-start = ((bf16[64,2,256]{2,1,0:T(2,128)(2,1)}), bf16[64,2,256]{2,1,0:T(2,128)(2,1)S(1)}, u32[]{:S(2)}, u32[]{:S(2)}) async-start(bf16[64,2,256]{2,1,0:T(2,128)(2,1)} %reshape.247), calls=%async_computation | async-start | bytes 131072 | tf_op jit(solution)/shard_map/all_to_all | solution.py:35
  267.9 19.2 %all-to-all-start.1 = ((bf16[64,128,4]{1,2,0:T(4,128)(2,1)}), bf16[64,128,4]{1,2,0:T(4,128)(2,1)S(1)}, u32[]{:S(2)}, u32[]{:S(2)}) async-start(bf16[64,128,4]{1,2,0:T(4,128)(2,1)} %copy.31), calls=%async_computation.1 | async-start | bytes 131072 | tf_op jit(solution)/shard_map/all_to_all | solution.py:40
Sparse Core Ops, SparseCore 0:
  9.5 127.6 all-gather.1
  140.2 89.5 all-reduce.1
where the time goes:
time: 385 us; the launch traced here: 381 us
  waiting for transfers between devices  248 us (64%)
  matrix products  52.1 us (14%)
  blocking collectives  36.7 us (10%)
  starting transfers between devices  23.5 us (6%)
  between operations  13.8 us (4%)
    all_gather x1, waiting for transfers between devices, local(): lax.all_gather(wake_field, 'sector', axis=0, tiled=True)  129 us
    psum x1, waiting for transfers between devices, local(): lax.psum(partial_proj.astype(jnp.bfloat16), 'dof').astype(jnp.float32)  89.6 us
    dot_general x5, matrix products, respond(): jnp.einsum('mts,ms->mt', kernel, force, precision=lax.Precision.HIGHEST)  46.2 us
    all_to_all x1, starting transfers between devices, to_harmonics(): lax.all_to_all(forcing[None], 'sector', split_axis=2, concat_axis=0, tile...  18.8 us
    all_to_all x1, blocking collectives, to_sectors(): lax.all_to_all(physical[None], 'sector', split_axis=2, concat_axis=0, til...  18.3 us
    all_to_all x1, blocking collectives, to_sectors(): lax.all_to_all(mixed.astype(jnp.bfloat16), 'sector', split_axis=0, concat...  18.3 us
    all_to_all x1, waiting for transfers between devices, to_harmonics(): lax.all_to_all(forcing[None], 'sector', split_axis=2, concat_axis=0, tile...  14.5 us
    all_to_all x1, waiting for transfers between devices, to_harmonics(): lax.all_to_all(mixed.astype(jnp.bfloat16), 'sector', split_axis=0, concat...  14.4 us
  transfers between devices with their start and end apart: 4, of which 4 were waited for; matrix products, arithmetic and copies ran while one was open for 0% of the time, Pallas kernels for 0%

commit v1 on v0

v1 whole, which is shorter than its diff:
```python
import numpy as np
import jax
import jax.numpy as jnp
from jax import lax
from jax.experimental import pallas as pl
from jax.experimental.pallas import tpu as pltpu
from jax.sharding import Mesh, PartitionSpec as P

AXES = ("yl", "z", "c", "x", "yh")
SIZES = (2, 16, 2, 4, 2)
PLANE = ("yl", "c", "x", "yh")
YL, Z, C, D = 2, 16, 2, 8
PEERS = YL * C * D
BLADES, PH, NT, NB, MODES = YL * Z * C, 8, 256, 128, 40
HALF = 896
TS = NT // PEERS
TD = NT // D
BF = jnp.bfloat16
F32 = jnp.float32
HI = lax.Precision.HIGHEST


def fourier_table(count):
    h = np.arange(count)[:, None]
    s = np.arange(count)[None, :]
    angle = 2.0 * np.pi * ((((h + 1) // 2) * s) % count) / count
    table = np.where(h % 2 == 1, np.cos(angle), np.sin(angle))
    table = np.where(h == 0, 1.0, table)
    edges = (h == 0) | (h == count - 1)
    return table * np.where(edges, np.sqrt(1.0 / count), np.sqrt(2.0 / count))


FOURIER = fourier_table(BLADES)
FORWARD = np.ascontiguousarray(
    FOURIER.reshape(YL, Z, C, YL, Z, C).transpose(1, 4, 3, 5, 0, 2).reshape(Z, 1, 256)
).astype(np.float32)
INVERSE = np.ascontiguousarray(
    FOURIER.reshape(YL, Z, C, YL, Z, C).transpose(0, 2, 4, 1, 3, 5).reshape(YL * C * Z, 1, 64)
).astype(np.float32)


def dot_nt(a, b, **kw):
    return lax.dot_general(
        a, b, (((1,), (1,)), ((), ())), preferred_element_type=F32, **kw
    )


def project_kernel(pos, own_ref, other_ref, mine_ref, got_ref, index_ref, out_ref):
    core = pos[1]
    basis = jnp.concatenate([mine_ref[...], got_ref[0:NB, :]], axis=0)
    table = [
        dot_nt(ref[...].reshape(YL * Z * PH, HALF), basis).astype(BF)
        for ref in (own_ref, other_ref)
    ]
    pair = lax.broadcasted_iota(jnp.int32, (NT, YL * Z * PH), 1).astype(F32)
    theirs = got_ref[NB : NB + 16, 0:NT].astype(F32)
    picks = []
    for r in range(2):
        if r == 0:
            block, phase = index_ref[0:1, :], index_ref[1:2, :]
        else:
            block = theirs[0:1, :].astype(jnp.int32)
            phase = theirs[1:2, :].astype(jnp.int32)
        code = ((block >> 1) * PH + phase).astype(F32)
        here = (block & 1) == core
        codes = jnp.concatenate(
            [jnp.where(here, code, -1.0), jnp.where(here, -1.0, code)]
            + [jnp.zeros((6, NT), F32)],
            axis=0,
        ).T
        total = jnp.zeros((NT, NB), F32)
        for k in range(2):
            onehot = jnp.where(codes[:, k : k + 1] == pair, 1.0, 0.0).astype(BF)
            total += jnp.dot(
                onehot, table[k][:, r * NB : (r + 1) * NB], preferred_element_type=F32
            )
        picks.append(total.reshape(PEERS, TS, NB))
    out_ref[...] = jnp.concatenate(picks, axis=1).astype(BF)


def gather_sum_kernel(in_ref, out_ref):
    sums = {}
    for yl in range(YL):
        for c in range(C):
            total = None
            for d in range(D):
                part = in_ref[(yl * C + c) * D + d].astype(F32)
                total = part if total is None else total + part
            sums[yl, c] = total
    rows = [
        sums[yl, c][0:TS] + sums[1 - yl, c][TS : 2 * TS] for yl in range(YL) for c in range(C)
    ]
    block = jnp.concatenate(rows, axis=0).astype(BF)
    out_ref[...] = jnp.broadcast_to(block[None], out_ref.shape)


def forward_kernel(pos, table_ref, in_ref, out_ref):
    acc = [None] * 4
    for z in range(Z):
        block = in_ref[z].astype(F32)
        for q in range(4):
            part = block[q * TS : (q + 1) * TS]
            for h in range(4):
                term = part * table_ref[0, 0, (z * 4 + q) * 4 + h]
                acc[h] = term if acc[h] is None else acc[h] + term
    for h in range(4):
        out_ref[h * D : (h + 1) * D] = jnp.broadcast_to(acc[h].astype(BF)[None], (D, TS, NB))


def modal_kernel(pos, in_ref, shapes_ref, flex_ref, damp_ref, out_ref, hold_ref):
    force = in_ref[...].reshape(NT, NB)
    shapes = shapes_ref[...]
    real = dot_nt(shapes, force)
    imag = None
    damp = jnp.concatenate([damp_ref[...], jnp.zeros((6, MODES), F32)], axis=0).T
    omega, zeta = damp[:, 0:1], damp[:, 1:2]
    size = jnp.exp(-omega * zeta)
    angle = omega * jnp.sqrt(1.0 - zeta * zeta)
    pr, pi = size * jnp.cos(angle), size * jnp.sin(angle)
    lane = lax.broadcasted_iota(jnp.int32, (MODES, NT), 1)
    shift = 1
    while shift < NT:
        keep = lane >= shift
        sr = jnp.where(keep, pltpu.roll(real, shift, 1), 0.0)
        if imag is None:
            real, imag = real + pr * sr, pi * sr
        else:
            si = jnp.where(keep, pltpu.roll(imag, shift, 1), 0.0)
            real, imag = real + (pr * sr - pi * si), imag + (pr * si + pi * sr)
        pr, pi = pr * pr - pi * pi, 2.0 * pr * pi
        shift *= 2
    hold_ref[...] = lax.dot_general(
        imag,
        shapes.astype(F32),
        (((0,), (0,)), ((), ())),
        precision=HI,
        preferred_element_type=F32,
    ) + dot_nt(force, flex_ref[...])
    block = hold_ref[pl.ds(pl.multiple_of(pos[2] * TD, TD), TD), :].astype(BF)
    out_ref[...] = jnp.broadcast_to(block[None], out_ref.shape)


def inverse_kernel(pos, table_ref, in_ref, out_ref):
    acc = [None] * 4
    for z in range(Z):
        block = in_ref[z].astype(F32)
        for s in range(4):
            term = block * table_ref[0, 0, z * 4 + s]
            acc[s] = term if acc[s] is None else acc[s] + term
    for s in range(4):
        out_ref[s * D : (s + 1) * D] = jnp.broadcast_to(acc[s].astype(BF)[None], (D, TD, NB))


def stress_kernel(in_ref, map_ref, out_ref, motion_ref):
    @pl.when(pl.program_id(0) == 0)
    def _():
        total = None
        for q in range(YL * C):
            part = in_ref[q * D : (q + 1) * D].astype(F32)
            total = part if total is None else total + part
        motion_ref[...] = total.reshape(NT, NB).astype(BF)

    out_ref[...] = dot_nt(map_ref[...], motion_ref[...]).astype(BF)


def whole(shape):
    return pl.BlockSpec(shape, lambda *_: (0,) * len(shape))


def call(kernel, pos, out, in_specs, *args, scratch=()):
    return pl.pallas_call(
        kernel,
        out_shape=jax.ShapeDtypeStruct(out, BF),
        grid_spec=pltpu.PrefetchScalarGridSpec(
            num_scalar_prefetch=1,
            grid=(1,),
            in_specs=in_specs,
            out_specs=whole(out),
            scratch_shapes=list(scratch),
        ),
        compiler_params=pltpu.CompilerParams(vmem_limit_bytes=24 * 1024 * 1024),
    )(pos, *args)


def local(wake, basis, block_index, phase_index, shapes, flex, omega, zeta, stress_map):
    yl, z, c = lax.axis_index("yl"), lax.axis_index("z"), lax.axis_index("c")
    d = lax.axis_index("x") * 2 + lax.axis_index("yh")
    pos = jnp.stack([yl, c, d, z, (yl * C + c) * Z + z]).astype(jnp.int32)
    index = jnp.concatenate([block_index, phase_index], axis=0)

    send = lax.dynamic_slice(basis[0], (0, (1 - yl) * HALF), (NB, HALF))
    send = jnp.concatenate([send, jnp.pad(index.astype(BF), ((0, 14), (0, HALF - NT)))], axis=0)
    got = lax.ppermute(send, "yl", [(0, 1), (1, 0)])

    mine = jnp.transpose(wake[0].reshape(PH, YL, HALF), (1, 0, 2))
    mine = jnp.broadcast_to(mine[:, None], (YL, Z, PH, HALF)).reshape(YL * Z, PH, HALF)
    own = lax.all_to_all(mine, ("yl", "z"), 0, 0, tiled=True)
    other = lax.ppermute(own, "c", [(0, 1), (1, 0)])

    picked = call(
        project_kernel,
        pos,
        (PEERS, 2 * TS, NB),
        [
            whole((YL * Z, PH, HALF)),
            whole((YL * Z, PH, HALF)),
            pl.BlockSpec((NB, HALF), lambda i, p: (0, p[0])),
            whole((NB + 16, HALF)),
            whole((2, NT)),
        ],
        own,
        other,
        basis[0],
        got,
        index,
    )
    parts = lax.all_to_all(picked, PLANE, 0, 0, tiled=True)
    forcing = pl.pallas_call(
        gather_sum_kernel, out_shape=jax.ShapeDtypeStruct((Z, 4 * TS, NB), BF)
    )(parts)
    forcing = lax.all_to_all(forcing, "z", 0, 0, tiled=True)
    harmonic = call(
        forward_kernel,
        pos,
        (PEERS, TS, NB),
        [
            pl.BlockSpec((1, 1, 256), lambda i, p: (p[3], 0, 0), memory_space=pltpu.SMEM),
            whole((Z, 4 * TS, NB)),
        ],
        jnp.asarray(FORWARD),
        forcing,
    )
    harmonic = lax.all_to_all(harmonic, PLANE, 0, 0, tiled=True)
    physical = call(
        modal_kernel,
        pos,
        (Z, TD, NB),
        [whole((PEERS, TS, NB)), whole((MODES, NB)), whole((NB, NB)), whole((2, MODES))],
        harmonic,
        shapes[0],
        flex[0],
        jnp.concatenate([omega, zeta], axis=0),
        scratch=[pltpu.VMEM((NT, NB), F32)],
    )
    physical = lax.all_to_all(physical, "z", 0, 0, tiled=True)
    sectoral = call(
        inverse_kernel,
        pos,
        (PEERS, TD, NB),
        [
            pl.BlockSpec((1, 1, 64), lambda i, p: (p[4], 0, 0), memory_space=pltpu.SMEM),
            whole((Z, TD, NB)),
        ],
        jnp.asarray(INVERSE),
        physical,
    )
    sectoral = lax.all_to_all(sectoral, PLANE, 0, 0, tiled=True)
    rows = stress_map.shape[1]
    step = rows // 4
    stress = pl.pallas_call(
        stress_kernel,
        out_shape=jax.ShapeDtypeStruct((rows, NT), BF),
        grid=(rows // step,),
        in_specs=[
            whole((PEERS, TD, NB)),
            pl.BlockSpec((step, NB), lambda i: (i, 0)),
        ],
        out_specs=pl.BlockSpec((step, NT), lambda i: (i, 0)),
        scratch_shapes=[pltpu.VMEM((NT, NB), BF)],
    )(sectoral, stress_map[0])
    return stress[None]


def solution(mesh):
    sector, dof = ("yl", "z", "c"), ("x", "yh")
    return jax.shard_map(
        local,
        mesh=Mesh(mesh.devices.reshape(SIZES), AXES),
        in_specs=(
            P(sector, None, dof),
            P(sector, None, dof),
            P(sector, None),
            P(sector, None),
            P(sector, None, None),
            P(sector, None, None),
            P(sector, None),
            P(sector, None),
            P(sector, dof, None),
        ),
        out_specs=P(sector, dof, None),
        check_vma=False,
    )
```

time: 385 us -> 150 us (0.39)
  waiting for transfers between devices: 248 us -> 42 us
  matrix products: 52.1 us -> 0 us
  blocking collectives: 36.7 us -> 63.9 us
  between operations: 13.8 us -> 0.18 us
  Pallas kernels: 0 us -> 11.5 us
  starting transfers between devices: 23.5 us -> 29.9 us
    all_gather x1 -> x0, waiting for transfers between devices: 129 us -> none  [local(): lax.all_gather(wake_field, 'sector', axis=0, tiled=True)]
    psum x1 -> x0, waiting for transfers between devices: 89.6 us -> none  [local(): lax.psum(partial_proj.astype(jnp.bfloat16), 'dof').astype(jnp.float32)]
    dot_general x13 -> x0, matrix products: 52.1 us -> none  [the longest x5 46.2 us: respond(): jnp.einsum('mts,ms->mt', kernel, force, precision=lax.Precision.HIGHEST)]
    all_to_all x2 -> x4, blocking collectives: 36.7 us -> 63.9 us  [the longest x1 16.9 us: local(): forcing = lax.all_to_all(forcing, 'z', 0, 0, tiled=True)]
    pallas_call x0 -> x6, Pallas kernels: none -> 11.5 us  [the longest x4 6.08 us: call(): pl.pallas_call(kernel, out_shape=jax.ShapeDtypeStruct(out, BF), grid_spec...]
    ppermute x0 -> x2, waiting for transfers between devices: none -> 6.97 us  [the longest x1 6.97 us: local(): got = lax.ppermute(send, 'yl', [(0, 1), (1, 0)])]
    ppermute x0 -> x2, starting transfers between devices: none -> 6.24 us  [the longest x1 3.58 us: local(): other = lax.ppermute(own, 'c', [(0, 1), (1, 0)])]
    all_to_all x2, waiting for transfers between devices: 28.9 us -> 35 us  [the longest x1 27.8 us: local(): own = lax.all_to_all(mine, ('yl', 'z'), 0, 0, tiled=True)]
  transfers between devices with their start and end apart: 4 -> 4, of which waited for: 4 -> 3; matrix products, arithmetic and copies ran while one was open for 0% -> 0% of each run, Pallas kernels for 0% -> 0%
where the time goes in v1:
time: 150 us; the launch traced here: 149 us
  blocking collectives  63.9 us (43%)
  waiting for transfers between devices  42 us (28%)
  starting transfers between devices  29.9 us (20%)
  Pallas kernels  11.5 us (8%)
  local copies, waits for them, and re-layouts  1.7 us (1%)
    all_to_all x1, waiting for transfers between devices, local(): own = lax.all_to_all(mine, ('yl', 'z'), 0, 0, tiled=True)  27.8 us
    all_to_all x1, starting transfers between devices, local(): own = lax.all_to_all(mine, ('yl', 'z'), 0, 0, tiled=True)  17.2 us
    all_to_all x1, blocking collectives, local(): forcing = lax.all_to_all(forcing, 'z', 0, 0, tiled=True)  16.9 us
    all_to_all x1, blocking collectives, local(): physical = lax.all_to_all(physical, 'z', 0, 0, tiled=True)  15.9 us
    all_to_all x1, blocking collectives, local(): sectoral = lax.all_to_all(sectoral, PLANE, 0, 0, tiled=True)  15.8 us
    all_to_all x1, blocking collectives, local(): parts = lax.all_to_all(picked, PLANE, 0, 0, tiled=True)  15.2 us
    all_to_all x1, waiting for transfers between devices, local(): harmonic = lax.all_to_all(harmonic, PLANE, 0, 0, tiled=True)  7.22 us
    ppermute x1, waiting for transfers between devices, local(): got = lax.ppermute(send, 'yl', [(0, 1), (1, 0)])  6.97 us
  transfers between devices with their start and end apart: 4, of which 3 were waited for; matrix products, arithmetic and copies ran while one was open for 0% of the time, Pallas kernels for 0%

profile of v1, /device:TPU:1, one launch (start us, length us, event | category | flops | bytes accessed | tf_op | source)
XLA Modules:
  0.0 149.2 jit_solution(7276531995334374927)
XLA Ops:
  0.0 1.5 %broadcast_in_dim.4 = bf16[2,16,8,896]{3,2,1,0:T(8,128)(2,1)} broadcast(bf16[2,8,896]{2,1,0:T(8,128)(2,1)} %bitcast.20), dimensions={0,2,3} | broadcast | bytes 487424 | tf_op jit(solution)/shard_map/broadcast_in_dim | solution.py:196
  1.5 0.0 copy-start
  1.6 17.2 %all-to-all-start = ((bf16[32,8,896]{2,1,0:T(8,128)(2,1)}), bf16[32,8,896]{2,1,0:T(8,128)(2,1)S(1)}, u32[]{:S(2)}, u32[]{:S(2)}) async-start(bf16[32,8,896]{2,1,0:T(8,128)(2,1)} %bitcast.7), calls=%async_computation | async-start | bytes 917504 | tf_op jit(solution)/shard_map/all_to_all | solution.py:197
  18.7 0.0 copy-done
  18.7 0.0 copy-start.5
  18.8 0.0 copy-start.6
  18.8 27.8 %all-to-all-done.own_ref = bf16[32,8,896]{2,1,0:T(8,128)(2,1)S(1)} async-done(((bf16[32,8,896]{2,1,0:T(8,128)(2,1)}), bf16[32,8,896]{2,1,0:T(8,128)(2,1)S(1)}, u32[]{:S(2)}, u32[]{:S(2)}) %all-to-all-start) | async-done | bytes 458784 | tf_op jit(solution)/shard_map/all_to_all | solution.py:197
  46.6 3.6 %collective-permute-start = (bf16[32,8,896]{2,1,0:T(8,128)(2,1)S(1)}, bf16[32,8,896]{2,1,0:T(8,128)(2,1)S(1)}, u32[]{:S(2)}, u32[]{:S(2)}) collective-permute-start(bf16[32,8,896]{2,1,0:T(8,128)(2,1)S(1)} %all-to-all-done.own_ref), channel_id=1, source_target_pairs={{0,8},{8,0},{1,9},{9,1},{2,10},{10,2},{3,11},{11,3},{4,12},{12,4},... | collective-permute-start | bytes 1376264 | tf_op jit(solution)/shard_map/ppermute | solution.py:198
  50.2 0.0 copy-done.5
  50.2 0.0 copy-done.6
  50.3 2.7 %collective-permute-start.1 = (bf16[144,896]{1,0:T(8,128)(2,1)S(1)}, bf16[144,896]{1,0:T(8,128)(2,1)S(1)}, u32[]{:S(2)}, u32[]{:S(2)}) collective-permute-start(bf16[144,896]{1,0:T(8,128)(2,1)S(1)} %fusion.1), channel_id=1, source_target_pairs={{0,256},{256,0},{1,257},{257,1},{2,258},{258,2},{3,259},{259,3},{4... | collective-permute-start | bytes 774152 | tf_op jit(solution)/shard_map/ppermute | solution.py:193
  53.0 0.1 stack.23.pos
  53.0 7.0 %collective-permute-done.1.got_ref = bf16[144,896]{1,0:T(8,128)(2,1)S(1)} collective-permute-done((bf16[144,896]{1,0:T(8,128)(2,1)S(1)}, bf16[144,896]{1,0:T(8,128)(2,1)S(1)}, u32[]{:S(2)}, u32[]{:S(2)}) %collective-permute-start.1) | collective-permute-done | bytes 258080 | tf_op jit(solution)/shard_map/ppermute | solution.py:193
  60.0 0.0 collective-permute-done.other_ref
  60.0 1.4 shard_map.109
  61.4 15.2 %all_to_all.30.in_ref = bf16[32,16,128]{2,1,0:T(8,128)(2,1)} all-to-all(bf16[32,16,128]{2,1,0:T(8,128)(2,1)S(1)} %shard_map.109), channel_id=1, replica_groups=mesh['yl'=2,'z'=16,'c'=2,'x'=4,'yh'=2] {'yl','c','x','yh'}, dimensions={0} | all-to-all | bytes 262144 | tf_op jit(solution)/shard_map/all_to_all | solution.py:217
  76.6 1.6 %shard_map.110 = bf16[16,32,128]{2,1,0:T(8,128)(2,1)} custom-call(bf16[32,16,128]{2,1,0:T(8,128)(2,1)} %all_to_all.30.in_ref), custom_call_target="tpu_custom_call" | custom-call | tf_op jit(solution)/shard_map/pallas_call | solution.py:218
  78.2 0.0 copy-start.3
  78.2 16.9 %all_to_all.31.in_ref = bf16[16,32,128]{2,1,0:T(8,128)(2,1)S(1)} all-to-all(bf16[16,32,128]{2,1,0:T(8,128)(2,1)} %shard_map.110), channel_id=1, replica_groups=mesh['yl'=2,'z'=16,'c'=2,'x'=4,'yh'=2] {'z'}, dimensions={0} | all-to-all | bytes 262144 | tf_op jit(solution)/shard_map/all_to_all | solution.py:221
  95.1 0.0 copy-done.3
  95.1 1.9 %shard_map.111 = bf16[32,8,128]{2,1,0:T(8,128)(2,1)} custom-call(s32[5]{0:T(128)S(1)} %stack.23.pos, f32[16,1,256]{2,1,0:T(1,128)S(1)} %copy-done.3, bf16[16,32,128]{2,1,0:T(8,128)(2,1)S(1)} %all_to_all.31.in_ref), custom_call_target="tpu_custom_call" | custom-call | tf_op jit(solution)/shard_map/pallas_call | solution.py:171
  97.0 0.0 copy-start.7
  97.0 0.0 copy-start.8
  97.0 0.0 copy-start.1
  97.0 0.0 copy-start.4
  97.0 6.5 %all-to-all-start.3 = ((bf16[32,8,128]{2,1,0:T(8,128)(2,1)}), bf16[32,8,128]{2,1,0:T(8,128)(2,1)S(1)}, u32[]{:S(2)}, u32[]{:S(2)}) async-start(bf16[32,8,128]{2,1,0:T(8,128)(2,1)} %shard_map.111), calls=%async_computation.3 | async-start | bytes 131072 | tf_op jit(solution)/shard_map/all_to_all | solution.py:233
  103.6 0.0 copy-done.7
  103.6 0.0 copy-done.8
  103.6 7.2 %all-to-all-done.3.in_ref = bf16[32,8,128]{2,1,0:T(8,128)(2,1)S(1)} async-done(((bf16[32,8,128]{2,1,0:T(8,128)(2,1)}), bf16[32,8,128]{2,1,0:T(8,128)(2,1)S(1)}, u32[]{:S(2)}, u32[]{:S(2)}) %all-to-all-start.3) | async-done | bytes 65568 | tf_op jit(solution)/shard_map/all_to_all | solution.py:233
  110.8 0.0 copy-done.1
  110.8 0.0 copy-done.4
  110.8 1.7 %shard_map.112 = bf16[16,32,128]{2,1,0:T(8,128)(2,1)S(1)} custom-call(s32[5]{0:T(128)S(1)} %stack.23.pos, bf16[32,8,128]{2,1,0:T(8,128)(2,1)S(1)} %all-to-all-done.3.in_ref, bf16[40,128]{1,0:T(8,128)(2,1)S(1)} %bitcast.18, bf16[128,128]{1,0:T(8,128)(2,1)S(1)} %bitcast.17, f32[2,40]{1,0:T(2,128)S(1)} %pad_maximum_fusion.damp_ref), custom_call_target="tpu_custom_call" | custom-call | tf_op jit(solution)/shard_map/pallas_call | solution.py:171
  112.5 0.0 copy-start.2
  112.5 15.9 %all_to_all.32.in_ref = bf16[16,32,128]{2,1,0:T(8,128)(2,1)S(1)} all-to-all(bf16[16,32,128]{2,1,0:T(8,128)(2,1)S(1)} %shard_map.112), channel_id=1, replica_groups=mesh['yl'=2,'z'=16,'c'=2,'x'=4,'yh'=2] {'z'}, dimensions={0} | all-to-all | bytes 262144 | tf_op jit(solution)/shard_map/all_to_all | solution.py:245
  128.4 0.0 copy-done.2
  128.4 1.2 shard_map.113
  129.6 15.8 %all_to_all.33.in_ref = bf16[32,32,128]{2,1,0:T(8,128)(2,1)} all-to-all(bf16[32,32,128]{2,1,0:T(8,128)(2,1)S(1)} %shard_map.113), channel_id=1, replica_groups=mesh['yl'=2,'z'=16,'c'=2,'x'=4,'yh'=2] {'yl','c','x','yh'}, dimensions={0} | all-to-all | bytes 524288 | tf_op jit(solution)/shard_map/all_to_all | solution.py:257
  145.4 3.8 %shard_map.114 = bf16[2048,256]{1,0:T(8,128)(2,1)} custom-call(bf16[32,32,128]{2,1,0:T(8,128)(2,1)} %all_to_all.33.in_ref, bf16[2048,128]{1,0:T(8,128)(2,1)} %bitcast.19), custom_call_target="tpu_custom_call" | custom-call | tf_op jit(solution)/shard_map/pallas_call | solution.py:260
  (4 shorter events, 0.1 us)
Async XLA Ops:
  1.5 17.2 %copy-start = (bf16[1,128,1792]{2,1,0:T(8,128)(2,1)S(1)}, bf16[1,128,1792]{2,1,0:T(8,128)(2,1)}, u32[]{:S(2)}) copy-start(bf16[1,128,1792]{2,1,0:T(8,128)(2,1)} %param.12) | copy-start | bytes 1376260
  1.6 45.1 %all-to-all-start = ((bf16[32,8,896]{2,1,0:T(8,128)(2,1)}), bf16[32,8,896]{2,1,0:T(8,128)(2,1)S(1)}, u32[]{:S(2)}, u32[]{:S(2)}) async-start(bf16[32,8,896]{2,1,0:T(8,128)(2,1)} %bitcast.7), calls=%async_computation | async-start | bytes 917504 | tf_op jit(solution)/shard_map/all_to_all | solution.py:197
  18.7 31.5 %copy-start.5 = (s32[1,256]{1,0:T(1,128)S(1)}, s32[1,256]{1,0:T(1,128)}, u32[]{:S(2)}) copy-start(s32[1,256]{1,0:T(1,128)} %param.14) | copy-start | bytes 3076
  18.8 31.5 %copy-start.6 = (s32[1,256]{1,0:T(1,128)S(1)}, s32[1,256]{1,0:T(1,128)}, u32[]{:S(2)}) copy-start(s32[1,256]{1,0:T(1,128)} %param.13) | copy-start | bytes 3076
  46.6 13.4 %collective-permute-start = (bf16[32,8,896]{2,1,0:T(8,128)(2,1)S(1)}, bf16[32,8,896]{2,1,0:T(8,128)(2,1)S(1)}, u32[]{:S(2)}, u32[]{:S(2)}) collective-permute-start(bf16[32,8,896]{2,1,0:T(8,128)(2,1)S(1)} %all-to-all-done.own_ref), channel_id=1, source_target_pairs={{0,8},{8,0},{1,9},{9,1},{2,10},{10,2},{3,11},{11,3},{4,12},{12,4},... | collective-permute-start | bytes 1376264 | tf_op jit(solution)/shard_map/ppermute | solution.py:198
  50.3 9.7 %collective-permute-start.1 = (bf16[144,896]{1,0:T(8,128)(2,1)S(1)}, bf16[144,896]{1,0:T(8,128)(2,1)S(1)}, u32[]{:S(2)}, u32[]{:S(2)}) collective-permute-start(bf16[144,896]{1,0:T(8,128)(2,1)S(1)} %fusion.1), channel_id=1, source_target_pairs={{0,256},{256,0},{1,257},{257,1},{2,258},{258,2},{3,259},{259,3},{4... | collective-permute-start | bytes 774152 | tf_op jit(solution)/shard_map/ppermute | solution.py:193
  78.2 16.9 %copy-start.3 = (f32[16,1,256]{2,1,0:T(1,128)S(1)}, f32[16,1,256]{2,1,0:T(1,128)}, u32[]{:S(2)}) copy-start(f32[16,1,256]{2,1,0:T(1,128)} %constant.39.clone.table_ref) | copy-start | bytes 49156
  97.0 6.6 %copy-start.7 = (f32[1,40]{1,0:T(1,128)S(1)}, f32[1,40]{1,0:T(1,128)}, u32[]{:S(2)}) copy-start(f32[1,40]{1,0:T(1,128)} %param.18) | copy-start | bytes 484
  97.0 6.6 %copy-start.8 = (f32[1,40]{1,0:T(1,128)S(1)}, f32[1,40]{1,0:T(1,128)}, u32[]{:S(2)}) copy-start(f32[1,40]{1,0:T(1,128)} %param.17) | copy-start | bytes 484
  97.0 13.8 %copy-start.1 = (bf16[1,128,128]{2,1,0:T(8,128)(2,1)S(1)}, bf16[1,128,128]{2,1,0:T(8,128)(2,1)}, u32[]{:S(2)}) copy-start(bf16[1,128,128]{2,1,0:T(8,128)(2,1)} %param.16) | copy-start | bytes 98308
  97.0 13.8 %copy-start.4 = (bf16[1,40,128]{2,1,0:T(8,128)(2,1)S(1)}, bf16[1,40,128]{2,1,0:T(8,128)(2,1)}, u32[]{:S(2)}) copy-start(bf16[1,40,128]{2,1,0:T(8,128)(2,1)} %param.15) | copy-start | bytes 30724
  97.0 13.8 %all-to-all-start.3 = ((bf16[32,8,128]{2,1,0:T(8,128)(2,1)}), bf16[32,8,128]{2,1,0:T(8,128)(2,1)S(1)}, u32[]{:S(2)}, u32[]{:S(2)}) async-start(bf16[32,8,128]{2,1,0:T(8,128)(2,1)} %shard_map.111), calls=%async_computation.3 | async-start | bytes 131072 | tf_op jit(solution)/shard_map/all_to_all | solution.py:233
  112.5 15.9 %copy-start.2 = (f32[64,1,64]{2,1,0:T(1,128)S(1)}, f32[64,1,64]{2,1,0:T(1,128)}, u32[]{:S(2)}) copy-start(f32[64,1,64]{2,1,0:T(1,128)} %constant.40.clone.table_ref) | copy-start | bytes 49156

commit v2 on v1

v2 whole, which is shorter than its diff:
```python
import numpy as np
import jax
import jax.numpy as jnp
from jax import lax
from jax.experimental import pallas as pl
from jax.experimental.pallas import tpu as pltpu
from jax.sharding import Mesh, PartitionSpec as P

AXES = ("yl", "z", "c", "x", "yh")
SIZES = (2, 16, 2, 4, 2)
PLANE = ("yl", "c", "x", "yh")
YL, Z, C, D = 2, 16, 2, 8
PEERS = YL * C * D
BLADES, PH, NT, NB, MODES = YL * Z * C, 8, 256, 128, 40
HALF = 896
TS = NT // PEERS
TD = NT // D
BF = jnp.bfloat16
F32 = jnp.float32
HI = lax.Precision.HIGHEST


def fourier_table(count):
    h = np.arange(count)[:, None]
    s = np.arange(count)[None, :]
    angle = 2.0 * np.pi * ((((h + 1) // 2) * s) % count) / count
    table = np.where(h % 2 == 1, np.cos(angle), np.sin(angle))
    table = np.where(h == 0, 1.0, table)
    edges = (h == 0) | (h == count - 1)
    return table * np.where(edges, np.sqrt(1.0 / count), np.sqrt(2.0 / count))


FOURIER = fourier_table(BLADES)
FORWARD = np.ascontiguousarray(
    FOURIER.reshape(YL, Z, C, YL, Z, C).transpose(1, 4, 3, 5, 0, 2).reshape(Z, 256)
).astype(np.float32)
INVERSE = np.ascontiguousarray(
    FOURIER.reshape(YL, Z, C, YL, Z, C).transpose(0, 2, 4, 1, 3, 5).reshape(YL * C * Z, 64)
).astype(np.float32)


def dot_nt(a, b, **kw):
    return lax.dot_general(
        a, b, (((1,), (1,)), ((), ())), preferred_element_type=F32, **kw
    )


def spread_kernel(in_ref, out_ref):
    for half in range(YL):
        part = in_ref[:, half * HALF : (half + 1) * HALF]
        out_ref[half * Z : (half + 1) * Z] = jnp.broadcast_to(part[None], (Z, PH, HALF))


def pack_kernel(pos, basis_ref, block_ref, phase_ref, near_ref, far_ref):
    index = jnp.concatenate(
        [block_ref[...].astype(F32), phase_ref[...].astype(F32), jnp.zeros((14, NT), F32)], axis=0
    )
    index = jnp.concatenate([index, jnp.zeros((16, HALF - NT), F32)], axis=1).astype(BF)
    for k, ref in enumerate((near_ref, far_ref)):
        half = (pos[0] + k) & 1
        ref[0:NB] = basis_ref[:, pl.ds(pl.multiple_of(half * HALF, 128), HALF)]
        ref[NB : NB + 16] = index


def project_kernel(pos, wake_ref, *refs):
    out_ref = refs[-1]
    basis = jnp.concatenate([ref[0:NB] for ref in refs[:4]], axis=0)
    table = dot_nt(wake_ref[...].reshape(YL * Z * PH, HALF), basis).astype(BF)
    pair = lax.broadcasted_iota(jnp.int32, (NT, YL * Z * PH), 1).astype(F32)
    codes = []
    for ref in refs[:4]:
        index = ref[NB : NB + 16, 0:NT].astype(F32)
        block, phase = index[0:1].astype(jnp.int32), index[1:2].astype(jnp.int32)
        code = ((block >> 1) * PH + phase).astype(F32)
        codes.append(jnp.where((block & 1) == pos[1], code, -1.0))
    codes = jnp.concatenate(codes + [jnp.zeros((4, NT), F32)], axis=0).T
    picks = []
    for r in range(4):
        onehot = jnp.where(codes[:, r : r + 1] == pair, 1.0, 0.0).astype(BF)
        part = jnp.dot(onehot, table[:, r * NB : (r + 1) * NB], preferred_element_type=F32)
        picks.append(part.reshape(PEERS, TS, NB))
    out_ref[...] = jnp.concatenate(picks, axis=1).astype(BF)


def gather_sum_kernel(in_ref, out_ref):
    sums = {}
    for yl in range(YL):
        for c in range(C):
            total = None
            for d in range(D):
                part = in_ref[(yl * C + c) * D + d].astype(F32)
                total = part if total is None else total + part
            sums[yl, c] = total
    rows = []
    for yl in range(YL):
        for c in range(C):
            total = None
            for y in range(YL):
                for k in range(C):
                    r = (yl ^ y) + 2 * (c ^ k)
                    part = sums[y, k][r * TS : (r + 1) * TS]
                    total = part if total is None else total + part
            rows.append(total)
    block = jnp.concatenate(rows, axis=0).astype(BF)
    out_ref[...] = jnp.broadcast_to(block[None], out_ref.shape)


def forward_kernel(table_ref, in_ref, out_ref):
    acc = [None] * 4
    for z in range(Z):
        block = in_ref[z].astype(F32)
        for q in range(4):
            part = block[q * TS : (q + 1) * TS]
            for h in range(4):
                term = part * table_ref[(z * 4 + q) * 4 + h]
                acc[h] = term if acc[h] is None else acc[h] + term
    for h in range(4):
        out_ref[h * D : (h + 1) * D] = jnp.broadcast_to(acc[h].astype(BF)[None], (D, TS, NB))


def modal_kernel(pos, in_ref, shapes_ref, flex_ref, damp_ref, out_ref, hold_ref):
    force = in_ref[...].reshape(NT, NB)
    shapes = shapes_ref[...]
    real = dot_nt(shapes, force)
    imag = None
    damp = jnp.concatenate([damp_ref[...], jnp.zeros((6, MODES), F32)], axis=0).T
    omega, zeta = damp[:, 0:1], damp[:, 1:2]
    size = jnp.exp(-omega * zeta)
    angle = omega * jnp.sqrt(1.0 - zeta * zeta)
    pr, pi = size * jnp.cos(angle), size * jnp.sin(angle)
    lane = lax.broadcasted_iota(jnp.int32, (MODES, NT), 1)
    shift = 1
    while shift < NT:
        keep = lane >= shift
        sr = jnp.where(keep, pltpu.roll(real, shift, 1), 0.0)
        if imag is None:
            real, imag = real + pr * sr, pi * sr
        else:
            si = jnp.where(keep, pltpu.roll(imag, shift, 1), 0.0)
            real, imag = real + (pr * sr - pi * si), imag + (pr * si + pi * sr)
        pr, pi = pr * pr - pi * pi, 2.0 * pr * pi
        shift *= 2
    hold_ref[...] = lax.dot_general(
        imag,
        shapes.astype(F32),
        (((0,), (0,)), ((), ())),
        precision=HI,
        preferred_element_type=F32,
    ) + dot_nt(force, flex_ref[...])
    block = hold_ref[pl.ds(pl.multiple_of(pos[2] * TD, TD), TD), :].astype(BF)
    out_ref[...] = jnp.broadcast_to(block[None], out_ref.shape)


def inverse_kernel(table_ref, in_ref, out_ref):
    acc = [None] * 4
    for z in range(Z):
        block = in_ref[z].astype(F32)
        for s in range(4):
            term = block * table_ref[z * 4 + s]
            acc[s] = term if acc[s] is None else acc[s] + term
    for s in range(4):
        out_ref[s * D : (s + 1) * D] = jnp.broadcast_to(acc[s].astype(BF)[None], (D, TD, NB))


CHUNKS = 4


def stress_kernel(in_ref, map_ref, out_ref, hold_ref, sems):
    total = None
    for q in range(YL * C):
        part = in_ref[q * D : (q + 1) * D].astype(F32)
        total = part if total is None else total + part
    motion = total.reshape(NT, NB).astype(BF)
    step = map_ref.shape[0] // CHUNKS
    copies = []
    for k in range(CHUNKS):
        rows = pl.ds(k * step, step)
        hold_ref[rows] = dot_nt(map_ref[rows], motion).astype(BF)
        copies.append(pltpu.make_async_copy(hold_ref.at[rows], out_ref.at[rows], sems.at[k]))
        copies[-1].start()
    for copy in copies:
        copy.wait()


VMEM = pl.BlockSpec(memory_space=pltpu.VMEM)
SMEM = pl.BlockSpec(memory_space=pltpu.SMEM)


def call(kernel, outs, specs, *args, out_specs=None, scratch=()):
    outs = [jax.ShapeDtypeStruct(shape, BF) for shape in outs]
    got = pl.pallas_call(
        kernel,
        out_shape=outs,
        in_specs=specs,
        out_specs=out_specs or [VMEM] * len(outs),
        scratch_shapes=list(scratch),
        compiler_params=pltpu.CompilerParams(vmem_limit_bytes=24 * 1024 * 1024),
    )(*args)
    return got[0] if len(outs) == 1 else got


def local(wake, basis, block_index, phase_index, shapes, flex, omega, zeta, stress_map):
    yl, z, c = lax.axis_index("yl"), lax.axis_index("z"), lax.axis_index("c")
    d = lax.axis_index("x") * 2 + lax.axis_index("yh")
    pos = jnp.stack([yl, c, d]).astype(jnp.int32)
    forward = lax.dynamic_slice(jnp.asarray(FORWARD), (z, 0), (1, 256)).reshape(256)
    inverse = lax.dynamic_slice(jnp.asarray(INVERSE), ((yl * C + c) * Z + z, 0), (1, 64)).reshape(64)
    damp = jnp.concatenate([omega, zeta], axis=0)

    spread = call(spread_kernel, [(YL * Z, PH, HALF)], [VMEM], wake[0])
    blocks = lax.all_to_all(spread, ("yl", "z"), 0, 0, tiled=True)

    near, far = call(
        pack_kernel,
        [(NB + 16, HALF)] * 2,
        [SMEM, VMEM, VMEM, VMEM],
        pos,
        basis[0],
        block_index,
        phase_index,
    )
    swap = [(0, 1), (1, 0)]
    by_yl = lax.ppermute(far, "yl", swap)
    by_c = lax.ppermute(near, "c", swap)
    by_both = lax.ppermute(far, ("yl", "c"), [(0, 3), (1, 2), (2, 1), (3, 0)])

    picked = call(
        project_kernel,
        [(PEERS, 4 * TS, NB)],
        [SMEM] + [VMEM] * 5,
        pos,
        blocks,
        near,
        by_yl,
        by_c,
        by_both,
    )
    parts = lax.all_to_all(picked, PLANE, 0, 0, tiled=True)
    forcing = call(gather_sum_kernel, [(Z, 4 * TS, NB)], [VMEM], parts)
    forcing = lax.all_to_all(forcing, "z", 0, 0, tiled=True)
    harmonic = call(forward_kernel, [(PEERS, TS, NB)], [SMEM, VMEM], forward, forcing)
    harmonic = lax.all_to_all(harmonic, PLANE, 0, 0, tiled=True)
    physical = call(
        modal_kernel,
        [(Z, TD, NB)],
        [SMEM] + [VMEM] * 4,
        pos,
        harmonic,
        shapes[0],
        flex[0],
        damp,
        scratch=[pltpu.VMEM((NT, NB), F32)],
    )
    physical = lax.all_to_all(physical, "z", 0, 0, tiled=True)
    sectoral = call(inverse_kernel, [(PEERS, TD, NB)], [SMEM, VMEM], inverse, physical)
    sectoral = lax.all_to_all(sectoral, PLANE, 0, 0, tiled=True)
    rows = stress_map.shape[1]
    stress = call(
        stress_kernel,
        [(rows, NT)],
        [VMEM, VMEM],
        sectoral,
        stress_map[0],
        out_specs=[pl.BlockSpec(memory_space=pl.ANY)],
        scratch=[pltpu.VMEM((rows, NT), BF), pltpu.SemaphoreType.DMA((CHUNKS,))],
    )
    return stress[None]


def solution(mesh):
    sector, dof = ("yl", "z", "c"), ("x", "yh")
    return jax.shard_map(
        local,
        mesh=Mesh(mesh.devices.reshape(SIZES), AXES),
        in_specs=(
            P(sector, None, dof),
            P(sector, None, dof),
            P(sector, None),
            P(sector, None),
            P(sector, None, None),
            P(sector, None, None),
            P(sector, None),
            P(sector, None),
            P(sector, dof, None),
        ),
        out_specs=P(sector, dof, None),
        check_vma=False,
    )
```

time: 150 us -> 135 us (0.900)
  blocking collectives: 63.9 us -> 33.1 us
  starting transfers between devices: 29.9 us -> 40.4 us
  waiting for transfers between devices: 42 us -> 48.4 us
  Pallas kernels: 11.5 us -> 8.97 us
    all_to_all x2 -> x0, blocking collectives: 32.8 us -> none  [the longest x1 16.9 us: local(): forcing = lax.all_to_all(forcing, 'z', 0, 0, tiled=True)]
    all_to_all x1 -> x3, starting transfers between devices: 17.2 us -> 25.7 us  [the longest x1 17.2 us: local(): blocks = lax.all_to_all(spread, ('yl', 'z'), 0, 0, tiled=True)]
    ppermute x2 -> x3, waiting for transfers between devices: 6.97 us -> 10.4 us  [the longest x1 9.5 us: local(): by_both = lax.ppermute(far, ('yl', 'c'), [(0, 3), (1, 2), (2, 1), (3, 0)])]
    all_to_all x1 -> x3, waiting for transfers between devices: 27.8 us -> 30.7 us  [the longest x1 11.8 us: local(): forcing = lax.all_to_all(forcing, 'z', 0, 0, tiled=True)]
    pallas_call x6 -> x8, Pallas kernels: 11.5 us -> 8.97 us  [call(): pl.pallas_call(kernel, out_shape=outs, in_specs=specs, out_specs=out_spec...]
    ppermute x2 -> x3, starting transfers between devices: 6.24 us -> 8.49 us  [the longest x1 3.42 us: local(): by_c = lax.ppermute(near, 'c', swap)]
    all_to_all x1, blocking collectives: 15.2 us -> 17.4 us  [local(): parts = lax.all_to_all(picked, PLANE, 0, 0, tiled=True)]
    broadcast_in_dim x1 -> x0, local copies, waits for them, and re-layouts: 1.55 us -> none  [local(): jnp.broadcast_to(mine[:, None], (YL, Z, PH, HALF)).reshape(YL * Z, PH, HALF)]
  transfers between devices with their start and end apart: 4 -> 7, of which waited for: 3 -> 6; matrix products, arithmetic and copies ran while one was open for 0% -> 1% of each run, Pallas kernels for 0% -> 0%
where the time goes in v2:
time: 135 us; the launch traced here: 134 us
  waiting for transfers between devices  48.4 us (36%)
  starting transfers between devices  40.4 us (30%)
  blocking collectives  33.1 us (25%)
  Pallas kernels  8.97 us (7%)
  local copies, waits for them, and re-layouts  2.92 us (2%)
    all_to_all x1, blocking collectives, local(): parts = lax.all_to_all(picked, PLANE, 0, 0, tiled=True)  17.4 us
    all_to_all x1, starting transfers between devices, local(): blocks = lax.all_to_all(spread, ('yl', 'z'), 0, 0, tiled=True)  17.2 us
    all_to_all x1, blocking collectives, local(): sectoral = lax.all_to_all(sectoral, PLANE, 0, 0, tiled=True)  15.7 us
    all_to_all x1, waiting for transfers between devices, local(): forcing = lax.all_to_all(forcing, 'z', 0, 0, tiled=True)  11.8 us
    all_to_all x1, waiting for transfers between devices, local(): physical = lax.all_to_all(physical, 'z', 0, 0, tiled=True)  11.4 us
    ppermute x1, waiting for transfers between devices, local(): by_both = lax.ppermute(far, ('yl', 'c'), [(0, 3), (1, 2), (2, 1), (3, 0)])  9.5 us
    pallas_call x8, Pallas kernels, call(): pl.pallas_call(kernel, out_shape=outs, in_specs=specs, out_specs=out_spec...  8.97 us
    all_to_all x1, waiting for transfers between devices, local(): blocks = lax.all_to_all(spread, ('yl', 'z'), 0, 0, tiled=True)  7.58 us
  transfers between devices with their start and end apart: 7, of which 6 were waited for; matrix products, arithmetic and copies ran while one was open for 1% of the time, Pallas kernels for 0%

profile of v2, /device:TPU:1, one launch (start us, length us, event | category | flops | bytes accessed | tf_op | source)
XLA Modules:
  0.0 134.1 jit_solution(3933251432440560656)
XLA Ops:
  0.0 0.0 copy-start.3
  0.0 0.7 copy-done.3
  0.7 0.8 shard_map.109
  1.6 0.0 copy-start.1
  1.6 17.2 %all-to-all-start = ((bf16[32,8,896]{2,1,0:T(8,128)(2,1)}), bf16[32,8,896]{2,1,0:T(8,128)(2,1)S(1)}, u32[]{:S(2)}, u32[]{:S(2)}) async-start(bf16[32,8,896]{2,1,0:T(8,128)(2,1)} %shard_map.109), calls=%async_computation | async-start | bytes 917504 | tf_op jit(solution)/shard_map/all_to_all | solution.py:211
  18.7 0.0 copy-start.6
  18.8 0.1 pad_add_fusion.pos
  18.8 0.0 copy-start.5
  18.8 0.0 copy-done.1
  18.8 0.6 copy-done.6
  19.4 0.1 copy-done.5
  19.5 0.6 shard_map.110
  20.1 3.1 %collective-permute-start = (bf16[144,896]{1,0:T(8,128)(2,1)S(1)}, bf16[144,896]{1,0:T(8,128)(2,1)S(1)}, u32[]{:S(2)}, u32[]{:S(2)}) collective-permute-start(bf16[144,896]{1,0:T(8,128)(2,1)S(1)} %get-tuple-element.8), channel_id=1, source_target_pairs={{0,256},{256,0},{1,257},{257,1},{2,258},{258,2},{3,259},{259,3},{4... | collective-permute-start | bytes 774152 | tf_op jit(solution)/shard_map/ppermute | solution.py:223
  23.3 3.4 %collective-permute-start.1 = (bf16[144,896]{1,0:T(8,128)(2,1)S(1)}, bf16[144,896]{1,0:T(8,128)(2,1)S(1)}, u32[]{:S(2)}, u32[]{:S(2)}) collective-permute-start(bf16[144,896]{1,0:T(8,128)(2,1)S(1)} %get-tuple-element.7.refs_0_), channel_id=1, source_target_pairs={{0,8},{8,0},{1,9},{9,1},{2,10},{10,2},{3,11},{11,3},{4,12},{12,4},... | collective-permute-start | bytes 774152 | tf_op jit(solution)/shard_map/ppermute | solution.py:224
  26.7 1.9 %collective-permute-start.2 = (bf16[144,896]{1,0:T(8,128)(2,1)S(1)}, bf16[144,896]{1,0:T(8,128)(2,1)S(1)}, u32[]{:S(2)}, u32[]{:S(2)}) collective-permute-start(bf16[144,896]{1,0:T(8,128)(2,1)S(1)} %get-tuple-element.8), channel_id=1, source_target_pairs={{0,264},{8,256},{256,8},{264,0},{1,265},{9,257},{257,9},{265,1},{2... | collective-permute-start | bytes 774152 | tf_op jit(solution)/shard_map/ppermute | solution.py:225
  28.6 0.9 collective-permute-done.refs_1_
  29.6 0.0 collective-permute-done.1.refs_2_
  29.6 9.5 %collective-permute-done.2.refs_3_ = bf16[144,896]{1,0:T(8,128)(2,1)S(1)} collective-permute-done((bf16[144,896]{1,0:T(8,128)(2,1)S(1)}, bf16[144,896]{1,0:T(8,128)(2,1)S(1)}, u32[]{:S(2)}, u32[]{:S(2)}) %collective-permute-start.2) | collective-permute-done | bytes 258080 | tf_op jit(solution)/shard_map/ppermute | solution.py:225
  39.1 7.6 %all-to-all-done.wake_ref = bf16[32,8,896]{2,1,0:T(8,128)(2,1)S(1)} async-done(((bf16[32,8,896]{2,1,0:T(8,128)(2,1)}), bf16[32,8,896]{2,1,0:T(8,128)(2,1)S(1)}, u32[]{:S(2)}, u32[]{:S(2)}) %all-to-all-start) | async-done | bytes 458784 | tf_op jit(solution)/shard_map/all_to_all | solution.py:211
  46.6 1.3 shard_map.111
  48.0 17.4 %all_to_all.30.in_ref = bf16[32,32,128]{2,1,0:T(8,128)(2,1)S(1)} all-to-all(bf16[32,32,128]{2,1,0:T(8,128)(2,1)S(1)} %shard_map.111), channel_id=1, replica_groups=mesh['yl'=2,'z'=16,'c'=2,'x'=4,'yh'=2] {'yl','c','x','yh'}, dimensions={0} | all-to-all | bytes 524288 | tf_op jit(solution)/shard_map/all_to_all | solution.py:238
  65.4 0.7 shard_map.112
  66.1 4.4 %all-to-all-start.2 = ((bf16[16,32,128]{2,1,0:T(8,128)(2,1)}), bf16[16,32,128]{2,1,0:T(8,128)(2,1)S(1)}, u32[]{:S(2)}, u32[]{:S(2)}) async-start(bf16[16,32,128]{2,1,0:T(8,128)(2,1)} %shard_map.112), calls=%async_computation.2 | async-start | bytes 262144 | tf_op jit(solution)/shard_map/all_to_all | solution.py:240
  70.5 0.7 constant_dynamic-slice_fusion
  71.2 11.8 %all-to-all-done.2.in_ref = bf16[16,32,128]{2,1,0:T(8,128)(2,1)S(1)} async-done(((bf16[16,32,128]{2,1,0:T(8,128)(2,1)}), bf16[16,32,128]{2,1,0:T(8,128)(2,1)S(1)}, u32[]{:S(2)}, u32[]{:S(2)}) %all-to-all-start.2) | async-done | bytes 131104 | tf_op jit(solution)/shard_map/all_to_all | solution.py:240
  83.0 1.3 shard_map.113
  84.3 0.0 copy-start.7
  84.3 0.0 copy-start.8
  84.4 0.0 copy-start.2
  84.4 0.0 copy-start.4
  84.4 6.3 %all-to-all-start.3 = ((bf16[32,8,128]{2,1,0:T(8,128)(2,1)}), bf16[32,8,128]{2,1,0:T(8,128)(2,1)S(1)}, u32[]{:S(2)}, u32[]{:S(2)}) async-start(bf16[32,8,128]{2,1,0:T(8,128)(2,1)} %shard_map.113), calls=%async_computation.3 | async-start | bytes 131072 | tf_op jit(solution)/shard_map/all_to_all | solution.py:242
  90.6 0.0 copy-done.7
  90.6 0.0 copy-done.8
  90.7 7.2 %all-to-all-done.3.in_ref = bf16[32,8,128]{2,1,0:T(8,128)(2,1)S(1)} async-done(((bf16[32,8,128]{2,1,0:T(8,128)(2,1)}), bf16[32,8,128]{2,1,0:T(8,128)(2,1)S(1)}, u32[]{:S(2)}, u32[]{:S(2)}) %all-to-all-start.3) | async-done | bytes 65568 | tf_op jit(solution)/shard_map/all_to_all | solution.py:242
  97.9 0.0 copy-done.2
  97.9 0.0 copy-done.4
  97.9 2.3 %shard_map.114 = bf16[16,32,128]{2,1,0:T(8,128)(2,1)} custom-call(s32[3]{0:T(128)S(1)} %pad_add_fusion.pos, bf16[32,8,128]{2,1,0:T(8,128)(2,1)S(1)} %all-to-all-done.3.in_ref, bf16[40,128]{1,0:T(8,128)(2,1)S(1)} %bitcast.16, bf16[128,128]{1,0:T(8,128)(2,1)S(1)} %bitcast.14, f32[2,40]{1,0:T(2,128)S(1)} %pad_maximum_fusion.damp_ref), custom_call_target="tpu_custom_call" | custom-call | tf_op jit(solution)/shard_map/pallas_call | solution.py:191
  100.2 4.1 %all-to-all-start.4 = ((bf16[16,32,128]{2,1,0:T(8,128)(2,1)}), bf16[16,32,128]{2,1,0:T(8,128)(2,1)S(1)}, u32[]{:S(2)}, u32[]{:S(2)}) async-start(bf16[16,32,128]{2,1,0:T(8,128)(2,1)} %shard_map.114), calls=%async_computation.4 | async-start | bytes 262144 | tf_op jit(solution)/shard_map/all_to_all | solution.py:254
  104.3 0.0 copy-start
  104.3 0.8 dynamic-slice_bitcast_fusion.table_ref
  105.1 11.4 %all-to-all-done.4.in_ref = bf16[16,32,128]{2,1,0:T(8,128)(2,1)S(1)} async-done(((bf16[16,32,128]{2,1,0:T(8,128)(2,1)}), bf16[16,32,128]{2,1,0:T(8,128)(2,1)S(1)}, u32[]{:S(2)}, u32[]{:S(2)}) %all-to-all-start.4) | async-done | bytes 131104 | tf_op jit(solution)/shard_map/all_to_all | solution.py:254
  116.5 0.6 shard_map.115
  117.1 15.7 %all_to_all.31.in_ref = bf16[32,32,128]{2,1,0:T(8,128)(2,1)S(1)} all-to-all(bf16[32,32,128]{2,1,0:T(8,128)(2,1)S(1)} %shard_map.115), channel_id=1, replica_groups=mesh['yl'=2,'z'=16,'c'=2,'x'=4,'yh'=2] {'yl','c','x','yh'}, dimensions={0} | all-to-all | bytes 524288 | tf_op jit(solution)/shard_map/all_to_all | solution.py:256
  132.8 0.0 copy-done
  132.8 1.3 shard_map.116
  (1 shorter events, 0.0 us)
Async XLA Ops:
  0.0 0.7 copy-start.3
  1.6 17.3 %copy-start.1 = (bf16[1,128,1792]{2,1,0:T(8,128)(2,1)S(1)}, bf16[1,128,1792]{2,1,0:T(8,128)(2,1)}, u32[]{:S(2)}) copy-start(bf16[1,128,1792]{2,1,0:T(8,128)(2,1)} %param.12) | copy-start | bytes 1376260
  1.6 45.1 %all-to-all-start = ((bf16[32,8,896]{2,1,0:T(8,128)(2,1)}), bf16[32,8,896]{2,1,0:T(8,128)(2,1)S(1)}, u32[]{:S(2)}, u32[]{:S(2)}) async-start(bf16[32,8,896]{2,1,0:T(8,128)(2,1)} %shard_map.109), calls=%async_computation | async-start | bytes 917504 | tf_op jit(solution)/shard_map/all_to_all | solution.py:211
  18.7 0.7 copy-start.6
  18.8 0.7 copy-start.5
  20.1 9.5 %collective-permute-start = (bf16[144,896]{1,0:T(8,128)(2,1)S(1)}, bf16[144,896]{1,0:T(8,128)(2,1)S(1)}, u32[]{:S(2)}, u32[]{:S(2)}) collective-permute-start(bf16[144,896]{1,0:T(8,128)(2,1)S(1)} %get-tuple-element.8), channel_id=1, source_target_pairs={{0,256},{256,0},{1,257},{257,1},{2,258},{258,2},{3,259},{259,3},{4... | collective-permute-start | bytes 774152 | tf_op jit(solution)/shard_map/ppermute | solution.py:223
  23.3 6.3 %collective-permute-start.1 = (bf16[144,896]{1,0:T(8,128)(2,1)S(1)}, bf16[144,896]{1,0:T(8,128)(2,1)S(1)}, u32[]{:S(2)}, u32[]{:S(2)}) collective-permute-start(bf16[144,896]{1,0:T(8,128)(2,1)S(1)} %get-tuple-element.7.refs_0_), channel_id=1, source_target_pairs={{0,8},{8,0},{1,9},{9,1},{2,10},{10,2},{3,11},{11,3},{4,12},{12,4},... | collective-permute-start | bytes 774152 | tf_op jit(solution)/shard_map/ppermute | solution.py:224
  26.7 12.4 %collective-permute-start.2 = (bf16[144,896]{1,0:T(8,128)(2,1)S(1)}, bf16[144,896]{1,0:T(8,128)(2,1)S(1)}, u32[]{:S(2)}, u32[]{:S(2)}) collective-permute-start(bf16[144,896]{1,0:T(8,128)(2,1)S(1)} %get-tuple-element.8), channel_id=1, source_target_pairs={{0,264},{8,256},{256,8},{264,0},{1,265},{9,257},{257,9},{265,1},{2... | collective-permute-start | bytes 774152 | tf_op jit(solution)/shard_map/ppermute | solution.py:225
  66.1 16.9 %all-to-all-start.2 = ((bf16[16,32,128]{2,1,0:T(8,128)(2,1)}), bf16[16,32,128]{2,1,0:T(8,128)(2,1)S(1)}, u32[]{:S(2)}, u32[]{:S(2)}) async-start(bf16[16,32,128]{2,1,0:T(8,128)(2,1)} %shard_map.112), calls=%async_computation.2 | async-start | bytes 262144 | tf_op jit(solution)/shard_map/all_to_all | solution.py:240
  84.3 6.3 %copy-start.7 = (f32[1,40]{1,0:T(1,128)S(1)}, f32[1,40]{1,0:T(1,128)}, u32[]{:S(2)}) copy-start(f32[1,40]{1,0:T(1,128)} %param.18) | copy-start | bytes 484
  84.3 6.3 %copy-start.8 = (f32[1,40]{1,0:T(1,128)S(1)}, f32[1,40]{1,0:T(1,128)}, u32[]{:S(2)}) copy-start(f32[1,40]{1,0:T(1,128)} %param.17) | copy-start | bytes 484
  84.4 13.5 %copy-start.2 = (bf16[1,128,128]{2,1,0:T(8,128)(2,1)S(1)}, bf16[1,128,128]{2,1,0:T(8,128)(2,1)}, u32[]{:S(2)}) copy-start(bf16[1,128,128]{2,1,0:T(8,128)(2,1)} %param.16) | copy-start | bytes 98308
  84.4 13.5 %copy-start.4 = (bf16[1,40,128]{2,1,0:T(8,128)(2,1)S(1)}, bf16[1,40,128]{2,1,0:T(8,128)(2,1)}, u32[]{:S(2)}) copy-start(bf16[1,40,128]{2,1,0:T(8,128)(2,1)} %param.15) | copy-start | bytes 30724
  84.4 13.5 %all-to-all-start.3 = ((bf16[32,8,128]{2,1,0:T(8,128)(2,1)}), bf16[32,8,128]{2,1,0:T(8,128)(2,1)S(1)}, u32[]{:S(2)}, u32[]{:S(2)}) async-start(bf16[32,8,128]{2,1,0:T(8,128)(2,1)} %shard_map.113), calls=%async_computation.3 | async-start | bytes 131072 | tf_op jit(solution)/shard_map/all_to_all | solution.py:242
  100.2 16.2 %all-to-all-start.4 = ((bf16[16,32,128]{2,1,0:T(8,128)(2,1)}), bf16[16,32,128]{2,1,0:T(8,128)(2,1)S(1)}, u32[]{:S(2)}, u32[]{:S(2)}) async-start(bf16[16,32,128]{2,1,0:T(8,128)(2,1)} %shard_map.114), calls=%async_computation.4 | async-start | bytes 262144 | tf_op jit(solution)/shard_map/all_to_all | solution.py:254
  104.3 28.5 %copy-start = (bf16[1,2048,128]{2,1,0:T(8,128)(2,1)S(1)}, bf16[1,2048,128]{2,1,0:T(8,128)(2,1)}, u32[]{:S(2)}) copy-start(bf16[1,2048,128]{2,1,0:T(8,128)(2,1)} %param.19) | copy-start | bytes 1572868

commit v3 on v2

--- a/solution.py
+++ b/solution.py
@@ -14,7 +14,6 @@
 BLADES, PH, NT, NB, MODES = YL * Z * C, 8, 256, 128, 40
 HALF = 896
 TS = NT // PEERS
-TD = NT // D
 BF = jnp.bfloat16
 F32 = jnp.float32
 HI = lax.Precision.HIGHEST
@@ -30,13 +29,32 @@
     return table * np.where(edges, np.sqrt(1.0 / count), np.sqrt(2.0 / count))
 
 
-FOURIER = fourier_table(BLADES)
-FORWARD = np.ascontiguousarray(
-    FOURIER.reshape(YL, Z, C, YL, Z, C).transpose(1, 4, 3, 5, 0, 2).reshape(Z, 256)
-).astype(np.float32)
-INVERSE = np.ascontiguousarray(
-    FOURIER.reshape(YL, Z, C, YL, Z, C).transpose(0, 2, 4, 1, 3, 5).reshape(YL * C * Z, 64)
-).astype(np.float32)
+FOURIER = fourier_table(BLADES).reshape(YL, Z, C, YL, Z, C)
+EYE = np.eye(TS)
+
+
+def halves(table):
+    high = table.astype(np.float32).astype(BF)
+    low = (table - high.astype(np.float64)).astype(np.float32).astype(BF)
+    return np.stack([high, low], axis=1)
+
+
+def forward_table():
+    table = FOURIER.reshape(YL, D, 2, C, YL, Z, C).transpose(0, 3, 1, 2, 5, 4, 6)
+    table = np.stack([table, table[:, :, :, ::-1]]).reshape(2, BLADES, BLADES)
+    return np.einsum("pij,tu->pitju", table, EYE).reshape(2, BLADES * TS, BLADES * TS)
+
+
+def inverse_table():
+    table = FOURIER.reshape(YL, D, 2, C, YL, Z, C).transpose(5, 4, 6, 0, 3, 1, 2)
+    table = np.stack([table[z] if z % 2 == 0 else table[z][..., ::-1] for z in range(Z)])
+    table = table.reshape(Z, 4, BLADES)
+    return np.einsum("zij,tu->zitju", table, EYE).reshape(Z, 4 * TS, BLADES * TS)
+
+
+FORWARD = halves(forward_table())
+INVERSE = halves(inverse_table())
+PACK = 2 * MODES + NB
 
 
 def dot_nt(a, b, **kw):
@@ -62,7 +80,7 @@
         ref[NB : NB + 16] = index
 
 
-def project_kernel(pos, wake_ref, *refs):
+def project_kernel(pos, kept_ref, wake_ref, *refs):
     out_ref = refs[-1]
     basis = jnp.concatenate([ref[0:NB] for ref in refs[:4]], axis=0)
     table = dot_nt(wake_ref[...].reshape(YL * Z * PH, HALF), basis).astype(BF)
@@ -105,72 +123,82 @@
     out_ref[...] = jnp.broadcast_to(block[None], out_ref.shape)
 
 
-def forward_kernel(table_ref, in_ref, out_ref):
-    acc = [None] * 4
-    for z in range(Z):
-        block = in_ref[z].astype(F32)
-        for q in range(4):
-            part = block[q * TS : (q + 1) * TS]
-            for h in range(4):
-                term = part * table_ref[(z * 4 + q) * 4 + h]
-                acc[h] = term if acc[h] is None else acc[h] + term
-    for h in range(4):
-        out_ref[h * D : (h + 1) * D] = jnp.broadcast_to(acc[h].astype(BF)[None], (D, TS, NB))
-
-
-def modal_kernel(pos, in_ref, shapes_ref, flex_ref, damp_ref, out_ref, hold_ref):
-    force = in_ref[...].reshape(NT, NB)
-    shapes = shapes_ref[...]
-    real = dot_nt(shapes, force)
-    imag = None
-    damp = jnp.concatenate([damp_ref[...], jnp.zeros((6, MODES), F32)], axis=0).T
+def fourier_sum(table_ref, in_ref):
+    block = in_ref[...].reshape(BLADES * TS, NB)
+    return sum(
+        jnp.dot(table_ref[k], block, preferred_element_type=F32) for k in range(2)
+    ).astype(BF)
+
+
+def forward_kernel(table_ref, in_ref, kept_ref, out_ref):
+    out_ref[...] = fourier_sum(table_ref, in_ref).reshape(PEERS, 2 * TS, NB)
+
+
+def inverse_kernel(table_ref, in_ref, out_ref):
+    block = fourier_sum(table_ref, in_ref)
+    for s in range(4):
+        part = block[s * TS : (s + 1) * TS]
+        out_ref[s * D : (s + 1) * D] = jnp.broadcast_to(part[None], (D, TS, NB))
+
+
+def parameter_kernel(shapes_ref, flex_ref, omega_ref, zeta_ref, out_ref):
+    damp = jnp.concatenate([omega_ref[...], zeta_ref[...], jnp.zeros((6, MODES), F32)], axis=0).T
     omega, zeta = damp[:, 0:1], damp[:, 1:2]
     size = jnp.exp(-omega * zeta)
     angle = omega * jnp.sqrt(1.0 - zeta * zeta)
-    pr, pi = size * jnp.cos(angle), size * jnp.sin(angle)
+    real, imag = size * jnp.cos(angle), size * jnp.sin(angle)
+    lane = lax.broadcasted_iota(jnp.int32, (MODES, NB), 1)
+    powers = jnp.zeros((MODES, NB), F32)
+    for k in range(8):
+        powers = jnp.where(lane == 2 * k, real, jnp.where(lane == 2 * k + 1, imag, powers))
+        real, imag = real * real - imag * imag, 2.0 * real * imag
+    high = powers.astype(BF).astype(F32)
+    middle = (powers - high).astype(BF).astype(F32)
+    low = powers - high - middle
+    terms = high + pltpu.roll(middle, 16, 1) + pltpu.roll(low, 32, 1)
+    out_ref[...] = jnp.concatenate(
+        [shapes_ref[...].astype(F32), terms, flex_ref[...].astype(F32)], axis=0
+    ).astype(BF)
+
+
+def respond(force, pack_ref):
+    shapes = pack_ref[0 : 2 * MODES][0:MODES]
+    terms = pack_ref[0 : 2 * MODES][MODES : 2 * MODES].astype(F32)
+    powers = terms[:, 0:16] + terms[:, 16:32] + terms[:, 32:48]
+    real = dot_nt(shapes, force)
+    imag = None
     lane = lax.broadcasted_iota(jnp.int32, (MODES, NT), 1)
-    shift = 1
-    while shift < NT:
-        keep = lane >= shift
-        sr = jnp.where(keep, pltpu.roll(real, shift, 1), 0.0)
+    for k in range(8):
+        pr, pi = powers[:, 2 * k : 2 * k + 1], powers[:, 2 * k + 1 : 2 * k + 2]
+        keep = lane >= 2**k
+        sr = jnp.where(keep, pltpu.roll(real, 2**k, 1), 0.0)
         if imag is None:
             real, imag = real + pr * sr, pi * sr
         else:
-            si = jnp.where(keep, pltpu.roll(imag, shift, 1), 0.0)
+            si = jnp.where(keep, pltpu.roll(imag, 2**k, 1), 0.0)
             real, imag = real + (pr * sr - pi * si), imag + (pr * si + pi * sr)
-        pr, pi = pr * pr - pi * pi, 2.0 * pr * pi
-        shift *= 2
-    hold_ref[...] = lax.dot_general(
+    return lax.dot_general(
         imag,
         shapes.astype(F32),
         (((0,), (0,)), ((), ())),
         precision=HI,
         preferred_element_type=F32,
-    ) + dot_nt(force, flex_ref[...])
-    block = hold_ref[pl.ds(pl.multiple_of(pos[2] * TD, TD), TD), :].astype(BF)
-    out_ref[...] = jnp.broadcast_to(block[None], out_ref.shape)
-
-
-def inverse_kernel(table_ref, in_ref, out_ref):
-    acc = [None] * 4
-    for z in range(Z):
-        block = in_ref[z].astype(F32)
-        for s in range(4):
-            term = block * table_ref[z * 4 + s]
-            acc[s] = term if acc[s] is None else acc[s] + term
-    for s in range(4):
-        out_ref[s * D : (s + 1) * D] = jnp.broadcast_to(acc[s].astype(BF)[None], (D, TD, NB))
+    ) + dot_nt(force, pack_ref[2 * MODES : PACK])
+
+
+def modal_kernel(in_ref, first_ref, second_ref, out_ref):
+    parts = []
+    for e, pack_ref in enumerate((first_ref, second_ref)):
+        force = in_ref[...].astype(F32)[:, e * TS : (e + 1) * TS].reshape(NT, NB).astype(BF)
+        parts.append(respond(force, pack_ref).reshape(PEERS, TS, NB))
+    out_ref[...] = jnp.concatenate(parts, axis=1).astype(BF)
 
 
 CHUNKS = 4
 
 
 def stress_kernel(in_ref, map_ref, out_ref, hold_ref, sems):
-    total = None
-    for q in range(YL * C):
-        part = in_ref[q * D : (q + 1) * D].astype(F32)
-        total = part if total is None else total + part
-    motion = total.reshape(NT, NB).astype(BF)
+    motion = in_ref[...].reshape(NT, NB)
     step = map_ref.shape[0] // CHUNKS
     copies = []
     for k in range(CHUNKS):
@@ -184,6 +212,7 @@
 
 VMEM = pl.BlockSpec(memory_space=pltpu.VMEM)
 SMEM = pl.BlockSpec(memory_space=pltpu.SMEM)
+HBM = pl.BlockSpec(memory_space=pl.ANY)
 
 
 def call(kernel, outs, specs, *args, out_specs=None, scratch=()):
@@ -201,11 +230,18 @@
 
 def local(wake, basis, block_index, phase_index, shapes, flex, omega, zeta, stress_map):
     yl, z, c = lax.axis_index("yl"), lax.axis_index("z"), lax.axis_index("c")
-    d = lax.axis_index("x") * 2 + lax.axis_index("yh")
-    pos = jnp.stack([yl, c, d]).astype(jnp.int32)
-    forward = lax.dynamic_slice(jnp.asarray(FORWARD), (z, 0), (1, 256)).reshape(256)
-    inverse = lax.dynamic_slice(jnp.asarray(INVERSE), ((yl * C + c) * Z + z, 0), (1, 64)).reshape(64)
-    damp = jnp.concatenate([omega, zeta], axis=0)
+    pos = jnp.stack([yl, c]).astype(jnp.int32)
+    forward = lax.dynamic_slice(
+        jnp.asarray(FORWARD), (z & 1, 0, 0, 0), (1,) + FORWARD.shape[1:]
+    )[0]
+    inverse = lax.dynamic_slice(jnp.asarray(INVERSE), (z, 0, 0, 0), (1,) + INVERSE.shape[1:])[0]
+
+    pack = call(parameter_kernel, [(PACK, NB)], [VMEM] * 4, shapes[0], flex[0], omega, zeta)
+    route = [
+        [(i * D + k, (2 * k + (i & 1 ^ e)) * D + i // 2) for i in range(Z) for k in range(D)]
+        for e in range(2)
+    ]
+    first = lax.ppermute(pack, ("z", "x", "yh"), route[0])
 
     spread = call(spread_kernel, [(YL * Z, PH, HALF)], [VMEM], wake[0])
     blocks = lax.all_to_all(spread, ("yl", "z"), 0, 0, tiled=True)
@@ -227,32 +263,27 @@
     picked = call(
         project_kernel,
         [(PEERS, 4 * TS, NB)],
-        [SMEM] + [VMEM] * 5,
+        [SMEM, HBM] + [VMEM] * 5,
         pos,
+        first,
         blocks,
         near,
         by_yl,
         by_c,
         by_both,
     )
+    pack, picked = lax.optimization_barrier((pack, picked))
+    second = lax.ppermute(pack, ("z", "x", "yh"), route[1])
     parts = lax.all_to_all(picked, PLANE, 0, 0, tiled=True)
     forcing = call(gather_sum_kernel, [(Z, 4 * TS, NB)], [VMEM], parts)
     forcing = lax.all_to_all(forcing, "z", 0, 0, tiled=True)
-    harmonic = call(forward_kernel, [(PEERS, TS, NB)], [SMEM, VMEM], forward, forcing)
+    harmonic = call(
+        forward_kernel, [(PEERS, 2 * TS, NB)], [VMEM, VMEM, HBM], forward, forcing, second
+    )
     harmonic = lax.all_to_all(harmonic, PLANE, 0, 0, tiled=True)
-    physical = call(
-        modal_kernel,
-        [(Z, TD, NB)],
-        [SMEM] + [VMEM] * 4,
-        pos,
-        harmonic,
-        shapes[0],
-        flex[0],
-        damp,
-        scratch=[pltpu.VMEM((NT, NB), F32)],
-    )
-    physical = lax.all_to_all(physical, "z", 0, 0, tiled=True)
-    sectoral = call(inverse_kernel, [(PEERS, TD, NB)], [SMEM, VMEM], inverse, physical)
+    physical = call(modal_kernel, [(PEERS, 2 * TS, NB)], [VMEM] * 3, harmonic, first, second)
+    physical = lax.all_to_all(physical, PLANE, 0, 0, tiled=True)
+    sectoral = call(inverse_kernel, [(PEERS, TS, NB)], [VMEM] * 2, inverse, physical)
     sectoral = lax.all_to_all(sectoral, PLANE, 0, 0, tiled=True)
     rows = stress_map.shape[1]
     stress = call(
@@ -261,7 +292,7 @@
         [VMEM, VMEM],
         sectoral,
         stress_map[0],
-        out_specs=[pl.BlockSpec(memory_space=pl.ANY)],
+        out_specs=[HBM],
         scratch=[pltpu.VMEM((rows, NT), BF), pltpu.SemaphoreType.DMA((CHUNKS,))],
     )
     return stress[None]

time: 135 us -> 141 us (1.044)
  waiting for transfers between devices: 48.4 us -> 27.4 us
  blocking collectives: 33.1 us -> 53.3 us
  local copies, waits for them, and re-layouts: 2.92 us -> 8.04 us
  starting transfers between devices: 40.4 us -> 42.5 us
    all_to_all x0 -> x1, blocking collectives: none -> 20.2 us  [local(): harmonic = lax.all_to_all(harmonic, PLANE, 0, 0, tiled=True)]
    all_to_all x2 -> x1, waiting for transfers between devices: 18.6 us -> 6.89 us  [local(): physical = lax.all_to_all(physical, PLANE, 0, 0, tiled=True)]
    all_to_all x1, waiting for transfers between devices: 11.8 us -> 3.92 us  [local(): forcing = lax.all_to_all(forcing, 'z', 0, 0, tiled=True)]
    all_to_all x2 -> x1, starting transfers between devices: 10.4 us -> 3.86 us  [local(): physical = lax.all_to_all(physical, PLANE, 0, 0, tiled=True)]
    ppermute x1, waiting for transfers between devices: 9.5 us -> 3.44 us  [local(): by_both = lax.ppermute(far, ('yl', 'c'), [(0, 3), (1, 2), (2, 1), (3, 0)])]
    ppermute x1, waiting for transfers between devices: 0.94 us -> 6.64 us  [local(): by_yl = lax.ppermute(far, 'yl', swap)]
    all_to_all x1, waiting for transfers between devices: 7.58 us -> 2.63 us  [local(): blocks = lax.all_to_all(spread, ('yl', 'z'), 0, 0, tiled=True)]
    all_to_all x1, starting transfers between devices: 4.41 us -> 9.3 us  [local(): forcing = lax.all_to_all(forcing, 'z', 0, 0, tiled=True)]
  transfers between devices with their start and end apart: 7 -> 8, of which waited for: 6 -> 6; matrix products, arithmetic and copies ran while one was open for 1% -> 2% of each run, Pallas kernels for 0% -> 1%
where the time goes in v3:
time: 141 us; the launch traced here: 140 us
  blocking collectives  53.3 us (38%)
  starting transfers between devices  42.5 us (30%)
  waiting for transfers between devices  27.4 us (19%)
  Pallas kernels  8.28 us (6%)
  local copies, waits for them, and re-layouts  8.04 us (6%)
    all_to_all x1, blocking collectives, local(): parts = lax.all_to_all(picked, PLANE, 0, 0, tiled=True)  22.2 us
    all_to_all x1, blocking collectives, local(): harmonic = lax.all_to_all(harmonic, PLANE, 0, 0, tiled=True)  20.2 us
    all_to_all x1, starting transfers between devices, local(): blocks = lax.all_to_all(spread, ('yl', 'z'), 0, 0, tiled=True)  17 us
    all_to_all x1, blocking collectives, local(): sectoral = lax.all_to_all(sectoral, PLANE, 0, 0, tiled=True)  10.9 us
    all_to_all x1, starting transfers between devices, local(): forcing = lax.all_to_all(forcing, 'z', 0, 0, tiled=True)  9.3 us
    pallas_call x9, Pallas kernels, call(): pl.pallas_call(kernel, out_shape=outs, in_specs=specs, out_specs=out_spec...  8.28 us
    all_to_all x1, waiting for transfers between devices, local(): physical = lax.all_to_all(physical, PLANE, 0, 0, tiled=True)  6.89 us
    ppermute x1, waiting for transfers between devices, local(): by_yl = lax.ppermute(far, 'yl', swap)  6.64 us
  transfers between devices with their start and end apart: 8, of which 6 were waited for; matrix products, arithmetic and copies ran while one was open for 2% of the time, Pallas kernels for 1%

profile of v3, /device:TPU:1, one launch (start us, length us, event | category | flops | bytes accessed | tf_op | source)
XLA Modules:
  0.0 139.8 jit_solution(674335318301245266)
XLA Ops:
  0.0 0.0 copy-start.3
  0.0 0.7 copy-done.3
  0.7 0.8 shard_map.110
  1.6 17.0 %all-to-all-start = ((bf16[32,8,896]{2,1,0:T(8,128)(2,1)}), bf16[32,8,896]{2,1,0:T(8,128)(2,1)S(1)}, u32[]{:S(2)}, u32[]{:S(2)}) async-start(bf16[32,8,896]{2,1,0:T(8,128)(2,1)} %shard_map.110), calls=%async_computation | async-start | bytes 917504 | tf_op jit(solution)/shard_map/all_to_all | solution.py:247
  18.6 0.1 pad_add_fusion.pos
  18.7 0.0 copy-start.1
  18.7 1.0 copy-done.1
  19.7 0.0 copy-start.5
  19.7 0.7 copy-done.5
  20.4 0.0 copy-start.6
  20.4 0.7 copy-done.6
  21.1 0.6 shard_map.111
  21.7 2.9 %collective-permute-start.2 = (bf16[144,896]{1,0:T(8,128)(2,1)S(1)}, bf16[144,896]{1,0:T(8,128)(2,1)S(1)}, u32[]{:S(2)}, u32[]{:S(2)}) collective-permute-start(bf16[144,896]{1,0:T(8,128)(2,1)S(1)} %get-tuple-element.9.refs_0_), channel_id=1, source_target_pairs={{0,8},{8,0},{1,9},{9,1},{2,10},{10,2},{3,11},{11,3},{4,12},{12,4},... | collective-permute-start | bytes 774152 | tf_op jit(solution)/shard_map/ppermute | solution.py:260
  24.5 3.3 %collective-permute-start.3 = (bf16[144,896]{1,0:T(8,128)(2,1)S(1)}, bf16[144,896]{1,0:T(8,128)(2,1)S(1)}, u32[]{:S(2)}, u32[]{:S(2)}) collective-permute-start(bf16[144,896]{1,0:T(8,128)(2,1)S(1)} %get-tuple-element.10), channel_id=1, source_target_pairs={{0,264},{8,256},{256,8},{264,0},{1,265},{9,257},{257,9},{265,1},{2... | collective-permute-start | bytes 774152 | tf_op jit(solution)/shard_map/ppermute | solution.py:261
  27.9 2.0 %collective-permute-start.1 = (bf16[144,896]{1,0:T(8,128)(2,1)S(1)}, bf16[144,896]{1,0:T(8,128)(2,1)S(1)}, u32[]{:S(2)}, u32[]{:S(2)}) collective-permute-start(bf16[144,896]{1,0:T(8,128)(2,1)S(1)} %get-tuple-element.10), channel_id=1, source_target_pairs={{0,256},{256,0},{1,257},{257,1},{2,258},{258,2},{3,259},{259,3},{4... | collective-permute-start | bytes 774152 | tf_op jit(solution)/shard_map/ppermute | solution.py:259
  29.9 0.0 copy-start.2
  29.9 0.7 copy-done.2
  30.6 0.0 copy-start.4
  30.6 0.7 copy-done.4
  31.3 0.0 copy-start.7
  31.4 0.7 copy-done.7
  32.0 0.0 copy-start.8
  32.0 0.7 copy-done.8
  32.7 0.4 shard_map.109
  33.1 0.7 collective-permute-start
  33.8 0.0 collective-permute-done.kept_ref.first_ref
  33.8 0.0 collective-permute-done.2.refs_2_
  33.8 3.4 %collective-permute-done.3.refs_3_ = bf16[144,896]{1,0:T(8,128)(2,1)S(1)} collective-permute-done((bf16[144,896]{1,0:T(8,128)(2,1)S(1)}, bf16[144,896]{1,0:T(8,128)(2,1)S(1)}, u32[]{:S(2)}, u32[]{:S(2)}) %collective-permute-start.3) | collective-permute-done | bytes 258080 | tf_op jit(solution)/shard_map/ppermute | solution.py:261
  37.2 6.6 %collective-permute-done.1.refs_1_ = bf16[144,896]{1,0:T(8,128)(2,1)S(1)} collective-permute-done((bf16[144,896]{1,0:T(8,128)(2,1)S(1)}, bf16[144,896]{1,0:T(8,128)(2,1)S(1)}, u32[]{:S(2)}, u32[]{:S(2)}) %collective-permute-start.1) | collective-permute-done | bytes 258080 | tf_op jit(solution)/shard_map/ppermute | solution.py:259
  43.9 2.6 %all-to-all-done.wake_ref = bf16[32,8,896]{2,1,0:T(8,128)(2,1)S(1)} async-done(((bf16[32,8,896]{2,1,0:T(8,128)(2,1)}), bf16[32,8,896]{2,1,0:T(8,128)(2,1)S(1)}, u32[]{:S(2)}, u32[]{:S(2)}) %all-to-all-start) | async-done | bytes 458784 | tf_op jit(solution)/shard_map/all_to_all | solution.py:247
  46.5 1.3 shard_map.112
  47.8 22.2 %all_to_all.30.in_ref = bf16[32,32,128]{2,1,0:T(8,128)(2,1)S(1)} all-to-all(bf16[32,32,128]{2,1,0:T(8,128)(2,1)S(1)} %shard_map.112), channel_id=1, replica_groups=mesh['yl'=2,'z'=16,'c'=2,'x'=4,'yh'=2] {'yl','c','x','yh'}, dimensions={0} | all-to-all | bytes 524288 | tf_op jit(solution)/shard_map/all_to_all | solution.py:277
  70.0 0.7 shard_map.113
  70.7 9.3 %all-to-all-start.2 = ((bf16[16,32,128]{2,1,0:T(8,128)(2,1)}), bf16[16,32,128]{2,1,0:T(8,128)(2,1)S(1)}, u32[]{:S(2)}, u32[]{:S(2)}) async-start(bf16[16,32,128]{2,1,0:T(8,128)(2,1)} %shard_map.113), calls=%async_computation.2 | async-start | bytes 262144 | tf_op jit(solution)/shard_map/all_to_all | solution.py:279
  80.0 0.0 copy-start
  80.1 3.4 %collective-permute-start.4 = (bf16[208,128]{1,0:T(8,128)(2,1)S(1)}, bf16[208,128]{1,0:T(8,128)(2,1)S(1)}, u32[]{:S(2)}, u32[]{:S(2)}) collective-permute-start(bf16[208,128]{1,0:T(8,128)(2,1)S(1)} %shard_map.109), channel_id=1, source_target_pairs={{0,16},{1,48},{2,80},{3,112},{4,144},{5,176},{6,208},{7,240},{16,0... | collective-permute-start | bytes 159752 | tf_op jit(solution)/shard_map/ppermute | solution.py:276
  83.5 1.3 dynamic-slice_bitcast_fusion.table_ref
  84.8 3.9 %collective-permute-done.4.kept_ref.second_ref = bf16[208,128]{1,0:T(8,128)(2,1)S(1)} collective-permute-done((bf16[208,128]{1,0:T(8,128)(2,1)S(1)}, bf16[208,128]{1,0:T(8,128)(2,1)S(1)}, u32[]{:S(2)}, u32[]{:S(2)}) %collective-permute-start.4) | collective-permute-done | bytes 53280 | tf_op jit(solution)/shard_map/ppermute | solution.py:276
  88.7 3.9 %all-to-all-done.2.in_ref = bf16[16,32,128]{2,1,0:T(8,128)(2,1)S(1)} async-done(((bf16[16,32,128]{2,1,0:T(8,128)(2,1)}), bf16[16,32,128]{2,1,0:T(8,128)(2,1)S(1)}, u32[]{:S(2)}, u32[]{:S(2)}) %all-to-all-start.2) | async-done | bytes 131104 | tf_op jit(solution)/shard_map/all_to_all | solution.py:279
  92.6 0.4 shard_map.114
  93.0 20.2 %all_to_all.31.in_ref = bf16[32,16,128]{2,1,0:T(8,128)(2,1)S(1)} all-to-all(bf16[32,16,128]{2,1,0:T(8,128)(2,1)S(1)} %shard_map.114), channel_id=1, replica_groups=mesh['yl'=2,'z'=16,'c'=2,'x'=4,'yh'=2] {'yl','c','x','yh'}, dimensions={0} | all-to-all | bytes 262144 | tf_op jit(solution)/shard_map/all_to_all | solution.py:283
  113.2 2.6 %shard_map.115 = bf16[32,16,128]{2,1,0:T(8,128)(2,1)} custom-call(bf16[32,16,128]{2,1,0:T(8,128)(2,1)S(1)} %all_to_all.31.in_ref, bf16[208,128]{1,0:T(8,128)(2,1)S(1)} %collective-permute-done.kept_ref.first_ref, bf16[208,128]{1,0:T(8,128)(2,1)S(1)} %collective-permute-done.4.kept_ref.second_ref), custom_call_target="tpu_custom_call" | custom-call | tf_op jit(solution)/shard_map/pallas_call | solution.py:220
  115.8 3.9 %all-to-all-start.4 = ((bf16[32,16,128]{2,1,0:T(8,128)(2,1)}), bf16[32,16,128]{2,1,0:T(8,128)(2,1)S(1)}, u32[]{:S(2)}, u32[]{:S(2)}) async-start(bf16[32,16,128]{2,1,0:T(8,128)(2,1)} %shard_map.115), calls=%async_computation.4 | async-start | bytes 262144 | tf_op jit(solution)/shard_map/all_to_all | solution.py:285
  119.6 0.9 dynamic-slice_bitcast_fusion.1.table_ref
  120.5 6.9 %all-to-all-done.4.in_ref = bf16[32,16,128]{2,1,0:T(8,128)(2,1)S(1)} async-done(((bf16[32,16,128]{2,1,0:T(8,128)(2,1)}), bf16[32,16,128]{2,1,0:T(8,128)(2,1)S(1)}, u32[]{:S(2)}, u32[]{:S(2)}) %all-to-all-start.4) | async-done | bytes 131104 | tf_op jit(solution)/shard_map/all_to_all | solution.py:285
  127.4 0.2 shard_map.116
  127.6 10.9 %all_to_all.32.in_ref = bf16[32,8,128]{2,1,0:T(8,128)(2,1)S(1)} all-to-all(bf16[32,8,128]{2,1,0:T(8,128)(2,1)S(1)} %shard_map.116), channel_id=1, replica_groups=mesh['yl'=2,'z'=16,'c'=2,'x'=4,'yh'=2] {'yl','c','x','yh'}, dimensions={0} | all-to-all | bytes 131072 | tf_op jit(solution)/shard_map/all_to_all | solution.py:287
  138.5 0.0 copy-done
  138.5 1.3 shard_map.117
Async XLA Ops:
  0.0 0.7 copy-start.3
  1.6 45.0 %all-to-all-start = ((bf16[32,8,896]{2,1,0:T(8,128)(2,1)}), bf16[32,8,896]{2,1,0:T(8,128)(2,1)S(1)}, u32[]{:S(2)}, u32[]{:S(2)}) async-start(bf16[32,8,896]{2,1,0:T(8,128)(2,1)} %shard_map.110), calls=%async_computation | async-start | bytes 917504 | tf_op jit(solution)/shard_map/all_to_all | solution.py:247
  18.7 1.0 copy-start.1
  19.7 0.7 copy-start.5
  20.4 0.7 copy-start.6
  21.7 12.1 %collective-permute-start.2 = (bf16[144,896]{1,0:T(8,128)(2,1)S(1)}, bf16[144,896]{1,0:T(8,128)(2,1)S(1)}, u32[]{:S(2)}, u32[]{:S(2)}) collective-permute-start(bf16[144,896]{1,0:T(8,128)(2,1)S(1)} %get-tuple-element.9.refs_0_), channel_id=1, source_target_pairs={{0,8},{8,0},{1,9},{9,1},{2,10},{10,2},{3,11},{11,3},{4,12},{12,4},... | collective-permute-start | bytes 774152 | tf_op jit(solution)/shard_map/ppermute | solution.py:260
  24.5 12.7 %collective-permute-start.3 = (bf16[144,896]{1,0:T(8,128)(2,1)S(1)}, bf16[144,896]{1,0:T(8,128)(2,1)S(1)}, u32[]{:S(2)}, u32[]{:S(2)}) collective-permute-start(bf16[144,896]{1,0:T(8,128)(2,1)S(1)} %get-tuple-element.10), channel_id=1, source_target_pairs={{0,264},{8,256},{256,8},{264,0},{1,265},{9,257},{257,9},{265,1},{2... | collective-permute-start | bytes 774152 | tf_op jit(solution)/shard_map/ppermute | solution.py:261
  27.9 16.0 %collective-permute-start.1 = (bf16[144,896]{1,0:T(8,128)(2,1)S(1)}, bf16[144,896]{1,0:T(8,128)(2,1)S(1)}, u32[]{:S(2)}, u32[]{:S(2)}) collective-permute-start(bf16[144,896]{1,0:T(8,128)(2,1)S(1)} %get-tuple-element.10), channel_id=1, source_target_pairs={{0,256},{256,0},{1,257},{257,1},{2,258},{258,2},{3,259},{259,3},{4... | collective-permute-start | bytes 774152 | tf_op jit(solution)/shard_map/ppermute | solution.py:259
  29.9 0.8 copy-start.2
  30.6 0.7 copy-start.4
  31.3 0.7 copy-start.7
  32.0 0.7 copy-start.8
  33.1 0.7 collective-permute-start
  70.7 21.8 %all-to-all-start.2 = ((bf16[16,32,128]{2,1,0:T(8,128)(2,1)}), bf16[16,32,128]{2,1,0:T(8,128)(2,1)S(1)}, u32[]{:S(2)}, u32[]{:S(2)}) async-start(bf16[16,32,128]{2,1,0:T(8,128)(2,1)} %shard_map.113), calls=%async_computation.2 | async-start | bytes 262144 | tf_op jit(solution)/shard_map/all_to_all | solution.py:279
  80.0 58.4 %copy-start = (bf16[1,2048,128]{2,1,0:T(8,128)(2,1)S(1)}, bf16[1,2048,128]{2,1,0:T(8,128)(2,1)}, u32[]{:S(2)}) copy-start(bf16[1,2048,128]{2,1,0:T(8,128)(2,1)} %param.19) | copy-start | bytes 1572868
  80.1 8.6 %collective-permute-start.4 = (bf16[208,128]{1,0:T(8,128)(2,1)S(1)}, bf16[208,128]{1,0:T(8,128)(2,1)S(1)}, u32[]{:S(2)}, u32[]{:S(2)}) collective-permute-start(bf16[208,128]{1,0:T(8,128)(2,1)S(1)} %shard_map.109), channel_id=1, source_target_pairs={{0,16},{1,48},{2,80},{3,112},{4,144},{5,176},{6,208},{7,240},{16,0... | collective-permute-start | bytes 159752 | tf_op jit(solution)/shard_map/ppermute | solution.py:276
  115.8 11.6 %all-to-all-start.4 = ((bf16[32,16,128]{2,1,0:T(8,128)(2,1)}), bf16[32,16,128]{2,1,0:T(8,128)(2,1)S(1)}, u32[]{:S(2)}, u32[]{:S(2)}) async-start(bf16[32,16,128]{2,1,0:T(8,128)(2,1)} %shard_map.115), calls=%async_computation.4 | async-start | bytes 262144 | tf_op jit(solution)/shard_map/all_to_all | solution.py:285

commit v4 on v2

--- a/solution.py
+++ b/solution.py
@@ -31,9 +31,17 @@
 
 
 FOURIER = fourier_table(BLADES)
-FORWARD = np.ascontiguousarray(
-    FOURIER.reshape(YL, Z, C, YL, Z, C).transpose(1, 4, 3, 5, 0, 2).reshape(Z, 256)
-).astype(np.float32)
+
+
+def forward_table():
+    table = FOURIER.reshape(YL, Z, C, YL, Z, C).transpose(1, 0, 2, 4, 3, 5)
+    table = np.einsum("zij,tu->zitju", table.reshape(Z, 4, BLADES), np.eye(TS))
+    table = table.reshape(Z, 4 * TS, BLADES * TS).astype(np.float32)
+    high = table.astype(BF)
+    return np.stack([high, (table - high.astype(np.float32)).astype(BF)], axis=1)
+
+
+FORWARD = forward_table()
 INVERSE = np.ascontiguousarray(
     FOURIER.reshape(YL, Z, C, YL, Z, C).transpose(0, 2, 4, 1, 3, 5).reshape(YL * C * Z, 64)
 ).astype(np.float32)
@@ -45,10 +53,16 @@
     )
 
 
-def spread_kernel(in_ref, out_ref):
+def spread_kernel(in_ref, out_ref, sem):
+    copies = []
     for half in range(YL):
-        part = in_ref[:, half * HALF : (half + 1) * HALF]
-        out_ref[half * Z : (half + 1) * Z] = jnp.broadcast_to(part[None], (Z, PH, HALF))
+        part = in_ref.at[:, pl.ds(half * HALF, HALF)]
+        for z in range(Z):
+            k = half * Z + z
+            copies.append(pltpu.make_async_copy(part, out_ref.at[k], sem.at[k]))
+            copies[-1].start()
+    for copy in copies:
+        copy.wait()
 
 
 def pack_kernel(pos, basis_ref, block_ref, phase_ref, near_ref, far_ref):
@@ -106,47 +120,51 @@
 
 
 def forward_kernel(table_ref, in_ref, out_ref):
-    acc = [None] * 4
-    for z in range(Z):
-        block = in_ref[z].astype(F32)
-        for q in range(4):
-            part = block[q * TS : (q + 1) * TS]
-            for h in range(4):
-                term = part * table_ref[(z * 4 + q) * 4 + h]
-                acc[h] = term if acc[h] is None else acc[h] + term
+    block = in_ref[...].reshape(BLADES * TS, NB)
+    block = sum(jnp.dot(table_ref[k], block, preferred_element_type=F32) for k in range(2))
     for h in range(4):
-        out_ref[h * D : (h + 1) * D] = jnp.broadcast_to(acc[h].astype(BF)[None], (D, TS, NB))
-
-
-def modal_kernel(pos, in_ref, shapes_ref, flex_ref, damp_ref, out_ref, hold_ref):
-    force = in_ref[...].reshape(NT, NB)
-    shapes = shapes_ref[...]
-    real = dot_nt(shapes, force)
-    imag = None
-    damp = jnp.concatenate([damp_ref[...], jnp.zeros((6, MODES), F32)], axis=0).T
+        part = block[h * TS : (h + 1) * TS].astype(BF)
+        out_ref[h * D : (h + 1) * D] = jnp.broadcast_to(part[None], (D, TS, NB))
+
+
+def powers_kernel(omega_ref, zeta_ref, out_ref):
+    damp = jnp.concatenate([omega_ref[...], zeta_ref[...], jnp.zeros((6, MODES), F32)], axis=0).T
     omega, zeta = damp[:, 0:1], damp[:, 1:2]
     size = jnp.exp(-omega * zeta)
     angle = omega * jnp.sqrt(1.0 - zeta * zeta)
-    pr, pi = size * jnp.cos(angle), size * jnp.sin(angle)
+    real, imag = size * jnp.cos(angle), size * jnp.sin(angle)
+    lane = lax.broadcasted_iota(jnp.int32, (MODES, NB), 1)
+    powers = jnp.zeros((MODES, NB), F32)
+    for k in range(8):
+        powers = jnp.where(lane == 2 * k, real, jnp.where(lane == 2 * k + 1, imag, powers))
+        real, imag = real * real - imag * imag, 2.0 * real * imag
+    out_ref[...] = powers
+
+
+def modal_kernel(pos, in_ref, shapes_ref, flex_ref, powers_ref, out_ref, hold_ref):
+    force = in_ref[...].reshape(NT, NB)
+    shapes = shapes_ref[...]
+    hold_ref[...] = dot_nt(force, flex_ref[...])
+    real = dot_nt(shapes, force)
+    imag = None
+    powers = powers_ref[...]
     lane = lax.broadcasted_iota(jnp.int32, (MODES, NT), 1)
-    shift = 1
-    while shift < NT:
-        keep = lane >= shift
-        sr = jnp.where(keep, pltpu.roll(real, shift, 1), 0.0)
+    for k in range(8):
+        pr, pi = powers[:, 2 * k : 2 * k + 1], powers[:, 2 * k + 1 : 2 * k + 2]
+        keep = lane >= 2**k
+        sr = jnp.where(keep, pltpu.roll(real, 2**k, 1), 0.0)
         if imag is None:
             real, imag = real + pr * sr, pi * sr
         else:
-            si = jnp.where(keep, pltpu.roll(imag, shift, 1), 0.0)
+            si = jnp.where(keep, pltpu.roll(imag, 2**k, 1), 0.0)
             real, imag = real + (pr * sr - pi * si), imag + (pr * si + pi * sr)
-        pr, pi = pr * pr - pi * pi, 2.0 * pr * pi
-        shift *= 2
-    hold_ref[...] = lax.dot_general(
+    hold_ref[...] += lax.dot_general(
         imag,
         shapes.astype(F32),
         (((0,), (0,)), ((), ())),
         precision=HI,
         preferred_element_type=F32,
-    ) + dot_nt(force, flex_ref[...])
+    )
     block = hold_ref[pl.ds(pl.multiple_of(pos[2] * TD, TD), TD), :].astype(BF)
     out_ref[...] = jnp.broadcast_to(block[None], out_ref.shape)
 
@@ -184,10 +202,11 @@
 
 VMEM = pl.BlockSpec(memory_space=pltpu.VMEM)
 SMEM = pl.BlockSpec(memory_space=pltpu.SMEM)
-
-
-def call(kernel, outs, specs, *args, out_specs=None, scratch=()):
-    outs = [jax.ShapeDtypeStruct(shape, BF) for shape in outs]
+HBM = pl.BlockSpec(memory_space=pl.ANY)
+
+
+def call(kernel, outs, specs, *args, out_specs=None, scratch=(), dtype=BF):
+    outs = [jax.ShapeDtypeStruct(shape, dtype) for shape in outs]
     got = pl.pallas_call(
         kernel,
         out_shape=outs,
@@ -203,11 +222,18 @@
     yl, z, c = lax.axis_index("yl"), lax.axis_index("z"), lax.axis_index("c")
     d = lax.axis_index("x") * 2 + lax.axis_index("yh")
     pos = jnp.stack([yl, c, d]).astype(jnp.int32)
-    forward = lax.dynamic_slice(jnp.asarray(FORWARD), (z, 0), (1, 256)).reshape(256)
+    forward = lax.dynamic_slice(jnp.asarray(FORWARD), (z, 0, 0, 0), (1,) + FORWARD.shape[1:])[0]
     inverse = lax.dynamic_slice(jnp.asarray(INVERSE), ((yl * C + c) * Z + z, 0), (1, 64)).reshape(64)
-    damp = jnp.concatenate([omega, zeta], axis=0)
-
-    spread = call(spread_kernel, [(YL * Z, PH, HALF)], [VMEM], wake[0])
+    powers = call(powers_kernel, [(MODES, NB)], [VMEM] * 2, omega, zeta, dtype=F32)
+
+    spread = call(
+        spread_kernel,
+        [(YL * Z, PH, HALF)],
+        [HBM],
+        wake[0],
+        out_specs=[HBM],
+        scratch=[pltpu.SemaphoreType.DMA((YL * Z,))],
+    )
     blocks = lax.all_to_all(spread, ("yl", "z"), 0, 0, tiled=True)
 
     near, far = call(
@@ -238,7 +264,7 @@
     parts = lax.all_to_all(picked, PLANE, 0, 0, tiled=True)
     forcing = call(gather_sum_kernel, [(Z, 4 * TS, NB)], [VMEM], parts)
     forcing = lax.all_to_all(forcing, "z", 0, 0, tiled=True)
-    harmonic = call(forward_kernel, [(PEERS, TS, NB)], [SMEM, VMEM], forward, forcing)
+    harmonic = call(forward_kernel, [(PEERS, TS, NB)], [VMEM, VMEM], forward, forcing)
     harmonic = lax.all_to_all(harmonic, PLANE, 0, 0, tiled=True)
     physical = call(
         modal_kernel,
@@ -248,7 +274,7 @@
         harmonic,
         shapes[0],
         flex[0],
-        damp,
+        powers,
         scratch=[pltpu.VMEM((NT, NB), F32)],
     )
     physical = lax.all_to_all(physical, "z", 0, 0, tiled=True)
@@ -261,7 +287,7 @@
         [VMEM, VMEM],
         sectoral,
         stress_map[0],
-        out_specs=[pl.BlockSpec(memory_space=pl.ANY)],
+        out_specs=[HBM],
         scratch=[pltpu.VMEM((rows, NT), BF), pltpu.SemaphoreType.DMA((CHUNKS,))],
     )
     return stress[None]

time: 135 us -> 134 us (level)
    pallas_call x8 -> x9, Pallas kernels: 8.97 us -> 9 us  [call(): pl.pallas_call(kernel, out_shape=outs, in_specs=specs, out_specs=out_spec...]
  transfers between devices with their start and end apart: 7 -> 7, of which waited for: 6 -> 6; matrix products, arithmetic and copies ran while one was open for 1% -> 1% of each run, Pallas kernels for 0% -> 1%
where the time goes in v4:
time: 134 us
  waiting for transfers between devices  47.9 us (36%)
  starting transfers between devices  40.4 us (30%)
  blocking collectives  33.1 us (25%)
  Pallas kernels  9 us (7%)
  local copies, waits for them, and re-layouts  3.06 us (2%)
    all_to_all x1, blocking collectives, local(): parts = lax.all_to_all(picked, PLANE, 0, 0, tiled=True)  17.4 us
    all_to_all x1, starting transfers between devices, local(): blocks = lax.all_to_all(spread, ('yl', 'z'), 0, 0, tiled=True)  17.2 us
    all_to_all x1, blocking collectives, local(): sectoral = lax.all_to_all(sectoral, PLANE, 0, 0, tiled=True)  15.7 us
    all_to_all x1, waiting for transfers between devices, local(): forcing = lax.all_to_all(forcing, 'z', 0, 0, tiled=True)  11.7 us
    all_to_all x1, waiting for transfers between devices, local(): physical = lax.all_to_all(physical, 'z', 0, 0, tiled=True)  11.4 us
    ppermute x1, waiting for transfers between devices, local(): by_both = lax.ppermute(far, ('yl', 'c'), [(0, 3), (1, 2), (2, 1), (3, 0)])  9.5 us
    pallas_call x9, Pallas kernels, call(): pl.pallas_call(kernel, out_shape=outs, in_specs=specs, out_specs=out_spec...  9 us
    all_to_all x1, waiting for transfers between devices, local(): blocks = lax.all_to_all(spread, ('yl', 'z'), 0, 0, tiled=True)  7.58 us
  transfers between devices with their start and end apart: 7, of which 6 were waited for; matrix products, arithmetic and copies ran while one was open for 1% of the time, Pallas kernels for 1%

profile of v4, /device:TPU:1, one launch (start us, length us, event | category | flops | bytes accessed | tf_op | source)
XLA Modules:
  0.0 133.7 jit_solution(10517785192951325235)
XLA Ops:
  0.0 0.0 copy-start.3
  0.0 0.7 copy-done.3
  0.7 1.0 shard_map.109
  1.8 0.0 copy-start.1
  1.8 17.2 %all-to-all-start = ((bf16[32,8,896]{2,1,0:T(8,128)(2,1)}), bf16[32,8,896]{2,1,0:T(8,128)(2,1)S(1)}, u32[]{:S(2)}, u32[]{:S(2)}) async-start(bf16[32,8,896]{2,1,0:T(8,128)(2,1)} %shard_map.109), calls=%async_computation | async-start | bytes 917504 | tf_op jit(solution)/shard_map/all_to_all | solution.py:237
  19.0 0.0 copy-start.6
  19.0 0.1 pad_add_fusion.pos
  19.1 0.0 copy-start.5
  19.1 0.0 copy-done.1
  19.1 0.6 copy-done.6
  19.7 0.1 copy-done.5
  19.8 0.6 shard_map.110
  20.3 3.1 %collective-permute-start = (bf16[144,896]{1,0:T(8,128)(2,1)S(1)}, bf16[144,896]{1,0:T(8,128)(2,1)S(1)}, u32[]{:S(2)}, u32[]{:S(2)}) collective-permute-start(bf16[144,896]{1,0:T(8,128)(2,1)S(1)} %get-tuple-element.8), channel_id=1, source_target_pairs={{0,256},{256,0},{1,257},{257,1},{2,258},{258,2},{3,259},{259,3},{4... | collective-permute-start | bytes 774152 | tf_op jit(solution)/shard_map/ppermute | solution.py:249
  23.5 3.4 %collective-permute-start.1 = (bf16[144,896]{1,0:T(8,128)(2,1)S(1)}, bf16[144,896]{1,0:T(8,128)(2,1)S(1)}, u32[]{:S(2)}, u32[]{:S(2)}) collective-permute-start(bf16[144,896]{1,0:T(8,128)(2,1)S(1)} %get-tuple-element.7.refs_0_), channel_id=1, source_target_pairs={{0,8},{8,0},{1,9},{9,1},{2,10},{10,2},{3,11},{11,3},{4,12},{12,4},... | collective-permute-start | bytes 774152 | tf_op jit(solution)/shard_map/ppermute | solution.py:250
  26.9 1.9 %collective-permute-start.2 = (bf16[144,896]{1,0:T(8,128)(2,1)S(1)}, bf16[144,896]{1,0:T(8,128)(2,1)S(1)}, u32[]{:S(2)}, u32[]{:S(2)}) collective-permute-start(bf16[144,896]{1,0:T(8,128)(2,1)S(1)} %get-tuple-element.8), channel_id=1, source_target_pairs={{0,264},{8,256},{256,8},{264,0},{1,265},{9,257},{257,9},{265,1},{2... | collective-permute-start | bytes 774152 | tf_op jit(solution)/shard_map/ppermute | solution.py:251
  28.9 0.9 collective-permute-done.refs_1_
  29.8 0.0 collective-permute-done.1.refs_2_
  29.8 9.5 %collective-permute-done.2.refs_3_ = bf16[144,896]{1,0:T(8,128)(2,1)S(1)} collective-permute-done((bf16[144,896]{1,0:T(8,128)(2,1)S(1)}, bf16[144,896]{1,0:T(8,128)(2,1)S(1)}, u32[]{:S(2)}, u32[]{:S(2)}) %collective-permute-start.2) | collective-permute-done | bytes 258080 | tf_op jit(solution)/shard_map/ppermute | solution.py:251
  39.3 7.6 %all-to-all-done.wake_ref = bf16[32,8,896]{2,1,0:T(8,128)(2,1)S(1)} async-done(((bf16[32,8,896]{2,1,0:T(8,128)(2,1)}), bf16[32,8,896]{2,1,0:T(8,128)(2,1)S(1)}, u32[]{:S(2)}, u32[]{:S(2)}) %all-to-all-start) | async-done | bytes 458784 | tf_op jit(solution)/shard_map/all_to_all | solution.py:237
  46.9 1.3 shard_map.111
  48.2 17.4 %all_to_all.30.in_ref = bf16[32,32,128]{2,1,0:T(8,128)(2,1)S(1)} all-to-all(bf16[32,32,128]{2,1,0:T(8,128)(2,1)S(1)} %shard_map.111), channel_id=1, replica_groups=mesh['yl'=2,'z'=16,'c'=2,'x'=4,'yh'=2] {'yl','c','x','yh'}, dimensions={0} | all-to-all | bytes 524288 | tf_op jit(solution)/shard_map/all_to_all | solution.py:264
  65.6 0.7 shard_map.112
  66.3 4.4 %all-to-all-start.2 = ((bf16[16,32,128]{2,1,0:T(8,128)(2,1)}), bf16[16,32,128]{2,1,0:T(8,128)(2,1)S(1)}, u32[]{:S(2)}, u32[]{:S(2)}) async-start(bf16[16,32,128]{2,1,0:T(8,128)(2,1)} %shard_map.112), calls=%async_computation.2 | async-start | bytes 262144 | tf_op jit(solution)/shard_map/all_to_all | solution.py:266
  70.7 0.9 dynamic-slice_bitcast_fusion.table_ref
  71.6 11.7 %all-to-all-done.2.in_ref = bf16[16,32,128]{2,1,0:T(8,128)(2,1)S(1)} async-done(((bf16[16,32,128]{2,1,0:T(8,128)(2,1)}), bf16[16,32,128]{2,1,0:T(8,128)(2,1)S(1)}, u32[]{:S(2)}, u32[]{:S(2)}) %all-to-all-start.2) | async-done | bytes 131104 | tf_op jit(solution)/shard_map/all_to_all | solution.py:266
  83.3 0.8 shard_map.113
  84.1 0.0 copy-start.7
  84.1 0.0 copy-start.8
  84.1 0.0 copy-start.2
  84.1 6.2 %all-to-all-start.3 = ((bf16[32,8,128]{2,1,0:T(8,128)(2,1)}), bf16[32,8,128]{2,1,0:T(8,128)(2,1)S(1)}, u32[]{:S(2)}, u32[]{:S(2)}) async-start(bf16[32,8,128]{2,1,0:T(8,128)(2,1)} %shard_map.113), calls=%async_computation.3 | async-start | bytes 131072 | tf_op jit(solution)/shard_map/all_to_all | solution.py:268
  90.3 0.0 copy-done.7
  90.3 0.0 copy-done.8
  90.3 0.0 copy-start.4
  90.3 0.4 shard_map.114.powers_ref
  90.7 6.9 %all-to-all-done.3.in_ref = bf16[32,8,128]{2,1,0:T(8,128)(2,1)S(1)} async-done(((bf16[32,8,128]{2,1,0:T(8,128)(2,1)}), bf16[32,8,128]{2,1,0:T(8,128)(2,1)S(1)}, u32[]{:S(2)}, u32[]{:S(2)}) %all-to-all-start.3) | async-done | bytes 65568 | tf_op jit(solution)/shard_map/all_to_all | solution.py:268
  97.6 0.0 copy-done.2
  97.6 0.0 copy-done.4
  97.6 2.3 %shard_map.115 = bf16[16,32,128]{2,1,0:T(8,128)(2,1)} custom-call(s32[3]{0:T(128)S(1)} %pad_add_fusion.pos, bf16[32,8,128]{2,1,0:T(8,128)(2,1)S(1)} %all-to-all-done.3.in_ref, bf16[40,128]{1,0:T(8,128)(2,1)S(1)} %bitcast.17, bf16[128,128]{1,0:T(8,128)(2,1)S(1)} %bitcast.15, f32[40,128]{1,0:T(8,128)S(1)} %shard_map.114.powers_ref), custom_call_target="tpu_custom_call" | custom-call | tf_op jit(solution)/shard_map/pallas_call | solution.py:210
  99.9 4.1 %all-to-all-start.4 = ((bf16[16,32,128]{2,1,0:T(8,128)(2,1)}), bf16[16,32,128]{2,1,0:T(8,128)(2,1)S(1)}, u32[]{:S(2)}, u32[]{:S(2)}) async-start(bf16[16,32,128]{2,1,0:T(8,128)(2,1)} %shard_map.115), calls=%async_computation.4 | async-start | bytes 262144 | tf_op jit(solution)/shard_map/all_to_all | solution.py:280
  104.0 0.0 copy-start
  104.0 0.8 dynamic-slice_bitcast_fusion.1.table_ref
  104.8 11.4 %all-to-all-done.4.in_ref = bf16[16,32,128]{2,1,0:T(8,128)(2,1)S(1)} async-done(((bf16[16,32,128]{2,1,0:T(8,128)(2,1)}), bf16[16,32,128]{2,1,0:T(8,128)(2,1)S(1)}, u32[]{:S(2)}, u32[]{:S(2)}) %all-to-all-start.4) | async-done | bytes 131104 | tf_op jit(solution)/shard_map/all_to_all | solution.py:280
  116.1 0.6 shard_map.116
  116.8 15.7 %all_to_all.31.in_ref = bf16[32,32,128]{2,1,0:T(8,128)(2,1)S(1)} all-to-all(bf16[32,32,128]{2,1,0:T(8,128)(2,1)S(1)} %shard_map.116), channel_id=1, replica_groups=mesh['yl'=2,'z'=16,'c'=2,'x'=4,'yh'=2] {'yl','c','x','yh'}, dimensions={0} | all-to-all | bytes 524288 | tf_op jit(solution)/shard_map/all_to_all | solution.py:282
  132.4 0.0 copy-done
  132.4 1.3 shard_map.117
Async XLA Ops:
  0.0 0.7 copy-start.3
  1.8 17.3 %copy-start.1 = (bf16[1,128,1792]{2,1,0:T(8,128)(2,1)S(1)}, bf16[1,128,1792]{2,1,0:T(8,128)(2,1)}, u32[]{:S(2)}) copy-start(bf16[1,128,1792]{2,1,0:T(8,128)(2,1)} %param.12) | copy-start | bytes 1376260
  1.8 45.1 %all-to-all-start = ((bf16[32,8,896]{2,1,0:T(8,128)(2,1)}), bf16[32,8,896]{2,1,0:T(8,128)(2,1)S(1)}, u32[]{:S(2)}, u32[]{:S(2)}) async-start(bf16[32,8,896]{2,1,0:T(8,128)(2,1)} %shard_map.109), calls=%async_computation | async-start | bytes 917504 | tf_op jit(solution)/shard_map/all_to_all | solution.py:237
  19.0 0.7 copy-start.6
  19.1 0.7 copy-start.5
  20.3 9.5 %collective-permute-start = (bf16[144,896]{1,0:T(8,128)(2,1)S(1)}, bf16[144,896]{1,0:T(8,128)(2,1)S(1)}, u32[]{:S(2)}, u32[]{:S(2)}) collective-permute-start(bf16[144,896]{1,0:T(8,128)(2,1)S(1)} %get-tuple-element.8), channel_id=1, source_target_pairs={{0,256},{256,0},{1,257},{257,1},{2,258},{258,2},{3,259},{259,3},{4... | collective-permute-start | bytes 774152 | tf_op jit(solution)/shard_map/ppermute | solution.py:249
  23.5 6.3 %collective-permute-start.1 = (bf16[144,896]{1,0:T(8,128)(2,1)S(1)}, bf16[144,896]{1,0:T(8,128)(2,1)S(1)}, u32[]{:S(2)}, u32[]{:S(2)}) collective-permute-start(bf16[144,896]{1,0:T(8,128)(2,1)S(1)} %get-tuple-element.7.refs_0_), channel_id=1, source_target_pairs={{0,8},{8,0},{1,9},{9,1},{2,10},{10,2},{3,11},{11,3},{4,12},{12,4},... | collective-permute-start | bytes 774152 | tf_op jit(solution)/shard_map/ppermute | solution.py:250
  26.9 12.4 %collective-permute-start.2 = (bf16[144,896]{1,0:T(8,128)(2,1)S(1)}, bf16[144,896]{1,0:T(8,128)(2,1)S(1)}, u32[]{:S(2)}, u32[]{:S(2)}) collective-permute-start(bf16[144,896]{1,0:T(8,128)(2,1)S(1)} %get-tuple-element.8), channel_id=1, source_target_pairs={{0,264},{8,256},{256,8},{264,0},{1,265},{9,257},{257,9},{265,1},{2... | collective-permute-start | bytes 774152 | tf_op jit(solution)/shard_map/ppermute | solution.py:251
  66.3 16.9 %all-to-all-start.2 = ((bf16[16,32,128]{2,1,0:T(8,128)(2,1)}), bf16[16,32,128]{2,1,0:T(8,128)(2,1)S(1)}, u32[]{:S(2)}, u32[]{:S(2)}) async-start(bf16[16,32,128]{2,1,0:T(8,128)(2,1)} %shard_map.112), calls=%async_computation.2 | async-start | bytes 262144 | tf_op jit(solution)/shard_map/all_to_all | solution.py:266
  84.1 6.3 %copy-start.7 = (f32[1,40]{1,0:T(1,128)S(1)}, f32[1,40]{1,0:T(1,128)}, u32[]{:S(2)}) copy-start(f32[1,40]{1,0:T(1,128)} %omega_ref.1) | copy-start | bytes 484
  84.1 6.3 %copy-start.8 = (f32[1,40]{1,0:T(1,128)S(1)}, f32[1,40]{1,0:T(1,128)}, u32[]{:S(2)}) copy-start(f32[1,40]{1,0:T(1,128)} %zeta_ref.1) | copy-start | bytes 484
  84.1 13.5 %copy-start.2 = (bf16[1,128,128]{2,1,0:T(8,128)(2,1)S(1)}, bf16[1,128,128]{2,1,0:T(8,128)(2,1)}, u32[]{:S(2)}) copy-start(bf16[1,128,128]{2,1,0:T(8,128)(2,1)} %param.16) | copy-start | bytes 98308
  84.1 13.5 %all-to-all-start.3 = ((bf16[32,8,128]{2,1,0:T(8,128)(2,1)}), bf16[32,8,128]{2,1,0:T(8,128)(2,1)S(1)}, u32[]{:S(2)}, u32[]{:S(2)}) async-start(bf16[32,8,128]{2,1,0:T(8,128)(2,1)} %shard_map.113), calls=%async_computation.3 | async-start | bytes 131072 | tf_op jit(solution)/shard_map/all_to_all | solution.py:268
  90.3 7.2 %copy-start.4 = (bf16[1,40,128]{2,1,0:T(8,128)(2,1)S(1)}, bf16[1,40,128]{2,1,0:T(8,128)(2,1)}, u32[]{:S(2)}) copy-start(bf16[1,40,128]{2,1,0:T(8,128)(2,1)} %param.15) | copy-start | bytes 30724
  99.9 16.2 %all-to-all-start.4 = ((bf16[16,32,128]{2,1,0:T(8,128)(2,1)}), bf16[16,32,128]{2,1,0:T(8,128)(2,1)S(1)}, u32[]{:S(2)}, u32[]{:S(2)}) async-start(bf16[16,32,128]{2,1,0:T(8,128)(2,1)} %shard_map.115), calls=%async_computation.4 | async-start | bytes 262144 | tf_op jit(solution)/shard_map/all_to_all | solution.py:280
  104.0 28.5 %copy-start = (bf16[1,2048,128]{2,1,0:T(8,128)(2,1)S(1)}, bf16[1,2048,128]{2,1,0:T(8,128)(2,1)}, u32[]{:S(2)}) copy-start(bf16[1,2048,128]{2,1,0:T(8,128)(2,1)} %param.19) | copy-start | bytes 1572868

commit v5 on v4

--- a/solution.py
+++ b/solution.py
@@ -141,11 +141,11 @@
     out_ref[...] = powers
 
 
-def modal_kernel(pos, in_ref, shapes_ref, flex_ref, powers_ref, out_ref, hold_ref):
-    force = in_ref[...].reshape(NT, NB)
+def modal_kernel(pos, in_ref, shapes_ref, flex_ref, powers_ref, out_ref):
     shapes = shapes_ref[...]
-    hold_ref[...] = dot_nt(force, flex_ref[...])
-    real = dot_nt(shapes, force)
+    real = dot_nt(shapes, in_ref[...].reshape(NT, NB))
+    rows = in_ref[pl.ds(pos[2] * (TD // TS), TD // TS)].reshape(TD, NB)
+    direct = dot_nt(rows, flex_ref[...])
     imag = None
     powers = powers_ref[...]
     lane = lax.broadcasted_iota(jnp.int32, (MODES, NT), 1)
@@ -158,15 +158,13 @@
         else:
             si = jnp.where(keep, pltpu.roll(imag, 2**k, 1), 0.0)
             real, imag = real + (pr * sr - pi * si), imag + (pr * si + pi * sr)
-    hold_ref[...] += lax.dot_general(
-        imag,
-        shapes.astype(F32),
-        (((0,), (0,)), ((), ())),
-        precision=HI,
-        preferred_element_type=F32,
-    )
-    block = hold_ref[pl.ds(pl.multiple_of(pos[2] * TD, TD), TD), :].astype(BF)
-    out_ref[...] = jnp.broadcast_to(block[None], out_ref.shape)
+    own = pltpu.roll(imag, lax.rem(NT - pos[2] * TD, NT), 1)[:, 0:128]
+    high = own.astype(BF).astype(F32)
+    amplitude = jnp.concatenate([high, own - high], axis=0).T[0:TD].astype(BF)
+    modal = jnp.dot(
+        amplitude, jnp.concatenate([shapes, shapes], axis=0), preferred_element_type=F32
+    )
+    out_ref[...] = jnp.broadcast_to((modal + direct).astype(BF)[None], out_ref.shape)
 
 
 def inverse_kernel(table_ref, in_ref, out_ref):
@@ -229,7 +227,7 @@
     spread = call(
         spread_kernel,
         [(YL * Z, PH, HALF)],
-        [HBM],
+        [pl.BlockSpec(memory_space=pltpu.HBM)],
         wake[0],
         out_specs=[HBM],
         scratch=[pltpu.SemaphoreType.DMA((YL * Z,))],
@@ -248,7 +246,8 @@
     swap = [(0, 1), (1, 0)]
     by_yl = lax.ppermute(far, "yl", swap)
     by_c = lax.ppermute(near, "c", swap)
-    by_both = lax.ppermute(far, ("yl", "c"), [(0, 3), (1, 2), (2, 1), (3, 0)])
+    by_both = lax.ppermute(by_yl, "c", swap)
+    near, forward, inverse, powers = lax.optimization_barrier((near, forward, inverse, powers))
 
     picked = call(
         project_kernel,
@@ -275,7 +274,6 @@
         shapes[0],
         flex[0],
         powers,
-        scratch=[pltpu.VMEM((NT, NB), F32)],
     )
     physical = lax.all_to_all(physical, "z", 0, 0, tiled=True)
     sectoral = call(inverse_kernel, [(PEERS, TD, NB)], [SMEM, VMEM], inverse, physical)

time: 134 us -> 131 us (0.978)
  blocking collectives: 33.1 us -> 78.7 us
  waiting for transfers between devices: 47.9 us -> 12.7 us
  starting transfers between devices: 40.4 us -> 28.4 us
  Pallas kernels: 9 us -> 6.91 us
    all_to_all x0 -> x3, blocking collectives: none -> 45.6 us  [the longest x1 16.7 us: local(): forcing = lax.all_to_all(forcing, 'z', 0, 0, tiled=True)]
    all_to_all x3 -> x0, waiting for transfers between devices: 29.9 us -> none  [the longest x1 11.7 us: local(): forcing = lax.all_to_all(forcing, 'z', 0, 0, tiled=True)]
    all_to_all x3 -> x0, starting transfers between devices: 14.7 us -> none  [the longest x1 6.24 us: local(): harmonic = lax.all_to_all(harmonic, PLANE, 0, 0, tiled=True)]
    ppermute x1, waiting for transfers between devices: 9.5 us -> 0.01 us  [local(): by_both = lax.ppermute(by_yl, 'c', swap)]
    ppermute x1, starting transfers between devices: 1.92 us -> 4.67 us  [local(): by_both = lax.ppermute(by_yl, 'c', swap)]
    all_to_all x1, waiting for transfers between devices: 7.58 us -> 9.79 us  [local(): blocks = lax.all_to_all(spread, ('yl', 'z'), 0, 0, tiled=True)]
    pallas_call x9, Pallas kernels: 9 us -> 6.91 us  [call(): pl.pallas_call(kernel, out_shape=outs, in_specs=specs, out_specs=out_spec...]
    ppermute x1, waiting for transfers between devices: 0.94 us -> 2.87 us  [local(): by_yl = lax.ppermute(far, 'yl', swap)]
  transfers between devices with their start and end apart: 7 -> 4, of which waited for: 6 -> 2; matrix products, arithmetic and copies ran while one was open for 1% -> 1% of each run, Pallas kernels for 1% -> 1%
where the time goes in v5:
time: 131 us
  blocking collectives  78.7 us (60%)
  starting transfers between devices  28.4 us (22%)
  waiting for transfers between devices  12.7 us (10%)
  Pallas kernels  6.91 us (5%)
  local copies, waits for them, and re-layouts  3.65 us (3%)
    all_to_all x1, blocking collectives, local(): parts = lax.all_to_all(picked, PLANE, 0, 0, tiled=True)  17.4 us
    all_to_all x1, starting transfers between devices, local(): blocks = lax.all_to_all(spread, ('yl', 'z'), 0, 0, tiled=True)  17.2 us
    all_to_all x1, blocking collectives, local(): forcing = lax.all_to_all(forcing, 'z', 0, 0, tiled=True)  16.7 us
    all_to_all x1, blocking collectives, local(): physical = lax.all_to_all(physical, 'z', 0, 0, tiled=True)  15.8 us
    all_to_all x1, blocking collectives, local(): sectoral = lax.all_to_all(sectoral, PLANE, 0, 0, tiled=True)  15.6 us
    all_to_all x1, blocking collectives, local(): harmonic = lax.all_to_all(harmonic, PLANE, 0, 0, tiled=True)  13.2 us
    all_to_all x1, waiting for transfers between devices, local(): blocks = lax.all_to_all(spread, ('yl', 'z'), 0, 0, tiled=True)  9.79 us
    pallas_call x9, Pallas kernels, call(): pl.pallas_call(kernel, out_shape=outs, in_specs=specs, out_specs=out_spec...  6.91 us
  transfers between devices with their start and end apart: 4, of which 2 were waited for; matrix products, arithmetic and copies ran while one was open for 1% of the time, Pallas kernels for 1%

profile of v5, /device:TPU:1, one launch (start us, length us, event | category | flops | bytes accessed | tf_op | source)
XLA Modules:
  0.0 130.6 jit_solution(18080887752213931039)
XLA Ops:
  0.0 0.0 copy-start.3
  0.0 0.7 copy-done.3
  0.7 1.0 shard_map.111
  1.8 0.0 copy-start.1
  1.8 17.2 %all-to-all-start = ((bf16[32,8,896]{2,1,0:T(8,128)(2,1)}), bf16[32,8,896]{2,1,0:T(8,128)(2,1)S(1)}, u32[]{:S(2)}, u32[]{:S(2)}) async-start(bf16[32,8,896]{2,1,0:T(8,128)(2,1)} %shard_map.111), calls=%async_computation | async-start | bytes 917504 | tf_op jit(solution)/shard_map/all_to_all | solution.py:235
  19.0 0.0 copy-start.6
  19.0 0.1 pad_add_fusion.pos
  19.1 0.0 copy-start.5
  19.1 0.0 copy-done.1
  19.1 0.6 copy-done.6
  19.7 0.1 copy-done.5
  19.8 0.6 shard_map.109
  20.3 3.1 %collective-permute-start = (bf16[144,896]{1,0:T(8,128)(2,1)S(1)}, bf16[144,896]{1,0:T(8,128)(2,1)S(1)}, u32[]{:S(2)}, u32[]{:S(2)}) collective-permute-start(bf16[144,896]{1,0:T(8,128)(2,1)S(1)} %get-tuple-element.15), channel_id=1, source_target_pairs={{0,256},{256,0},{1,257},{257,1},{2,258},{258,2},{3,259},{259,3},{4... | collective-permute-start | bytes 774152 | tf_op jit(solution)/shard_map/ppermute | solution.py:247
  23.5 3.4 %collective-permute-start.1 = (bf16[144,896]{1,0:T(8,128)(2,1)S(1)}, bf16[144,896]{1,0:T(8,128)(2,1)S(1)}, u32[]{:S(2)}, u32[]{:S(2)}) collective-permute-start(bf16[144,896]{1,0:T(8,128)(2,1)S(1)} %get-tuple-element.14.refs_0_), channel_id=1, source_target_pairs={{0,8},{8,0},{1,9},{9,1},{2,10},{10,2},{3,11},{11,3},{4,12},{12,4},... | collective-permute-start | bytes 774152 | tf_op jit(solution)/shard_map/ppermute | solution.py:248
  26.9 2.9 %collective-permute-done.refs_1_ = bf16[144,896]{1,0:T(8,128)(2,1)S(1)} collective-permute-done((bf16[144,896]{1,0:T(8,128)(2,1)S(1)}, bf16[144,896]{1,0:T(8,128)(2,1)S(1)}, u32[]{:S(2)}, u32[]{:S(2)}) %collective-permute-start) | collective-permute-done | bytes 258080 | tf_op jit(solution)/shard_map/ppermute | solution.py:247
  29.8 4.7 %collective-permute-start.2 = (bf16[144,896]{1,0:T(8,128)(2,1)S(1)}, bf16[144,896]{1,0:T(8,128)(2,1)S(1)}, u32[]{:S(2)}, u32[]{:S(2)}) collective-permute-start(bf16[144,896]{1,0:T(8,128)(2,1)S(1)} %collective-permute-done.refs_1_), channel_id=1, source_target_pairs={{0,8},{8,0},{1,9},{9,1},{2,10},{10,2},{3,11},{11,3},{4,12},{12,4},... | collective-permute-start | bytes 774152 | tf_op jit(solution)/shard_map/ppermute | solution.py:249
  34.5 0.0 copy-start.7
  34.5 0.0 copy-start.8
  34.5 0.6 copy-done.7
  35.1 0.0 copy-done.8
  35.2 0.4 shard_map.110.powers_ref
  35.5 0.7 dynamic-slice_bitcast_fusion.1.table_ref
  36.2 0.8 dynamic-slice_bitcast_fusion.table_ref
  37.1 0.0 collective-permute-done.1.refs_2_
  37.1 0.0 collective-permute-done.2.refs_3_
  37.1 9.8 %all-to-all-done.wake_ref = bf16[32,8,896]{2,1,0:T(8,128)(2,1)S(1)} async-done(((bf16[32,8,896]{2,1,0:T(8,128)(2,1)}), bf16[32,8,896]{2,1,0:T(8,128)(2,1)S(1)}, u32[]{:S(2)}, u32[]{:S(2)}) %all-to-all-start) | async-done | bytes 458784 | tf_op jit(solution)/shard_map/all_to_all | solution.py:235
  46.9 1.3 %shard_map.112 = bf16[32,32,128]{2,1,0:T(8,128)(2,1)S(1)} custom-call(s32[3]{0:T(128)S(1)} %pad_add_fusion.pos, bf16[32,8,896]{2,1,0:T(8,128)(2,1)S(1)} %all-to-all-done.wake_ref, bf16[144,896]{1,0:T(8,128)(2,1)S(1)} %get-tuple-element.14.refs_0_, bf16[144,896]{1,0:T(8,128)(2,1)S(1)} %collective-permute-done.refs_1_, ...), custom_call_target="tpu_custom_call" | custom-call | tf_op jit(solution)/shard_map/pallas_call | solution.py:208
  48.2 17.4 %all_to_all.30.in_ref = bf16[32,32,128]{2,1,0:T(8,128)(2,1)S(1)} all-to-all(bf16[32,32,128]{2,1,0:T(8,128)(2,1)S(1)} %shard_map.112), channel_id=1, replica_groups=mesh['yl'=2,'z'=16,'c'=2,'x'=4,'yh'=2] {'yl','c','x','yh'}, dimensions={0} | all-to-all | bytes 524288 | tf_op jit(solution)/shard_map/all_to_all | solution.py:263
  65.7 16.7 %all_to_all.31.in_ref = bf16[16,32,128]{2,1,0:T(8,128)(2,1)S(1)} all-to-all(bf16[16,32,128]{2,1,0:T(8,128)(2,1)S(1)} %shard_map.113), channel_id=1, replica_groups=mesh['yl'=2,'z'=16,'c'=2,'x'=4,'yh'=2] {'z'}, dimensions={0} | all-to-all | bytes 262144 | tf_op jit(solution)/shard_map/all_to_all | solution.py:265
  82.4 0.2 shard_map.114
  82.6 0.0 copy-start.2
  82.6 0.0 copy-start.4
  82.6 13.2 %all_to_all.32.in_ref = bf16[32,8,128]{2,1,0:T(8,128)(2,1)S(1)} all-to-all(bf16[32,8,128]{2,1,0:T(8,128)(2,1)S(1)} %shard_map.114), channel_id=1, replica_groups=mesh['yl'=2,'z'=16,'c'=2,'x'=4,'yh'=2] {'yl','c','x','yh'}, dimensions={0} | all-to-all | bytes 131072 | tf_op jit(solution)/shard_map/all_to_all | solution.py:267
  95.8 0.0 copy-done.2
  95.8 0.0 copy-done.4
  95.8 1.5 %shard_map.115 = bf16[16,32,128]{2,1,0:T(8,128)(2,1)S(1)} custom-call(s32[3]{0:T(128)S(1)} %pad_add_fusion.pos, bf16[32,8,128]{2,1,0:T(8,128)(2,1)S(1)} %all_to_all.32.in_ref, bf16[40,128]{1,0:T(8,128)(2,1)S(1)} %bitcast.17, bf16[128,128]{1,0:T(8,128)(2,1)S(1)} %bitcast.15, f32[40,128]{1,0:T(8,128)S(1)} %shard_map.110.powers_ref), custom_call_target="tpu_custom_call" | custom-call | tf_op jit(solution)/shard_map/pallas_call | solution.py:208
  97.3 15.8 %all_to_all.33.in_ref = bf16[16,32,128]{2,1,0:T(8,128)(2,1)S(1)} all-to-all(bf16[16,32,128]{2,1,0:T(8,128)(2,1)S(1)} %shard_map.115), channel_id=1, replica_groups=mesh['yl'=2,'z'=16,'c'=2,'x'=4,'yh'=2] {'z'}, dimensions={0} | all-to-all | bytes 262144 | tf_op jit(solution)/shard_map/all_to_all | solution.py:278
  113.0 0.0 copy-start
  113.0 0.6 shard_map.116
  113.7 15.6 %all_to_all.34.in_ref = bf16[32,32,128]{2,1,0:T(8,128)(2,1)S(1)} all-to-all(bf16[32,32,128]{2,1,0:T(8,128)(2,1)S(1)} %shard_map.116), channel_id=1, replica_groups=mesh['yl'=2,'z'=16,'c'=2,'x'=4,'yh'=2] {'yl','c','x','yh'}, dimensions={0} | all-to-all | bytes 524288 | tf_op jit(solution)/shard_map/all_to_all | solution.py:280
  129.3 0.0 copy-done
  129.3 1.3 shard_map.117
  (1 shorter events, 0.0 us)
Async XLA Ops:
  0.0 0.7 copy-start.3
  1.8 17.3 %copy-start.1 = (bf16[1,128,1792]{2,1,0:T(8,128)(2,1)S(1)}, bf16[1,128,1792]{2,1,0:T(8,128)(2,1)}, u32[]{:S(2)}) copy-start(bf16[1,128,1792]{2,1,0:T(8,128)(2,1)} %param.12) | copy-start | bytes 1376260
  1.8 45.1 %all-to-all-start = ((bf16[32,8,896]{2,1,0:T(8,128)(2,1)}), bf16[32,8,896]{2,1,0:T(8,128)(2,1)S(1)}, u32[]{:S(2)}, u32[]{:S(2)}) async-start(bf16[32,8,896]{2,1,0:T(8,128)(2,1)} %shard_map.111), calls=%async_computation | async-start | bytes 917504 | tf_op jit(solution)/shard_map/all_to_all | solution.py:235
  19.0 0.7 copy-start.6
  19.1 0.7 copy-start.5
  20.3 9.5 %collective-permute-start = (bf16[144,896]{1,0:T(8,128)(2,1)S(1)}, bf16[144,896]{1,0:T(8,128)(2,1)S(1)}, u32[]{:S(2)}, u32[]{:S(2)}) collective-permute-start(bf16[144,896]{1,0:T(8,128)(2,1)S(1)} %get-tuple-element.15), channel_id=1, source_target_pairs={{0,256},{256,0},{1,257},{257,1},{2,258},{258,2},{3,259},{259,3},{4... | collective-permute-start | bytes 774152 | tf_op jit(solution)/shard_map/ppermute | solution.py:247
  23.5 13.6 %collective-permute-start.1 = (bf16[144,896]{1,0:T(8,128)(2,1)S(1)}, bf16[144,896]{1,0:T(8,128)(2,1)S(1)}, u32[]{:S(2)}, u32[]{:S(2)}) collective-permute-start(bf16[144,896]{1,0:T(8,128)(2,1)S(1)} %get-tuple-element.14.refs_0_), channel_id=1, source_target_pairs={{0,8},{8,0},{1,9},{9,1},{2,10},{10,2},{3,11},{11,3},{4,12},{12,4},... | collective-permute-start | bytes 774152 | tf_op jit(solution)/shard_map/ppermute | solution.py:248
  29.8 7.3 %collective-permute-start.2 = (bf16[144,896]{1,0:T(8,128)(2,1)S(1)}, bf16[144,896]{1,0:T(8,128)(2,1)S(1)}, u32[]{:S(2)}, u32[]{:S(2)}) collective-permute-start(bf16[144,896]{1,0:T(8,128)(2,1)S(1)} %collective-permute-done.refs_1_), channel_id=1, source_target_pairs={{0,8},{8,0},{1,9},{9,1},{2,10},{10,2},{3,11},{11,3},{4,12},{12,4},... | collective-permute-start | bytes 774152 | tf_op jit(solution)/shard_map/ppermute | solution.py:249
  34.5 0.7 copy-start.7
  34.5 0.7 copy-start.8
  82.6 13.2 %copy-start.2 = (bf16[1,128,128]{2,1,0:T(8,128)(2,1)S(1)}, bf16[1,128,128]{2,1,0:T(8,128)(2,1)}, u32[]{:S(2)}) copy-start(bf16[1,128,128]{2,1,0:T(8,128)(2,1)} %param.16) | copy-start | bytes 98308
  82.6 13.2 %copy-start.4 = (bf16[1,40,128]{2,1,0:T(8,128)(2,1)S(1)}, bf16[1,40,128]{2,1,0:T(8,128)(2,1)}, u32[]{:S(2)}) copy-start(bf16[1,40,128]{2,1,0:T(8,128)(2,1)} %param.15) | copy-start | bytes 30724
  113.0 16.2 %copy-start = (bf16[1,2048,128]{2,1,0:T(8,128)(2,1)S(1)}, bf16[1,2048,128]{2,1,0:T(8,128)(2,1)}, u32[]{:S(2)}) copy-start(bf16[1,2048,128]{2,1,0:T(8,128)(2,1)} %param.19) | copy-start | bytes 1572868

commit v6 on v5

--- a/solution.py
+++ b/solution.py
@@ -42,9 +42,17 @@
 
 
 FORWARD = forward_table()
-INVERSE = np.ascontiguousarray(
-    FOURIER.reshape(YL, Z, C, YL, Z, C).transpose(0, 2, 4, 1, 3, 5).reshape(YL * C * Z, 64)
-).astype(np.float32)
+
+
+def inverse_table():
+    table = FOURIER.reshape(YL, Z, C, YL, Z, C).transpose(0, 2, 4, 3, 5, 1)
+    table = np.einsum("dij,tu->ditju", table.reshape(BLADES, 4, Z), np.eye(TS))
+    table = table.reshape(BLADES, 4 * TS, Z * TS).astype(np.float32)
+    high = table.astype(BF)
+    return np.stack([high, (table - high.astype(np.float32)).astype(BF)], axis=1)
+
+
+INVERSE = inverse_table()
 
 
 def dot_nt(a, b, **kw):
@@ -76,22 +84,28 @@
         ref[NB : NB + 16] = index
 
 
-def project_kernel(pos, wake_ref, *refs):
-    out_ref = refs[-1]
-    basis = jnp.concatenate([ref[0:NB] for ref in refs[:4]], axis=0)
-    table = dot_nt(wake_ref[...].reshape(YL * Z * PH, HALF), basis).astype(BF)
-    pair = lax.broadcasted_iota(jnp.int32, (NT, YL * Z * PH), 1).astype(F32)
+def select_kernel(pos, *refs):
+    basis_ref, onehot_ref = refs[4:]
     codes = []
-    for ref in refs[:4]:
+    for r, ref in enumerate(refs[:4]):
+        basis_ref[r * NB : (r + 1) * NB] = ref[0:NB]
         index = ref[NB : NB + 16, 0:NT].astype(F32)
         block, phase = index[0:1].astype(jnp.int32), index[1:2].astype(jnp.int32)
         code = ((block >> 1) * PH + phase).astype(F32)
         codes.append(jnp.where((block & 1) == pos[1], code, -1.0))
     codes = jnp.concatenate(codes + [jnp.zeros((4, NT), F32)], axis=0).T
+    pair = lax.broadcasted_iota(jnp.int32, (NT, YL * Z * PH), 1).astype(F32)
+    for r in range(4):
+        onehot_ref[r] = jnp.where(codes[:, r : r + 1] == pair, 1.0, 0.0).astype(BF)
+
+
+def project_kernel(wake_ref, basis_ref, onehot_ref, out_ref):
+    table = dot_nt(wake_ref[...].reshape(YL * Z * PH, HALF), basis_ref[...]).astype(BF)
     picks = []
     for r in range(4):
-        onehot = jnp.where(codes[:, r : r + 1] == pair, 1.0, 0.0).astype(BF)
-        part = jnp.dot(onehot, table[:, r * NB : (r + 1) * NB], preferred_element_type=F32)
+        part = jnp.dot(
+            onehot_ref[r], table[:, r * NB : (r + 1) * NB], preferred_element_type=F32
+        )
         picks.append(part.reshape(PEERS, TS, NB))
     out_ref[...] = jnp.concatenate(picks, axis=1).astype(BF)
 
@@ -168,14 +182,16 @@
 
 
 def inverse_kernel(table_ref, in_ref, out_ref):
-    acc = [None] * 4
-    for z in range(Z):
-        block = in_ref[z].astype(F32)
-        for s in range(4):
-            term = block * table_ref[z * 4 + s]
-            acc[s] = term if acc[s] is None else acc[s] + term
+    block = in_ref[...].astype(F32)
+    parts = []
+    for g in range(TD // TS):
+        part = block[:, g * TS : (g + 1) * TS].reshape(Z * TS, NB).astype(BF)
+        parts.append(
+            sum(jnp.dot(table_ref[k], part, preferred_element_type=F32) for k in range(2))
+        )
     for s in range(4):
-        out_ref[s * D : (s + 1) * D] = jnp.broadcast_to(acc[s].astype(BF)[None], (D, TD, NB))
+        part = jnp.concatenate([p[s * TS : (s + 1) * TS] for p in parts], axis=0).astype(BF)
+        out_ref[s * D : (s + 1) * D] = jnp.broadcast_to(part[None], (D, TD, NB))
 
 
 CHUNKS = 4
@@ -203,7 +219,7 @@
 HBM = pl.BlockSpec(memory_space=pl.ANY)
 
 
-def call(kernel, outs, specs, *args, out_specs=None, scratch=(), dtype=BF):
+def call(kernel, outs, specs, *args, out_specs=None, scratch=(), dtype=BF, vmem=24):
     outs = [jax.ShapeDtypeStruct(shape, dtype) for shape in outs]
     got = pl.pallas_call(
         kernel,
@@ -211,7 +227,7 @@
         in_specs=specs,
         out_specs=out_specs or [VMEM] * len(outs),
         scratch_shapes=list(scratch),
-        compiler_params=pltpu.CompilerParams(vmem_limit_bytes=24 * 1024 * 1024),
+        compiler_params=pltpu.CompilerParams(vmem_limit_bytes=vmem * 1024 * 1024),
     )(*args)
     return got[0] if len(outs) == 1 else got
 
@@ -221,15 +237,18 @@
     d = lax.axis_index("x") * 2 + lax.axis_index("yh")
     pos = jnp.stack([yl, c, d]).astype(jnp.int32)
     forward = lax.dynamic_slice(jnp.asarray(FORWARD), (z, 0, 0, 0), (1,) + FORWARD.shape[1:])[0]
-    inverse = lax.dynamic_slice(jnp.asarray(INVERSE), ((yl * C + c) * Z + z, 0), (1, 64)).reshape(64)
+    inverse = lax.dynamic_slice(
+        jnp.asarray(INVERSE), ((yl * C + c) * Z + z, 0, 0, 0), (1,) + INVERSE.shape[1:]
+    )[0]
     powers = call(powers_kernel, [(MODES, NB)], [VMEM] * 2, omega, zeta, dtype=F32)
 
     spread = call(
         spread_kernel,
         [(YL * Z, PH, HALF)],
-        [pl.BlockSpec(memory_space=pltpu.HBM)],
+        [HBM],
         wake[0],
         out_specs=[HBM],
+        vmem=60,
         scratch=[pltpu.SemaphoreType.DMA((YL * Z,))],
     )
     blocks = lax.all_to_all(spread, ("yl", "z"), 0, 0, tiled=True)
@@ -249,17 +268,17 @@
     by_both = lax.ppermute(by_yl, "c", swap)
     near, forward, inverse, powers = lax.optimization_barrier((near, forward, inverse, powers))
 
-    picked = call(
-        project_kernel,
-        [(PEERS, 4 * TS, NB)],
-        [SMEM] + [VMEM] * 5,
+    joined, onehot = call(
+        select_kernel,
+        [(4 * NB, HALF), (4, NT, YL * Z * PH)],
+        [SMEM] + [VMEM] * 4,
         pos,
-        blocks,
         near,
         by_yl,
         by_c,
         by_both,
     )
+    picked = call(project_kernel, [(PEERS, 4 * TS, NB)], [VMEM] * 3, blocks, joined, onehot)
     parts = lax.all_to_all(picked, PLANE, 0, 0, tiled=True)
     forcing = call(gather_sum_kernel, [(Z, 4 * TS, NB)], [VMEM], parts)
     forcing = lax.all_to_all(forcing, "z", 0, 0, tiled=True)
@@ -276,7 +295,7 @@
         powers,
     )
     physical = lax.all_to_all(physical, "z", 0, 0, tiled=True)
-    sectoral = call(inverse_kernel, [(PEERS, TD, NB)], [SMEM, VMEM], inverse, physical)
+    sectoral = call(inverse_kernel, [(PEERS, TD, NB)], [VMEM] * 2, inverse, physical)
     sectoral = lax.all_to_all(sectoral, PLANE, 0, 0, tiled=True)
     rows = stress_map.shape[1]
     stress = call(

time: 131 us -> 144 us (1.099)
  Pallas kernels: 6.91 us -> 21.1 us
    pallas_call x9 -> x10, Pallas kernels: 6.91 us -> 21.1 us  [call(): pl.pallas_call(kernel, out_shape=outs, in_specs=specs, out_specs=out_spec...]
where the time goes in v6:
time: 144 us; the launch traced here: 143 us
  blocking collectives  78.7 us (55%)
  starting transfers between devices  28.4 us (20%)
  Pallas kernels  21.1 us (15%)
  waiting for transfers between devices  11.7 us (8%)
  local copies, waits for them, and re-layouts  2.93 us (2%)
    pallas_call x10, Pallas kernels, call(): pl.pallas_call(kernel, out_shape=outs, in_specs=specs, out_specs=out_spec...  21.1 us
    all_to_all x1, blocking collectives, local(): parts = lax.all_to_all(picked, PLANE, 0, 0, tiled=True)  17.4 us
    all_to_all x1, starting transfers between devices, local(): blocks = lax.all_to_all(spread, ('yl', 'z'), 0, 0, tiled=True)  17.2 us
    all_to_all x1, blocking collectives, local(): forcing = lax.all_to_all(forcing, 'z', 0, 0, tiled=True)  16.7 us
    all_to_all x1, blocking collectives, local(): physical = lax.all_to_all(physical, 'z', 0, 0, tiled=True)  15.8 us
    all_to_all x1, blocking collectives, local(): sectoral = lax.all_to_all(sectoral, PLANE, 0, 0, tiled=True)  15.6 us
    all_to_all x1, blocking collectives, local(): harmonic = lax.all_to_all(harmonic, PLANE, 0, 0, tiled=True)  13.2 us
    all_to_all x1, waiting for transfers between devices, local(): blocks = lax.all_to_all(spread, ('yl', 'z'), 0, 0, tiled=True)  8.83 us
  transfers between devices with their start and end apart: 4, of which 2 were waited for; matrix products, arithmetic and copies ran while one was open for 1% of the time, Pallas kernels for 1%

profile of v6, /device:TPU:1, one launch (start us, length us, event | category | flops | bytes accessed | tf_op | source)
XLA Modules:
  0.0 143.1 jit_solution(4461826656282027239)
XLA Ops:
  0.0 15.3 %shard_map.111 = bf16[32,8,896]{2,1,0:T(8,128)(2,1)} custom-call(bf16[8,1792]{1,0:T(8,128)(2,1)} %bitcast.17), custom_call_target="tpu_custom_call" | custom-call | tf_op jit(solution)/shard_map/pallas_call | solution.py:224
  15.3 0.0 copy-start.1
  15.3 17.2 %all-to-all-start = ((bf16[32,8,896]{2,1,0:T(8,128)(2,1)}), bf16[32,8,896]{2,1,0:T(8,128)(2,1)S(1)}, u32[]{:S(2)}, u32[]{:S(2)}) async-start(bf16[32,8,896]{2,1,0:T(8,128)(2,1)} %shard_map.111), calls=%async_computation | async-start | bytes 917504 | tf_op jit(solution)/shard_map/all_to_all | solution.py:254
  32.5 0.0 copy-start.5
  32.5 0.1 pad_add_fusion.pos
  32.6 0.0 copy-start.4
  32.6 0.0 copy-done.1
  32.6 0.6 copy-done.5
  33.2 0.1 copy-done.4
  33.3 0.6 shard_map.109
  33.9 3.1 %collective-permute-start = (bf16[144,896]{1,0:T(8,128)(2,1)S(1)}, bf16[144,896]{1,0:T(8,128)(2,1)S(1)}, u32[]{:S(2)}, u32[]{:S(2)}) collective-permute-start(bf16[144,896]{1,0:T(8,128)(2,1)S(1)} %get-tuple-element.17), channel_id=1, source_target_pairs={{0,256},{256,0},{1,257},{257,1},{2,258},{258,2},{3,259},{259,3},{4... | collective-permute-start | bytes 774152 | tf_op jit(solution)/shard_map/ppermute | solution.py:266
  37.0 3.4 %collective-permute-start.1 = (bf16[144,896]{1,0:T(8,128)(2,1)S(1)}, bf16[144,896]{1,0:T(8,128)(2,1)S(1)}, u32[]{:S(2)}, u32[]{:S(2)}) collective-permute-start(bf16[144,896]{1,0:T(8,128)(2,1)S(1)} %get-tuple-element.16.refs_0_), channel_id=1, source_target_pairs={{0,8},{8,0},{1,9},{9,1},{2,10},{10,2},{3,11},{11,3},{4,12},{12,4},... | collective-permute-start | bytes 774152 | tf_op jit(solution)/shard_map/ppermute | solution.py:267
  40.5 2.9 %collective-permute-done.refs_1_ = bf16[144,896]{1,0:T(8,128)(2,1)S(1)} collective-permute-done((bf16[144,896]{1,0:T(8,128)(2,1)S(1)}, bf16[144,896]{1,0:T(8,128)(2,1)S(1)}, u32[]{:S(2)}, u32[]{:S(2)}) %collective-permute-start) | collective-permute-done | bytes 258080 | tf_op jit(solution)/shard_map/ppermute | solution.py:266
  43.3 4.7 %collective-permute-start.2 = (bf16[144,896]{1,0:T(8,128)(2,1)S(1)}, bf16[144,896]{1,0:T(8,128)(2,1)S(1)}, u32[]{:S(2)}, u32[]{:S(2)}) collective-permute-start(bf16[144,896]{1,0:T(8,128)(2,1)S(1)} %collective-permute-done.refs_1_), channel_id=1, source_target_pairs={{0,8},{8,0},{1,9},{9,1},{2,10},{10,2},{3,11},{11,3},{4,12},{12,4},... | collective-permute-start | bytes 774152 | tf_op jit(solution)/shard_map/ppermute | solution.py:268
  48.0 0.0 copy-start.6
  48.0 0.0 copy-start.7
  48.0 0.6 copy-done.6
  48.7 0.0 copy-done.7
  48.7 0.4 shard_map.110.powers_ref
  49.1 0.7 dynamic-slice_bitcast_fusion.1.table_ref
  49.8 0.8 dynamic-slice_bitcast_fusion.table_ref
  50.6 0.0 collective-permute-done.1.refs_2_
  50.6 0.0 collective-permute-done.2.refs_3_
  50.6 0.9 shard_map.112
  51.6 8.8 %all-to-all-done.wake_ref = bf16[32,8,896]{2,1,0:T(8,128)(2,1)S(1)} async-done(((bf16[32,8,896]{2,1,0:T(8,128)(2,1)}), bf16[32,8,896]{2,1,0:T(8,128)(2,1)S(1)}, u32[]{:S(2)}, u32[]{:S(2)}) %all-to-all-start) | async-done | bytes 458784 | tf_op jit(solution)/shard_map/all_to_all | solution.py:254
  60.4 0.7 shard_map.113
  61.2 17.4 %all_to_all.30.in_ref = bf16[32,32,128]{2,1,0:T(8,128)(2,1)S(1)} all-to-all(bf16[32,32,128]{2,1,0:T(8,128)(2,1)S(1)} %shard_map.113), channel_id=1, replica_groups=mesh['yl'=2,'z'=16,'c'=2,'x'=4,'yh'=2] {'yl','c','x','yh'}, dimensions={0} | all-to-all | bytes 524288 | tf_op jit(solution)/shard_map/all_to_all | solution.py:282
  78.6 16.7 %all_to_all.31.in_ref = bf16[16,32,128]{2,1,0:T(8,128)(2,1)S(1)} all-to-all(bf16[16,32,128]{2,1,0:T(8,128)(2,1)S(1)} %shard_map.114), channel_id=1, replica_groups=mesh['yl'=2,'z'=16,'c'=2,'x'=4,'yh'=2] {'z'}, dimensions={0} | all-to-all | bytes 262144 | tf_op jit(solution)/shard_map/all_to_all | solution.py:284
  95.4 0.2 shard_map.115
  95.5 0.0 copy-start.2
  95.5 0.0 copy-start.3
  95.6 13.2 %all_to_all.32.in_ref = bf16[32,8,128]{2,1,0:T(8,128)(2,1)S(1)} all-to-all(bf16[32,8,128]{2,1,0:T(8,128)(2,1)S(1)} %shard_map.115), channel_id=1, replica_groups=mesh['yl'=2,'z'=16,'c'=2,'x'=4,'yh'=2] {'yl','c','x','yh'}, dimensions={0} | all-to-all | bytes 131072 | tf_op jit(solution)/shard_map/all_to_all | solution.py:286
  108.7 0.0 copy-done.2
  108.7 0.0 copy-done.3
  108.7 1.5 %shard_map.116 = bf16[16,32,128]{2,1,0:T(8,128)(2,1)S(1)} custom-call(s32[3]{0:T(128)S(1)} %pad_add_fusion.pos, bf16[32,8,128]{2,1,0:T(8,128)(2,1)S(1)} %all_to_all.32.in_ref, bf16[40,128]{1,0:T(8,128)(2,1)S(1)} %bitcast.16, bf16[128,128]{1,0:T(8,128)(2,1)S(1)} %bitcast.15, f32[40,128]{1,0:T(8,128)S(1)} %shard_map.110.powers_ref), custom_call_target="tpu_custom_call" | custom-call | tf_op jit(solution)/shard_map/pallas_call | solution.py:224
  110.2 15.8 %all_to_all.33.in_ref = bf16[16,32,128]{2,1,0:T(8,128)(2,1)S(1)} all-to-all(bf16[16,32,128]{2,1,0:T(8,128)(2,1)S(1)} %shard_map.116), channel_id=1, replica_groups=mesh['yl'=2,'z'=16,'c'=2,'x'=4,'yh'=2] {'z'}, dimensions={0} | all-to-all | bytes 262144 | tf_op jit(solution)/shard_map/all_to_all | solution.py:297
  126.0 0.0 copy-start
  126.0 0.2 shard_map.117
  126.2 15.6 %all_to_all.34.in_ref = bf16[32,32,128]{2,1,0:T(8,128)(2,1)S(1)} all-to-all(bf16[32,32,128]{2,1,0:T(8,128)(2,1)S(1)} %shard_map.117), channel_id=1, replica_groups=mesh['yl'=2,'z'=16,'c'=2,'x'=4,'yh'=2] {'yl','c','x','yh'}, dimensions={0} | all-to-all | bytes 524288 | tf_op jit(solution)/shard_map/all_to_all | solution.py:299
  141.8 0.0 copy-done
  141.8 1.3 shard_map.118
  (1 shorter events, 0.0 us)
Async XLA Ops:
  15.3 17.3 %copy-start.1 = (bf16[1,128,1792]{2,1,0:T(8,128)(2,1)S(1)}, bf16[1,128,1792]{2,1,0:T(8,128)(2,1)}, u32[]{:S(2)}) copy-start(bf16[1,128,1792]{2,1,0:T(8,128)(2,1)} %param.12) | copy-start | bytes 1376260
  15.3 45.1 %all-to-all-start = ((bf16[32,8,896]{2,1,0:T(8,128)(2,1)}), bf16[32,8,896]{2,1,0:T(8,128)(2,1)S(1)}, u32[]{:S(2)}, u32[]{:S(2)}) async-start(bf16[32,8,896]{2,1,0:T(8,128)(2,1)} %shard_map.111), calls=%async_computation | async-start | bytes 917504 | tf_op jit(solution)/shard_map/all_to_all | solution.py:254
  32.5 0.7 copy-start.5
  32.6 0.7 copy-start.4
  33.9 9.5 %collective-permute-start = (bf16[144,896]{1,0:T(8,128)(2,1)S(1)}, bf16[144,896]{1,0:T(8,128)(2,1)S(1)}, u32[]{:S(2)}, u32[]{:S(2)}) collective-permute-start(bf16[144,896]{1,0:T(8,128)(2,1)S(1)} %get-tuple-element.17), channel_id=1, source_target_pairs={{0,256},{256,0},{1,257},{257,1},{2,258},{258,2},{3,259},{259,3},{4... | collective-permute-start | bytes 774152 | tf_op jit(solution)/shard_map/ppermute | solution.py:266
  37.0 13.6 %collective-permute-start.1 = (bf16[144,896]{1,0:T(8,128)(2,1)S(1)}, bf16[144,896]{1,0:T(8,128)(2,1)S(1)}, u32[]{:S(2)}, u32[]{:S(2)}) collective-permute-start(bf16[144,896]{1,0:T(8,128)(2,1)S(1)} %get-tuple-element.16.refs_0_), channel_id=1, source_target_pairs={{0,8},{8,0},{1,9},{9,1},{2,10},{10,2},{3,11},{11,3},{4,12},{12,4},... | collective-permute-start | bytes 774152 | tf_op jit(solution)/shard_map/ppermute | solution.py:267
  43.3 7.3 %collective-permute-start.2 = (bf16[144,896]{1,0:T(8,128)(2,1)S(1)}, bf16[144,896]{1,0:T(8,128)(2,1)S(1)}, u32[]{:S(2)}, u32[]{:S(2)}) collective-permute-start(bf16[144,896]{1,0:T(8,128)(2,1)S(1)} %collective-permute-done.refs_1_), channel_id=1, source_target_pairs={{0,8},{8,0},{1,9},{9,1},{2,10},{10,2},{3,11},{11,3},{4,12},{12,4},... | collective-permute-start | bytes 774152 | tf_op jit(solution)/shard_map/ppermute | solution.py:268
  48.0 0.7 copy-start.6
  48.0 0.7 copy-start.7
  95.5 13.2 %copy-start.2 = (bf16[1,128,128]{2,1,0:T(8,128)(2,1)S(1)}, bf16[1,128,128]{2,1,0:T(8,128)(2,1)}, u32[]{:S(2)}) copy-start(bf16[1,128,128]{2,1,0:T(8,128)(2,1)} %param.16) | copy-start | bytes 98308
  95.5 13.2 %copy-start.3 = (bf16[1,40,128]{2,1,0:T(8,128)(2,1)S(1)}, bf16[1,40,128]{2,1,0:T(8,128)(2,1)}, u32[]{:S(2)}) copy-start(bf16[1,40,128]{2,1,0:T(8,128)(2,1)} %param.15) | copy-start | bytes 30724
  126.0 15.8 %copy-start = (bf16[1,2048,128]{2,1,0:T(8,128)(2,1)S(1)}, bf16[1,2048,128]{2,1,0:T(8,128)(2,1)}, u32[]{:S(2)}) copy-start(bf16[1,2048,128]{2,1,0:T(8,128)(2,1)} %param.19) | copy-start | bytes 1572868

commit v7 on v6

--- a/solution.py
+++ b/solution.py
@@ -61,14 +61,17 @@
     )
 
 
-def spread_kernel(in_ref, out_ref, sem):
+def spread_kernel(in_ref, out_ref, wake_ref, hold_ref, sems):
+    copy = pltpu.make_async_copy(in_ref, wake_ref, sems.at[YL])
+    copy.start()
+    copy.wait()
     copies = []
     for half in range(YL):
-        part = in_ref.at[:, pl.ds(half * HALF, HALF)]
-        for z in range(Z):
-            k = half * Z + z
-            copies.append(pltpu.make_async_copy(part, out_ref.at[k], sem.at[k]))
-            copies[-1].start()
+        rows = pl.ds(half * Z, Z)
+        part = wake_ref[:, half * HALF : (half + 1) * HALF]
+        hold_ref[rows] = jnp.broadcast_to(part[None], (Z, PH, HALF))
+        copies.append(pltpu.make_async_copy(hold_ref.at[rows], out_ref.at[rows], sems.at[half]))
+        copies[-1].start()
     for copy in copies:
         copy.wait()
 
@@ -249,7 +252,11 @@
         wake[0],
         out_specs=[HBM],
         vmem=60,
-        scratch=[pltpu.SemaphoreType.DMA((YL * Z,))],
+        scratch=[
+            pltpu.VMEM((PH, YL * HALF), BF),
+            pltpu.VMEM((YL * Z, PH, HALF), BF),
+            pltpu.SemaphoreType.DMA((YL + 1,)),
+        ],
     )
     blocks = lax.all_to_all(spread, ("yl", "z"), 0, 0, tiled=True)
 

time: 144 us -> 130 us (0.903)
  Pallas kernels: 21.1 us -> 7.35 us
    pallas_call x10, Pallas kernels: 21.1 us -> 7.35 us  [call(): pl.pallas_call(kernel, out_shape=outs, in_specs=specs, out_specs=out_spec...]
where the time goes in v7:
time: 130 us; the launch traced here: 129 us
  blocking collectives  78.7 us (61%)
  starting transfers between devices  28.4 us (22%)
  waiting for transfers between devices  11.7 us (9%)
  Pallas kernels  7.35 us (6%)
  local copies, waits for them, and re-layouts  2.93 us (2%)
    all_to_all x1, blocking collectives, local(): parts = lax.all_to_all(picked, PLANE, 0, 0, tiled=True)  17.4 us
    all_to_all x1, starting transfers between devices, local(): blocks = lax.all_to_all(spread, ('yl', 'z'), 0, 0, tiled=True)  17.2 us
    all_to_all x1, blocking collectives, local(): forcing = lax.all_to_all(forcing, 'z', 0, 0, tiled=True)  16.7 us
    all_to_all x1, blocking collectives, local(): physical = lax.all_to_all(physical, 'z', 0, 0, tiled=True)  15.8 us
    all_to_all x1, blocking collectives, local(): sectoral = lax.all_to_all(sectoral, PLANE, 0, 0, tiled=True)  15.6 us
    all_to_all x1, blocking collectives, local(): harmonic = lax.all_to_all(harmonic, PLANE, 0, 0, tiled=True)  13.2 us
    all_to_all x1, waiting for transfers between devices, local(): blocks = lax.all_to_all(spread, ('yl', 'z'), 0, 0, tiled=True)  8.83 us
    pallas_call x10, Pallas kernels, call(): pl.pallas_call(kernel, out_shape=outs, in_specs=specs, out_specs=out_spec...  7.35 us
  transfers between devices with their start and end apart: 4, of which 2 were waited for; matrix products, arithmetic and copies ran while one was open for 1% of the time, Pallas kernels for 1%

profile of v7, /device:TPU:1, one launch (start us, length us, event | category | flops | bytes accessed | tf_op | source)
XLA Modules:
  0.0 129.3 jit_solution(6653266555302684040)
XLA Ops:
  0.0 1.6 %shard_map.111 = bf16[32,8,896]{2,1,0:T(8,128)(2,1)} custom-call(bf16[8,1792]{1,0:T(8,128)(2,1)} %bitcast.17), custom_call_target="tpu_custom_call" | custom-call | tf_op jit(solution)/shard_map/pallas_call | solution.py:227
  1.6 0.0 copy-start.1
  1.6 17.2 %all-to-all-start = ((bf16[32,8,896]{2,1,0:T(8,128)(2,1)}), bf16[32,8,896]{2,1,0:T(8,128)(2,1)S(1)}, u32[]{:S(2)}, u32[]{:S(2)}) async-start(bf16[32,8,896]{2,1,0:T(8,128)(2,1)} %shard_map.111), calls=%async_computation | async-start | bytes 917504 | tf_op jit(solution)/shard_map/all_to_all | solution.py:261
  18.8 0.0 copy-start.5
  18.8 0.1 pad_add_fusion.pos
  18.9 0.0 copy-start.4
  18.9 0.0 copy-done.1
  18.9 0.6 copy-done.5
  19.5 0.1 copy-done.4
  19.5 0.6 shard_map.109
  20.1 3.1 %collective-permute-start = (bf16[144,896]{1,0:T(8,128)(2,1)S(1)}, bf16[144,896]{1,0:T(8,128)(2,1)S(1)}, u32[]{:S(2)}, u32[]{:S(2)}) collective-permute-start(bf16[144,896]{1,0:T(8,128)(2,1)S(1)} %get-tuple-element.17), channel_id=1, source_target_pairs={{0,256},{256,0},{1,257},{257,1},{2,258},{258,2},{3,259},{259,3},{4... | collective-permute-start | bytes 774152 | tf_op jit(solution)/shard_map/ppermute | solution.py:273
  23.3 3.4 %collective-permute-start.1 = (bf16[144,896]{1,0:T(8,128)(2,1)S(1)}, bf16[144,896]{1,0:T(8,128)(2,1)S(1)}, u32[]{:S(2)}, u32[]{:S(2)}) collective-permute-start(bf16[144,896]{1,0:T(8,128)(2,1)S(1)} %get-tuple-element.16.refs_0_), channel_id=1, source_target_pairs={{0,8},{8,0},{1,9},{9,1},{2,10},{10,2},{3,11},{11,3},{4,12},{12,4},... | collective-permute-start | bytes 774152 | tf_op jit(solution)/shard_map/ppermute | solution.py:274
  26.7 2.9 %collective-permute-done.refs_1_ = bf16[144,896]{1,0:T(8,128)(2,1)S(1)} collective-permute-done((bf16[144,896]{1,0:T(8,128)(2,1)S(1)}, bf16[144,896]{1,0:T(8,128)(2,1)S(1)}, u32[]{:S(2)}, u32[]{:S(2)}) %collective-permute-start) | collective-permute-done | bytes 258080 | tf_op jit(solution)/shard_map/ppermute | solution.py:273
  29.6 4.7 %collective-permute-start.2 = (bf16[144,896]{1,0:T(8,128)(2,1)S(1)}, bf16[144,896]{1,0:T(8,128)(2,1)S(1)}, u32[]{:S(2)}, u32[]{:S(2)}) collective-permute-start(bf16[144,896]{1,0:T(8,128)(2,1)S(1)} %collective-permute-done.refs_1_), channel_id=1, source_target_pairs={{0,8},{8,0},{1,9},{9,1},{2,10},{10,2},{3,11},{11,3},{4,12},{12,4},... | collective-permute-start | bytes 774152 | tf_op jit(solution)/shard_map/ppermute | solution.py:275
  34.3 0.0 copy-start.6
  34.3 0.0 copy-start.7
  34.3 0.6 copy-done.6
  34.9 0.0 copy-done.7
  34.9 0.4 shard_map.110.powers_ref
  35.3 0.7 dynamic-slice_bitcast_fusion.1.table_ref
  36.0 0.8 dynamic-slice_bitcast_fusion.table_ref
  36.9 0.0 collective-permute-done.1.refs_2_
  36.9 0.0 collective-permute-done.2.refs_3_
  36.9 0.9 shard_map.112
  37.8 8.8 %all-to-all-done.wake_ref = bf16[32,8,896]{2,1,0:T(8,128)(2,1)S(1)} async-done(((bf16[32,8,896]{2,1,0:T(8,128)(2,1)}), bf16[32,8,896]{2,1,0:T(8,128)(2,1)S(1)}, u32[]{:S(2)}, u32[]{:S(2)}) %all-to-all-start) | async-done | bytes 458784 | tf_op jit(solution)/shard_map/all_to_all | solution.py:261
  46.7 0.7 shard_map.113
  47.4 17.4 %all_to_all.30.in_ref = bf16[32,32,128]{2,1,0:T(8,128)(2,1)S(1)} all-to-all(bf16[32,32,128]{2,1,0:T(8,128)(2,1)S(1)} %shard_map.113), channel_id=1, replica_groups=mesh['yl'=2,'z'=16,'c'=2,'x'=4,'yh'=2] {'yl','c','x','yh'}, dimensions={0} | all-to-all | bytes 524288 | tf_op jit(solution)/shard_map/all_to_all | solution.py:289
  64.9 16.7 %all_to_all.31.in_ref = bf16[16,32,128]{2,1,0:T(8,128)(2,1)S(1)} all-to-all(bf16[16,32,128]{2,1,0:T(8,128)(2,1)S(1)} %shard_map.114), channel_id=1, replica_groups=mesh['yl'=2,'z'=16,'c'=2,'x'=4,'yh'=2] {'z'}, dimensions={0} | all-to-all | bytes 262144 | tf_op jit(solution)/shard_map/all_to_all | solution.py:291
  81.6 0.2 shard_map.115
  81.8 0.0 copy-start.2
  81.8 0.0 copy-start.3
  81.8 13.2 %all_to_all.32.in_ref = bf16[32,8,128]{2,1,0:T(8,128)(2,1)S(1)} all-to-all(bf16[32,8,128]{2,1,0:T(8,128)(2,1)S(1)} %shard_map.115), channel_id=1, replica_groups=mesh['yl'=2,'z'=16,'c'=2,'x'=4,'yh'=2] {'yl','c','x','yh'}, dimensions={0} | all-to-all | bytes 131072 | tf_op jit(solution)/shard_map/all_to_all | solution.py:293
  95.0 0.0 copy-done.2
  95.0 0.0 copy-done.3
  95.0 1.5 %shard_map.116 = bf16[16,32,128]{2,1,0:T(8,128)(2,1)S(1)} custom-call(s32[3]{0:T(128)S(1)} %pad_add_fusion.pos, bf16[32,8,128]{2,1,0:T(8,128)(2,1)S(1)} %all_to_all.32.in_ref, bf16[40,128]{1,0:T(8,128)(2,1)S(1)} %bitcast.16, bf16[128,128]{1,0:T(8,128)(2,1)S(1)} %bitcast.15, f32[40,128]{1,0:T(8,128)S(1)} %shard_map.110.powers_ref), custom_call_target="tpu_custom_call" | custom-call | tf_op jit(solution)/shard_map/pallas_call | solution.py:227
  96.5 15.8 %all_to_all.33.in_ref = bf16[16,32,128]{2,1,0:T(8,128)(2,1)S(1)} all-to-all(bf16[16,32,128]{2,1,0:T(8,128)(2,1)S(1)} %shard_map.116), channel_id=1, replica_groups=mesh['yl'=2,'z'=16,'c'=2,'x'=4,'yh'=2] {'z'}, dimensions={0} | all-to-all | bytes 262144 | tf_op jit(solution)/shard_map/all_to_all | solution.py:304
  112.3 0.0 copy-start
  112.3 0.2 shard_map.117
  112.4 15.6 %all_to_all.34.in_ref = bf16[32,32,128]{2,1,0:T(8,128)(2,1)S(1)} all-to-all(bf16[32,32,128]{2,1,0:T(8,128)(2,1)S(1)} %shard_map.117), channel_id=1, replica_groups=mesh['yl'=2,'z'=16,'c'=2,'x'=4,'yh'=2] {'yl','c','x','yh'}, dimensions={0} | all-to-all | bytes 524288 | tf_op jit(solution)/shard_map/all_to_all | solution.py:306
  128.0 0.0 copy-done
  128.0 1.3 %shard_map.118 = bf16[2048,256]{1,0:T(8,128)(2,1)} custom-call(bf16[32,32,128]{2,1,0:T(8,128)(2,1)S(1)} %all_to_all.34.in_ref, bf16[2048,128]{1,0:T(8,128)(2,1)S(1)} %bitcast.13), custom_call_target="tpu_custom_call" | custom-call | tf_op jit(solution)/shard_map/pallas_call | solution.py:227
  (1 shorter events, 0.0 us)
Async XLA Ops:
  1.6 17.3 %copy-start.1 = (bf16[1,128,1792]{2,1,0:T(8,128)(2,1)S(1)}, bf16[1,128,1792]{2,1,0:T(8,128)(2,1)}, u32[]{:S(2)}) copy-start(bf16[1,128,1792]{2,1,0:T(8,128)(2,1)} %param.12) | copy-start | bytes 1376260
  1.6 45.1 %all-to-all-start = ((bf16[32,8,896]{2,1,0:T(8,128)(2,1)}), bf16[32,8,896]{2,1,0:T(8,128)(2,1)S(1)}, u32[]{:S(2)}, u32[]{:S(2)}) async-start(bf16[32,8,896]{2,1,0:T(8,128)(2,1)} %shard_map.111), calls=%async_computation | async-start | bytes 917504 | tf_op jit(solution)/shard_map/all_to_all | solution.py:261
  18.8 0.7 copy-start.5
  18.9 0.7 copy-start.4
  20.1 9.5 %collective-permute-start = (bf16[144,896]{1,0:T(8,128)(2,1)S(1)}, bf16[144,896]{1,0:T(8,128)(2,1)S(1)}, u32[]{:S(2)}, u32[]{:S(2)}) collective-permute-start(bf16[144,896]{1,0:T(8,128)(2,1)S(1)} %get-tuple-element.17), channel_id=1, source_target_pairs={{0,256},{256,0},{1,257},{257,1},{2,258},{258,2},{3,259},{259,3},{4... | collective-permute-start | bytes 774152 | tf_op jit(solution)/shard_map/ppermute | solution.py:273
  23.3 13.6 %collective-permute-start.1 = (bf16[144,896]{1,0:T(8,128)(2,1)S(1)}, bf16[144,896]{1,0:T(8,128)(2,1)S(1)}, u32[]{:S(2)}, u32[]{:S(2)}) collective-permute-start(bf16[144,896]{1,0:T(8,128)(2,1)S(1)} %get-tuple-element.16.refs_0_), channel_id=1, source_target_pairs={{0,8},{8,0},{1,9},{9,1},{2,10},{10,2},{3,11},{11,3},{4,12},{12,4},... | collective-permute-start | bytes 774152 | tf_op jit(solution)/shard_map/ppermute | solution.py:274
  29.6 7.3 %collective-permute-start.2 = (bf16[144,896]{1,0:T(8,128)(2,1)S(1)}, bf16[144,896]{1,0:T(8,128)(2,1)S(1)}, u32[]{:S(2)}, u32[]{:S(2)}) collective-permute-start(bf16[144,896]{1,0:T(8,128)(2,1)S(1)} %collective-permute-done.refs_1_), channel_id=1, source_target_pairs={{0,8},{8,0},{1,9},{9,1},{2,10},{10,2},{3,11},{11,3},{4,12},{12,4},... | collective-permute-start | bytes 774152 | tf_op jit(solution)/shard_map/ppermute | solution.py:275
  34.3 0.7 copy-start.6
  34.3 0.7 copy-start.7
  81.8 13.2 %copy-start.2 = (bf16[1,128,128]{2,1,0:T(8,128)(2,1)S(1)}, bf16[1,128,128]{2,1,0:T(8,128)(2,1)}, u32[]{:S(2)}) copy-start(bf16[1,128,128]{2,1,0:T(8,128)(2,1)} %param.16) | copy-start | bytes 98308
  81.8 13.2 %copy-start.3 = (bf16[1,40,128]{2,1,0:T(8,128)(2,1)S(1)}, bf16[1,40,128]{2,1,0:T(8,128)(2,1)}, u32[]{:S(2)}) copy-start(bf16[1,40,128]{2,1,0:T(8,128)(2,1)} %param.15) | copy-start | bytes 30724
  112.3 15.8 %copy-start = (bf16[1,2048,128]{2,1,0:T(8,128)(2,1)S(1)}, bf16[1,2048,128]{2,1,0:T(8,128)(2,1)}, u32[]{:S(2)}) copy-start(bf16[1,2048,128]{2,1,0:T(8,128)(2,1)} %param.19) | copy-start | bytes 1572868

commit v8 on v7

--- a/solution.py
+++ b/solution.py
@@ -145,43 +145,49 @@
 
 
 def powers_kernel(omega_ref, zeta_ref, out_ref):
-    damp = jnp.concatenate([omega_ref[...], zeta_ref[...], jnp.zeros((6, MODES), F32)], axis=0).T
-    omega, zeta = damp[:, 0:1], damp[:, 1:2]
+    omega, zeta = omega_ref[...], zeta_ref[...]
     size = jnp.exp(-omega * zeta)
     angle = omega * jnp.sqrt(1.0 - zeta * zeta)
     real, imag = size * jnp.cos(angle), size * jnp.sin(angle)
-    lane = lax.broadcasted_iota(jnp.int32, (MODES, NB), 1)
-    powers = jnp.zeros((MODES, NB), F32)
+    out_ref[...] = jnp.zeros_like(out_ref)
     for k in range(8):
-        powers = jnp.where(lane == 2 * k, real, jnp.where(lane == 2 * k + 1, imag, powers))
+        out_ref[2 * k : 2 * k + 1, 0:MODES] = real
+        out_ref[2 * k + 1 : 2 * k + 2, 0:MODES] = imag
         real, imag = real * real - imag * imag, 2.0 * real * imag
-    out_ref[...] = powers
-
-
-def modal_kernel(pos, in_ref, shapes_ref, flex_ref, powers_ref, out_ref):
-    shapes = shapes_ref[...]
-    real = dot_nt(shapes, in_ref[...].reshape(NT, NB))
+
+
+def modal_kernel(pos, in_ref, shapes_ref, flex_ref, powers_ref, out_ref, hold_ref):
+    shapes = jnp.concatenate(
+        [shapes_ref[...].astype(F32), jnp.zeros((NB - MODES, NB), F32)], axis=0
+    ).astype(BF)
+    real = dot_nt(in_ref[...].reshape(NT, NB), shapes)
+    imag = jnp.zeros_like(real)
+    row = lax.broadcasted_iota(jnp.int32, (NT, NB), 0)
+    for k in range(8):
+        s = 2**k
+        pr, pi = powers_ref[2 * k : 2 * k + 1, :], powers_ref[2 * k + 1 : 2 * k + 2, :]
+        if s < 8:
+            sr = jnp.where(row >= s, pltpu.roll(real, s, 0), 0.0)
+            if k == 0:
+                real, imag = real + pr * sr, pi * sr
+            else:
+                si = jnp.where(row >= s, pltpu.roll(imag, s, 0), 0.0)
+                real, imag = real + (pr * sr - pi * si), imag + (pr * si + pi * sr)
+        else:
+            sr, si = real[: NT - s], imag[: NT - s]
+            real = jnp.concatenate([real[:s], real[s:] + (pr * sr - pi * si)], axis=0)
+            imag = jnp.concatenate([imag[:s], imag[s:] + (pr * si + pi * sr)], axis=0)
+    hold_ref[...] = imag
+    own = hold_ref[pl.ds(pl.multiple_of(pos[2] * TD, TD), TD), :]
+    high = own.astype(BF)
+    low = (own - high.astype(F32)).astype(BF)
     rows = in_ref[pl.ds(pos[2] * (TD // TS), TD // TS)].reshape(TD, NB)
-    direct = dot_nt(rows, flex_ref[...])
-    imag = None
-    powers = powers_ref[...]
-    lane = lax.broadcasted_iota(jnp.int32, (MODES, NT), 1)
-    for k in range(8):
-        pr, pi = powers[:, 2 * k : 2 * k + 1], powers[:, 2 * k + 1 : 2 * k + 2]
-        keep = lane >= 2**k
-        sr = jnp.where(keep, pltpu.roll(real, 2**k, 1), 0.0)
-        if imag is None:
-            real, imag = real + pr * sr, pi * sr
-        else:
-            si = jnp.where(keep, pltpu.roll(imag, 2**k, 1), 0.0)
-            real, imag = real + (pr * sr - pi * si), imag + (pr * si + pi * sr)
-    own = pltpu.roll(imag, lax.rem(NT - pos[2] * TD, NT), 1)[:, 0:128]
-    high = own.astype(BF).astype(F32)
-    amplitude = jnp.concatenate([high, own - high], axis=0).T[0:TD].astype(BF)
-    modal = jnp.dot(
-        amplitude, jnp.concatenate([shapes, shapes], axis=0), preferred_element_type=F32
-    )
-    out_ref[...] = jnp.broadcast_to((modal + direct).astype(BF)[None], out_ref.shape)
+    total = (
+        jnp.dot(high, shapes, preferred_element_type=F32)
+        + jnp.dot(low, shapes, preferred_element_type=F32)
+        + dot_nt(rows, flex_ref[...])
+    )
+    out_ref[...] = jnp.broadcast_to(total.astype(BF)[None], out_ref.shape)
 
 
 def inverse_kernel(table_ref, in_ref, out_ref):
@@ -197,7 +203,7 @@
         out_ref[s * D : (s + 1) * D] = jnp.broadcast_to(part[None], (D, TD, NB))
 
 
-CHUNKS = 4
+CHUNKS = 8
 
 
 def stress_kernel(in_ref, map_ref, out_ref, hold_ref, sems):
@@ -243,7 +249,7 @@
     inverse = lax.dynamic_slice(
         jnp.asarray(INVERSE), ((yl * C + c) * Z + z, 0, 0, 0), (1,) + INVERSE.shape[1:]
     )[0]
-    powers = call(powers_kernel, [(MODES, NB)], [VMEM] * 2, omega, zeta, dtype=F32)
+    powers = call(powers_kernel, [(16, NB)], [VMEM] * 2, omega, zeta, dtype=F32)
 
     spread = call(
         spread_kernel,
@@ -300,6 +306,7 @@
         shapes[0],
         flex[0],
         powers,
+        scratch=[pltpu.VMEM((NT, NB), F32)],
     )
     physical = lax.all_to_all(physical, "z", 0, 0, tiled=True)
     sectoral = call(inverse_kernel, [(PEERS, TD, NB)], [VMEM] * 2, inverse, physical)

time: 130 us -> 130 us (level)
  no operation moved by 1% of the time
where the time goes in v8:
time: 130 us; the launch traced here: 129 us
  blocking collectives  78.7 us (61%)
  starting transfers between devices  28.4 us (22%)
  waiting for transfers between devices  12 us (9%)
  Pallas kernels  6.61 us (5%)
  local copies, waits for them, and re-layouts  2.93 us (2%)
    all_to_all x1, blocking collectives, local(): parts = lax.all_to_all(picked, PLANE, 0, 0, tiled=True)  17.4 us
    all_to_all x1, starting transfers between devices, local(): blocks = lax.all_to_all(spread, ('yl', 'z'), 0, 0, tiled=True)  17.2 us
    all_to_all x1, blocking collectives, local(): forcing = lax.all_to_all(forcing, 'z', 0, 0, tiled=True)  16.7 us
    all_to_all x1, blocking collectives, local(): physical = lax.all_to_all(physical, 'z', 0, 0, tiled=True)  15.8 us
    all_to_all x1, blocking collectives, local(): sectoral = lax.all_to_all(sectoral, PLANE, 0, 0, tiled=True)  15.6 us
    all_to_all x1, blocking collectives, local(): harmonic = lax.all_to_all(harmonic, PLANE, 0, 0, tiled=True)  13.2 us
    all_to_all x1, waiting for transfers between devices, local(): blocks = lax.all_to_all(spread, ('yl', 'z'), 0, 0, tiled=True)  9.13 us
    pallas_call x10, Pallas kernels, call(): pl.pallas_call(kernel, out_shape=outs, in_specs=specs, out_specs=out_spec...  6.61 us
  transfers between devices with their start and end apart: 4, of which 2 were waited for; matrix products, arithmetic and copies ran while one was open for 1% of the time, Pallas kernels for 1%

profile of v8, /device:TPU:1, one launch (start us, length us, event | category | flops | bytes accessed | tf_op | source)
XLA Modules:
  0.0 128.9 jit_solution(346226702801017968)
XLA Ops:
  0.0 1.6 %shard_map.111 = bf16[32,8,896]{2,1,0:T(8,128)(2,1)} custom-call(bf16[8,1792]{1,0:T(8,128)(2,1)} %bitcast.17), custom_call_target="tpu_custom_call" | custom-call | tf_op jit(solution)/shard_map/pallas_call | solution.py:233
  1.6 0.0 copy-start.1
  1.6 17.2 %all-to-all-start = ((bf16[32,8,896]{2,1,0:T(8,128)(2,1)}), bf16[32,8,896]{2,1,0:T(8,128)(2,1)S(1)}, u32[]{:S(2)}, u32[]{:S(2)}) async-start(bf16[32,8,896]{2,1,0:T(8,128)(2,1)} %shard_map.111), calls=%async_computation | async-start | bytes 917504 | tf_op jit(solution)/shard_map/all_to_all | solution.py:267
  18.8 0.0 copy-start.5
  18.8 0.1 pad_add_fusion.pos
  18.9 0.0 copy-start.4
  18.9 0.0 copy-done.1
  18.9 0.6 copy-done.5
  19.5 0.1 copy-done.4
  19.5 0.6 shard_map.109
  20.1 3.1 %collective-permute-start = (bf16[144,896]{1,0:T(8,128)(2,1)S(1)}, bf16[144,896]{1,0:T(8,128)(2,1)S(1)}, u32[]{:S(2)}, u32[]{:S(2)}) collective-permute-start(bf16[144,896]{1,0:T(8,128)(2,1)S(1)} %get-tuple-element.17), channel_id=1, source_target_pairs={{0,256},{256,0},{1,257},{257,1},{2,258},{258,2},{3,259},{259,3},{4... | collective-permute-start | bytes 774152 | tf_op jit(solution)/shard_map/ppermute | solution.py:279
  23.3 3.4 %collective-permute-start.1 = (bf16[144,896]{1,0:T(8,128)(2,1)S(1)}, bf16[144,896]{1,0:T(8,128)(2,1)S(1)}, u32[]{:S(2)}, u32[]{:S(2)}) collective-permute-start(bf16[144,896]{1,0:T(8,128)(2,1)S(1)} %get-tuple-element.16.refs_0_), channel_id=1, source_target_pairs={{0,8},{8,0},{1,9},{9,1},{2,10},{10,2},{3,11},{11,3},{4,12},{12,4},... | collective-permute-start | bytes 774152 | tf_op jit(solution)/shard_map/ppermute | solution.py:280
  26.7 2.9 %collective-permute-done.refs_1_ = bf16[144,896]{1,0:T(8,128)(2,1)S(1)} collective-permute-done((bf16[144,896]{1,0:T(8,128)(2,1)S(1)}, bf16[144,896]{1,0:T(8,128)(2,1)S(1)}, u32[]{:S(2)}, u32[]{:S(2)}) %collective-permute-start) | collective-permute-done | bytes 258080 | tf_op jit(solution)/shard_map/ppermute | solution.py:279
  29.6 4.7 %collective-permute-start.2 = (bf16[144,896]{1,0:T(8,128)(2,1)S(1)}, bf16[144,896]{1,0:T(8,128)(2,1)S(1)}, u32[]{:S(2)}, u32[]{:S(2)}) collective-permute-start(bf16[144,896]{1,0:T(8,128)(2,1)S(1)} %collective-permute-done.refs_1_), channel_id=1, source_target_pairs={{0,8},{8,0},{1,9},{9,1},{2,10},{10,2},{3,11},{11,3},{4,12},{12,4},... | collective-permute-start | bytes 774152 | tf_op jit(solution)/shard_map/ppermute | solution.py:281
  34.3 0.0 copy-start.6
  34.3 0.0 copy-start.7
  34.3 0.6 copy-done.6
  34.9 0.0 copy-done.7
  34.9 0.1 shard_map.110.powers_ref
  35.0 0.7 dynamic-slice_bitcast_fusion.1.table_ref
  35.7 0.8 dynamic-slice_bitcast_fusion.table_ref
  36.6 0.0 collective-permute-done.1.refs_2_
  36.6 0.0 collective-permute-done.2.refs_3_
  36.6 0.9 shard_map.112
  37.5 9.1 %all-to-all-done.wake_ref = bf16[32,8,896]{2,1,0:T(8,128)(2,1)S(1)} async-done(((bf16[32,8,896]{2,1,0:T(8,128)(2,1)}), bf16[32,8,896]{2,1,0:T(8,128)(2,1)S(1)}, u32[]{:S(2)}, u32[]{:S(2)}) %all-to-all-start) | async-done | bytes 458784 | tf_op jit(solution)/shard_map/all_to_all | solution.py:267
  46.7 0.7 shard_map.113
  47.4 17.4 %all_to_all.30.in_ref = bf16[32,32,128]{2,1,0:T(8,128)(2,1)S(1)} all-to-all(bf16[32,32,128]{2,1,0:T(8,128)(2,1)S(1)} %shard_map.113), channel_id=1, replica_groups=mesh['yl'=2,'z'=16,'c'=2,'x'=4,'yh'=2] {'yl','c','x','yh'}, dimensions={0} | all-to-all | bytes 524288 | tf_op jit(solution)/shard_map/all_to_all | solution.py:295
  64.9 16.7 %all_to_all.31.in_ref = bf16[16,32,128]{2,1,0:T(8,128)(2,1)S(1)} all-to-all(bf16[16,32,128]{2,1,0:T(8,128)(2,1)S(1)} %shard_map.114), channel_id=1, replica_groups=mesh['yl'=2,'z'=16,'c'=2,'x'=4,'yh'=2] {'z'}, dimensions={0} | all-to-all | bytes 262144 | tf_op jit(solution)/shard_map/all_to_all | solution.py:297
  81.6 0.2 shard_map.115
  81.8 0.0 copy-start.2
  81.8 0.0 copy-start.3
  81.8 13.2 %all_to_all.32.in_ref = bf16[32,8,128]{2,1,0:T(8,128)(2,1)S(1)} all-to-all(bf16[32,8,128]{2,1,0:T(8,128)(2,1)S(1)} %shard_map.115), channel_id=1, replica_groups=mesh['yl'=2,'z'=16,'c'=2,'x'=4,'yh'=2] {'yl','c','x','yh'}, dimensions={0} | all-to-all | bytes 131072 | tf_op jit(solution)/shard_map/all_to_all | solution.py:299
  95.0 0.0 copy-done.2
  95.0 0.0 copy-done.3
  95.0 1.1 shard_map.116
  96.1 15.8 %all_to_all.33.in_ref = bf16[16,32,128]{2,1,0:T(8,128)(2,1)S(1)} all-to-all(bf16[16,32,128]{2,1,0:T(8,128)(2,1)S(1)} %shard_map.116), channel_id=1, replica_groups=mesh['yl'=2,'z'=16,'c'=2,'x'=4,'yh'=2] {'z'}, dimensions={0} | all-to-all | bytes 262144 | tf_op jit(solution)/shard_map/all_to_all | solution.py:311
  111.8 0.0 copy-start
  111.8 0.2 shard_map.117
  112.0 15.6 %all_to_all.34.in_ref = bf16[32,32,128]{2,1,0:T(8,128)(2,1)S(1)} all-to-all(bf16[32,32,128]{2,1,0:T(8,128)(2,1)S(1)} %shard_map.117), channel_id=1, replica_groups=mesh['yl'=2,'z'=16,'c'=2,'x'=4,'yh'=2] {'yl','c','x','yh'}, dimensions={0} | all-to-all | bytes 524288 | tf_op jit(solution)/shard_map/all_to_all | solution.py:313
  127.6 0.0 copy-done
  127.6 1.3 shard_map.118
  (1 shorter events, 0.0 us)
Async XLA Ops:
  1.6 17.3 %copy-start.1 = (bf16[1,128,1792]{2,1,0:T(8,128)(2,1)S(1)}, bf16[1,128,1792]{2,1,0:T(8,128)(2,1)}, u32[]{:S(2)}) copy-start(bf16[1,128,1792]{2,1,0:T(8,128)(2,1)} %param.12) | copy-start | bytes 1376260
  1.6 45.1 %all-to-all-start = ((bf16[32,8,896]{2,1,0:T(8,128)(2,1)}), bf16[32,8,896]{2,1,0:T(8,128)(2,1)S(1)}, u32[]{:S(2)}, u32[]{:S(2)}) async-start(bf16[32,8,896]{2,1,0:T(8,128)(2,1)} %shard_map.111), calls=%async_computation | async-start | bytes 917504 | tf_op jit(solution)/shard_map/all_to_all | solution.py:267
  18.8 0.7 copy-start.5
  18.9 0.7 copy-start.4
  20.1 9.5 %collective-permute-start = (bf16[144,896]{1,0:T(8,128)(2,1)S(1)}, bf16[144,896]{1,0:T(8,128)(2,1)S(1)}, u32[]{:S(2)}, u32[]{:S(2)}) collective-permute-start(bf16[144,896]{1,0:T(8,128)(2,1)S(1)} %get-tuple-element.17), channel_id=1, source_target_pairs={{0,256},{256,0},{1,257},{257,1},{2,258},{258,2},{3,259},{259,3},{4... | collective-permute-start | bytes 774152 | tf_op jit(solution)/shard_map/ppermute | solution.py:279
  23.3 13.3 %collective-permute-start.1 = (bf16[144,896]{1,0:T(8,128)(2,1)S(1)}, bf16[144,896]{1,0:T(8,128)(2,1)S(1)}, u32[]{:S(2)}, u32[]{:S(2)}) collective-permute-start(bf16[144,896]{1,0:T(8,128)(2,1)S(1)} %get-tuple-element.16.refs_0_), channel_id=1, source_target_pairs={{0,8},{8,0},{1,9},{9,1},{2,10},{10,2},{3,11},{11,3},{4,12},{12,4},... | collective-permute-start | bytes 774152 | tf_op jit(solution)/shard_map/ppermute | solution.py:280
  29.6 7.0 %collective-permute-start.2 = (bf16[144,896]{1,0:T(8,128)(2,1)S(1)}, bf16[144,896]{1,0:T(8,128)(2,1)S(1)}, u32[]{:S(2)}, u32[]{:S(2)}) collective-permute-start(bf16[144,896]{1,0:T(8,128)(2,1)S(1)} %collective-permute-done.refs_1_), channel_id=1, source_target_pairs={{0,8},{8,0},{1,9},{9,1},{2,10},{10,2},{3,11},{11,3},{4,12},{12,4},... | collective-permute-start | bytes 774152 | tf_op jit(solution)/shard_map/ppermute | solution.py:281
  34.3 0.7 copy-start.6
  34.3 0.7 copy-start.7
  81.8 13.2 %copy-start.2 = (bf16[1,128,128]{2,1,0:T(8,128)(2,1)S(1)}, bf16[1,128,128]{2,1,0:T(8,128)(2,1)}, u32[]{:S(2)}) copy-start(bf16[1,128,128]{2,1,0:T(8,128)(2,1)} %param.16) | copy-start | bytes 98308
  81.8 13.2 %copy-start.3 = (bf16[1,40,128]{2,1,0:T(8,128)(2,1)S(1)}, bf16[1,40,128]{2,1,0:T(8,128)(2,1)}, u32[]{:S(2)}) copy-start(bf16[1,40,128]{2,1,0:T(8,128)(2,1)} %param.15) | copy-start | bytes 30724
  111.8 15.8 %copy-start = (bf16[1,2048,128]{2,1,0:T(8,128)(2,1)S(1)}, bf16[1,2048,128]{2,1,0:T(8,128)(2,1)}, u32[]{:S(2)}) copy-start(bf16[1,2048,128]{2,1,0:T(8,128)(2,1)} %param.19) | copy-start | bytes 1572868

commit v9 on v8

--- a/solution.py
+++ b/solution.py
@@ -33,25 +33,34 @@
 FOURIER = fourier_table(BLADES)
 
 
+SHIFT = ((0, 1, -1, 2, -2, 3, -3, 4), (8, -7, 7, -6, 6, -5, 5, -4))
+PACK = 48 + NB
+
+
+def halves(table, axis):
+    table = table.astype(np.float32)
+    high = table.astype(BF)
+    return np.stack([high, (table - high.astype(np.float32)).astype(BF)], axis=axis)
+
+
 def forward_table():
-    table = FOURIER.reshape(YL, Z, C, YL, Z, C).transpose(1, 0, 2, 4, 3, 5)
-    table = np.einsum("zij,tu->zitju", table.reshape(Z, 4, BLADES), np.eye(TS))
-    table = table.reshape(Z, 4 * TS, BLADES * TS).astype(np.float32)
-    high = table.astype(BF)
-    return np.stack([high, (table - high.astype(np.float32)).astype(BF)], axis=1)
+    table = FOURIER.reshape(BLADES, YL, Z, C).transpose(0, 2, 1, 3).reshape(BLADES, BLADES)
+    table = np.einsum("ij,tu->itju", table, np.eye(TS))
+    return halves(table.reshape(BLADES * TS, BLADES * TS), 0)
+
+
+def inverse_table():
+    table = FOURIER.reshape(YL, Z, C, YL, Z, C)
+    rows = []
+    for z in range(Z):
+        source = (z + np.array(SHIFT).T) % Z
+        part = table[:, source][..., z, :]
+        rows.append(part.transpose(4, 5, 0, 3, 1, 2).reshape(4, BLADES))
+    table = np.einsum("zij,tu->zitju", np.stack(rows), np.eye(TS))
+    return halves(table.reshape(Z, 4 * TS, BLADES * TS), 1)
 
 
 FORWARD = forward_table()
-
-
-def inverse_table():
-    table = FOURIER.reshape(YL, Z, C, YL, Z, C).transpose(0, 2, 4, 3, 5, 1)
-    table = np.einsum("dij,tu->ditju", table.reshape(BLADES, 4, Z), np.eye(TS))
-    table = table.reshape(BLADES, 4 * TS, Z * TS).astype(np.float32)
-    high = table.astype(BF)
-    return np.stack([high, (table - high.astype(np.float32)).astype(BF)], axis=1)
-
-
 INVERSE = inverse_table()
 
 
@@ -113,7 +122,7 @@
     out_ref[...] = jnp.concatenate(picks, axis=1).astype(BF)
 
 
-def gather_sum_kernel(in_ref, out_ref):
+def gather_sum_kernel(in_ref, kept_ref, out_ref):
     sums = {}
     for yl in range(YL):
         for c in range(C):
@@ -136,31 +145,61 @@
     out_ref[...] = jnp.broadcast_to(block[None], out_ref.shape)
 
 
-def forward_kernel(table_ref, in_ref, out_ref):
+def fourier_sum(table_ref, in_ref):
     block = in_ref[...].reshape(BLADES * TS, NB)
-    block = sum(jnp.dot(table_ref[k], block, preferred_element_type=F32) for k in range(2))
-    for h in range(4):
-        part = block[h * TS : (h + 1) * TS].astype(BF)
-        out_ref[h * D : (h + 1) * D] = jnp.broadcast_to(part[None], (D, TS, NB))
-
-
-def powers_kernel(omega_ref, zeta_ref, out_ref):
-    omega, zeta = omega_ref[...], zeta_ref[...]
+    return sum(jnp.dot(table_ref[k], block, preferred_element_type=F32) for k in range(2))
+
+
+def forward_kernel(pos, table_ref, in_ref, shapes_ref, out_ref, hold_ref):
+    hold_ref[...] = fourier_sum(table_ref, in_ref).reshape(BLADES, TS, NB)
+    for yl in range(YL):
+        for c in range(C):
+            for d in range(D):
+                parts = [
+                    hold_ref[yl * Z * C + ((pos[2] + SHIFT[e][d] + Z) & (Z - 1)) * C + c]
+                    for e in range(2)
+                ]
+                out_ref[(yl * C + c) * D + d] = jnp.concatenate(parts, axis=0).astype(BF)
+
+
+def parameter_kernel(shapes_ref, flex_ref, omega_ref, zeta_ref, out_ref):
+    rows = []
+    for ref in (omega_ref, zeta_ref):
+        value = ref[...]
+        high = value.astype(BF).astype(F32)
+        middle = (value - high).astype(BF).astype(F32)
+        rows += [high, middle, value - high - middle]
+    rows = jnp.concatenate(rows + [jnp.zeros((2, MODES), F32)], axis=0)
+    rows = jnp.concatenate([rows, jnp.zeros((8, NB - MODES), F32)], axis=1)
+    out_ref[...] = jnp.concatenate(
+        [shapes_ref[...].astype(F32), rows, flex_ref[...].astype(F32)], axis=0
+    ).astype(BF)
+
+
+def prepare_kernel(first_ref, second_ref, shapes_ref, powers_ref):
+    packs = [ref[0:48].astype(F32) for ref in (first_ref, second_ref)]
+    none = jnp.zeros((64, NB), F32)
+    rest = jnp.zeros((64 - MODES, NB), F32)
+    shapes_ref[0] = jnp.concatenate([packs[0][0:MODES], rest, none], axis=0).astype(BF)
+    shapes_ref[1] = jnp.concatenate([none, packs[1][0:MODES], rest], axis=0).astype(BF)
+    damp = []
+    for row in (MODES, MODES + 3):
+        parts = [p[row : row + 1] + p[row + 1 : row + 2] + p[row + 2 : row + 3] for p in packs]
+        damp.append(jnp.concatenate([p[:, 0:64] for p in parts], axis=1))
+    omega, zeta = damp
     size = jnp.exp(-omega * zeta)
     angle = omega * jnp.sqrt(1.0 - zeta * zeta)
     real, imag = size * jnp.cos(angle), size * jnp.sin(angle)
-    out_ref[...] = jnp.zeros_like(out_ref)
     for k in range(8):
-        out_ref[2 * k : 2 * k + 1, 0:MODES] = real
-        out_ref[2 * k + 1 : 2 * k + 2, 0:MODES] = imag
+        powers_ref[2 * k : 2 * k + 1] = real
+        powers_ref[2 * k + 1 : 2 * k + 2] = imag
         real, imag = real * real - imag * imag, 2.0 * real * imag
 
 
-def modal_kernel(pos, in_ref, shapes_ref, flex_ref, powers_ref, out_ref, hold_ref):
-    shapes = jnp.concatenate(
-        [shapes_ref[...].astype(F32), jnp.zeros((NB - MODES, NB), F32)], axis=0
-    ).astype(BF)
-    real = dot_nt(in_ref[...].reshape(NT, NB), shapes)
+def modal_kernel(in_ref, first_ref, second_ref, shapes_ref, powers_ref, out_ref):
+    block = in_ref[...].astype(F32)
+    force = [block[:, e * TS : (e + 1) * TS].reshape(NT, NB).astype(BF) for e in range(2)]
+    real = dot_nt(force[0], shapes_ref[0]) + dot_nt(force[1], shapes_ref[1])
     imag = jnp.zeros_like(real)
     row = lax.broadcasted_iota(jnp.int32, (NT, NB), 0)
     for k in range(8):
@@ -177,41 +216,31 @@
             sr, si = real[: NT - s], imag[: NT - s]
             real = jnp.concatenate([real[:s], real[s:] + (pr * sr - pi * si)], axis=0)
             imag = jnp.concatenate([imag[:s], imag[s:] + (pr * si + pi * sr)], axis=0)
-    hold_ref[...] = imag
-    own = hold_ref[pl.ds(pl.multiple_of(pos[2] * TD, TD), TD), :]
-    high = own.astype(BF)
-    low = (own - high.astype(F32)).astype(BF)
-    rows = in_ref[pl.ds(pos[2] * (TD // TS), TD // TS)].reshape(TD, NB)
-    total = (
-        jnp.dot(high, shapes, preferred_element_type=F32)
-        + jnp.dot(low, shapes, preferred_element_type=F32)
-        + dot_nt(rows, flex_ref[...])
-    )
-    out_ref[...] = jnp.broadcast_to(total.astype(BF)[None], out_ref.shape)
+    high = imag.astype(BF)
+    low = (imag - high.astype(F32)).astype(BF)
+    parts = []
+    for e, ref in enumerate((first_ref, second_ref)):
+        total = (
+            jnp.dot(high, shapes_ref[e], preferred_element_type=F32)
+            + jnp.dot(low, shapes_ref[e], preferred_element_type=F32)
+            + dot_nt(force[e], ref[48:PACK])
+        )
+        parts.append(total.reshape(PEERS, TS, NB))
+    out_ref[...] = jnp.concatenate(parts, axis=1).astype(BF)
 
 
 def inverse_kernel(table_ref, in_ref, out_ref):
-    block = in_ref[...].astype(F32)
-    parts = []
-    for g in range(TD // TS):
-        part = block[:, g * TS : (g + 1) * TS].reshape(Z * TS, NB).astype(BF)
-        parts.append(
-            sum(jnp.dot(table_ref[k], part, preferred_element_type=F32) for k in range(2))
-        )
+    block = fourier_sum(table_ref, in_ref).astype(BF)
     for s in range(4):
-        part = jnp.concatenate([p[s * TS : (s + 1) * TS] for p in parts], axis=0).astype(BF)
-        out_ref[s * D : (s + 1) * D] = jnp.broadcast_to(part[None], (D, TD, NB))
+        part = block[s * TS : (s + 1) * TS]
+        out_ref[s * D : (s + 1) * D] = jnp.broadcast_to(part[None], (D, TS, NB))
 
 
 CHUNKS = 8
 
 
 def stress_kernel(in_ref, map_ref, out_ref, hold_ref, sems):
-    total = None
-    for q in range(YL * C):
-        part = in_ref[q * D : (q + 1) * D].astype(F32)
-        total = part if total is None else total + part
-    motion = total.reshape(NT, NB).astype(BF)
+    motion = in_ref[...].reshape(NT, NB)
     step = map_ref.shape[0] // CHUNKS
     copies = []
     for k in range(CHUNKS):
@@ -228,8 +257,8 @@
 HBM = pl.BlockSpec(memory_space=pl.ANY)
 
 
-def call(kernel, outs, specs, *args, out_specs=None, scratch=(), dtype=BF, vmem=24):
-    outs = [jax.ShapeDtypeStruct(shape, dtype) for shape in outs]
+def call(kernel, outs, specs, *args, out_specs=None, scratch=(), dtypes=(BF, BF), vmem=24):
+    outs = [jax.ShapeDtypeStruct(shape, dtype) for shape, dtype in zip(outs, dtypes)]
     got = pl.pallas_call(
         kernel,
         out_shape=outs,
@@ -243,13 +272,13 @@
 
 def local(wake, basis, block_index, phase_index, shapes, flex, omega, zeta, stress_map):
     yl, z, c = lax.axis_index("yl"), lax.axis_index("z"), lax.axis_index("c")
-    d = lax.axis_index("x") * 2 + lax.axis_index("yh")
-    pos = jnp.stack([yl, c, d]).astype(jnp.int32)
-    forward = lax.dynamic_slice(jnp.asarray(FORWARD), (z, 0, 0, 0), (1,) + FORWARD.shape[1:])[0]
-    inverse = lax.dynamic_slice(
-        jnp.asarray(INVERSE), ((yl * C + c) * Z + z, 0, 0, 0), (1,) + INVERSE.shape[1:]
-    )[0]
-    powers = call(powers_kernel, [(16, NB)], [VMEM] * 2, omega, zeta, dtype=F32)
+    pos = jnp.stack([yl, c, z]).astype(jnp.int32)
+    inverse = lax.dynamic_slice(jnp.asarray(INVERSE), (z, 0, 0, 0), (1,) + INVERSE.shape[1:])[0]
+    pack = call(parameter_kernel, [(PACK, NB)], [VMEM] * 4, shapes[0], flex[0], omega, zeta)
+    route = [
+        [(i * D + k, (i - SHIFT[e][k]) % Z * D + k) for i in range(Z) for k in range(D)]
+        for e in range(2)
+    ]
 
     spread = call(
         spread_kernel,
@@ -279,7 +308,7 @@
     by_yl = lax.ppermute(far, "yl", swap)
     by_c = lax.ppermute(near, "c", swap)
     by_both = lax.ppermute(by_yl, "c", swap)
-    near, forward, inverse, powers = lax.optimization_barrier((near, forward, inverse, powers))
+    near, inverse, pack = lax.optimization_barrier((near, inverse, pack))
 
     joined, onehot = call(
         select_kernel,
@@ -292,24 +321,40 @@
         by_both,
     )
     picked = call(project_kernel, [(PEERS, 4 * TS, NB)], [VMEM] * 3, blocks, joined, onehot)
+    column = ("z", "x", "yh")
+    pack, picked = lax.optimization_barrier((pack, picked))
+    first = lax.ppermute(pack, column, route[0])
     parts = lax.all_to_all(picked, PLANE, 0, 0, tiled=True)
-    forcing = call(gather_sum_kernel, [(Z, 4 * TS, NB)], [VMEM], parts)
+    forcing = call(gather_sum_kernel, [(Z, 4 * TS, NB)], [VMEM, HBM], parts, first)
+    pack, forcing = lax.optimization_barrier((pack, forcing))
+    second = lax.ppermute(pack, column, route[1])
+    spreads, powers = call(
+        prepare_kernel, [(2, NB, NB), (16, NB)], [VMEM] * 2, first, second, dtypes=(BF, F32)
+    )
     forcing = lax.all_to_all(forcing, "z", 0, 0, tiled=True)
-    harmonic = call(forward_kernel, [(PEERS, TS, NB)], [VMEM, VMEM], forward, forcing)
+    harmonic = call(
+        forward_kernel,
+        [(PEERS, 2 * TS, NB)],
+        [SMEM, VMEM, VMEM, HBM],
+        pos,
+        jnp.asarray(FORWARD),
+        forcing,
+        spreads,
+        scratch=[pltpu.VMEM((BLADES, TS, NB), F32)],
+    )
     harmonic = lax.all_to_all(harmonic, PLANE, 0, 0, tiled=True)
     physical = call(
         modal_kernel,
-        [(Z, TD, NB)],
-        [SMEM] + [VMEM] * 4,
-        pos,
+        [(PEERS, 2 * TS, NB)],
+        [VMEM] * 5,
         harmonic,
-        shapes[0],
-        flex[0],
+        first,
+        second,
+        spreads,
         powers,
-        scratch=[pltpu.VMEM((NT, NB), F32)],
-    )
-    physical = lax.all_to_all(physical, "z", 0, 0, tiled=True)
-    sectoral = call(inverse_kernel, [(PEERS, TD, NB)], [VMEM] * 2, inverse, physical)
+    )
+    physical = lax.all_to_all(physical, PLANE, 0, 0, tiled=True)
+    sectoral = call(inverse_kernel, [(PEERS, TS, NB)], [VMEM] * 2, inverse, physical)
     sectoral = lax.all_to_all(sectoral, PLANE, 0, 0, tiled=True)
     rows = stress_map.shape[1]
     stress = call(

time: 130 us -> 130 us (level)
  blocking collectives: 78.7 us -> 36 us
  starting transfers between devices: 28.4 us -> 54 us
  waiting for transfers between devices: 12 us -> 28.7 us
  Pallas kernels: 6.61 us -> 8.42 us
    all_to_all x3 -> x1, blocking collectives: 49.9 us -> 11.4 us  [local(): physical = lax.all_to_all(physical, PLANE, 0, 0, tiled=True)]
    all_to_all x0 -> x2, starting transfers between devices: none -> 13 us  [the longest x1 8.61 us: local(): parts = lax.all_to_all(picked, PLANE, 0, 0, tiled=True)]
    ppermute x0 -> x2, starting transfers between devices: none -> 12.6 us  [the longest x1 12 us: local(): second = lax.ppermute(pack, column, route[1])]
    all_to_all x0 -> x2, waiting for transfers between devices: none -> 8.46 us  [the longest x1 8.46 us: local(): parts = lax.all_to_all(picked, PLANE, 0, 0, tiled=True)]
    ppermute x0 -> x2, waiting for transfers between devices: none -> 7.39 us  [the longest x1 7.39 us: local(): second = lax.ppermute(pack, column, route[1])]
    all_to_all x1, blocking collectives: 15.6 us -> 10.9 us  [local(): sectoral = lax.all_to_all(sectoral, PLANE, 0, 0, tiled=True)]
    pallas_call x10 -> x11, Pallas kernels: 6.61 us -> 8.42 us  [call(): pl.pallas_call(kernel, out_shape=outs, in_specs=specs, out_specs=out_spec...]
  transfers between devices with their start and end apart: 4 -> 8, of which waited for: 2 -> 4; matrix products, arithmetic and copies ran while one was open for 1% -> 1% of each run, Pallas kernels for 1% -> 1%
where the time goes in v9:
time: 130 us
  starting transfers between devices  54 us (42%)
  blocking collectives  36 us (28%)
  waiting for transfers between devices  28.7 us (22%)
  Pallas kernels  8.42 us (6%)
  local copies, waits for them, and re-layouts  2.19 us (2%)
    all_to_all x1, starting transfers between devices, local(): blocks = lax.all_to_all(spread, ('yl', 'z'), 0, 0, tiled=True)  17.2 us
    all_to_all x1, blocking collectives, local(): harmonic = lax.all_to_all(harmonic, PLANE, 0, 0, tiled=True)  13.7 us
    ppermute x1, starting transfers between devices, local(): second = lax.ppermute(pack, column, route[1])  12 us
    all_to_all x1, blocking collectives, local(): physical = lax.all_to_all(physical, PLANE, 0, 0, tiled=True)  11.4 us
    all_to_all x1, blocking collectives, local(): sectoral = lax.all_to_all(sectoral, PLANE, 0, 0, tiled=True)  10.9 us
    all_to_all x1, waiting for transfers between devices, local(): blocks = lax.all_to_all(spread, ('yl', 'z'), 0, 0, tiled=True)  9.9 us
    all_to_all x1, starting transfers between devices, local(): parts = lax.all_to_all(picked, PLANE, 0, 0, tiled=True)  8.61 us
    all_to_all x1, waiting for transfers between devices, local(): parts = lax.all_to_all(picked, PLANE, 0, 0, tiled=True)  8.46 us
  transfers between devices with their start and end apart: 8, of which 4 were waited for; matrix products, arithmetic and copies ran while one was open for 1% of the time, Pallas kernels for 1%

profile of v9, /device:TPU:1, one launch (start us, length us, event | category | flops | bytes accessed | tf_op | source)
XLA Modules:
  0.0 129.6 jit_solution(1715869834287523387)
XLA Ops:
  0.0 1.6 %shard_map.111 = bf16[32,8,896]{2,1,0:T(8,128)(2,1)} custom-call(bf16[8,1792]{1,0:T(8,128)(2,1)} %bitcast.15), custom_call_target="tpu_custom_call" | custom-call | tf_op jit(solution)/shard_map/pallas_call | solution.py:262
  1.6 0.0 copy-start.2
  1.6 17.2 %all-to-all-start = ((bf16[32,8,896]{2,1,0:T(8,128)(2,1)}), bf16[32,8,896]{2,1,0:T(8,128)(2,1)S(1)}, u32[]{:S(2)}, u32[]{:S(2)}) async-start(bf16[32,8,896]{2,1,0:T(8,128)(2,1)} %shard_map.111), calls=%async_computation | async-start | bytes 917504 | tf_op jit(solution)/shard_map/all_to_all | solution.py:296
  18.8 0.0 copy-start.6
  18.8 0.1 pad_add_fusion.pos
  18.9 0.0 copy-start.5
  18.9 0.0 copy-done.2
  18.9 0.6 copy-done.6
  19.5 0.1 copy-done.5
  19.5 0.0 copy-start.3
  19.5 0.6 shard_map.109
  20.1 0.0 copy-start.4
  20.1 3.1 %collective-permute-start = (bf16[144,896]{1,0:T(8,128)(2,1)S(1)}, bf16[144,896]{1,0:T(8,128)(2,1)S(1)}, u32[]{:S(2)}, u32[]{:S(2)}) collective-permute-start(bf16[144,896]{1,0:T(8,128)(2,1)S(1)} %get-tuple-element.22), channel_id=1, source_target_pairs={{0,256},{256,0},{1,257},{257,1},{2,258},{258,2},{3,259},{259,3},{4... | collective-permute-start | bytes 774152 | tf_op jit(solution)/shard_map/ppermute | solution.py:308
  23.3 3.4 %collective-permute-start.1 = (bf16[144,896]{1,0:T(8,128)(2,1)S(1)}, bf16[144,896]{1,0:T(8,128)(2,1)S(1)}, u32[]{:S(2)}, u32[]{:S(2)}) collective-permute-start(bf16[144,896]{1,0:T(8,128)(2,1)S(1)} %get-tuple-element.21.refs_0_), channel_id=1, source_target_pairs={{0,8},{8,0},{1,9},{9,1},{2,10},{10,2},{3,11},{11,3},{4,12},{12,4},... | collective-permute-start | bytes 774152 | tf_op jit(solution)/shard_map/ppermute | solution.py:309
  26.7 2.9 %collective-permute-done.refs_1_ = bf16[144,896]{1,0:T(8,128)(2,1)S(1)} collective-permute-done((bf16[144,896]{1,0:T(8,128)(2,1)S(1)}, bf16[144,896]{1,0:T(8,128)(2,1)S(1)}, u32[]{:S(2)}, u32[]{:S(2)}) %collective-permute-start) | collective-permute-done | bytes 258080 | tf_op jit(solution)/shard_map/ppermute | solution.py:308
  29.7 4.6 %collective-permute-start.2 = (bf16[144,896]{1,0:T(8,128)(2,1)S(1)}, bf16[144,896]{1,0:T(8,128)(2,1)S(1)}, u32[]{:S(2)}, u32[]{:S(2)}) collective-permute-start(bf16[144,896]{1,0:T(8,128)(2,1)S(1)} %collective-permute-done.refs_1_), channel_id=1, source_target_pairs={{0,8},{8,0},{1,9},{9,1},{2,10},{10,2},{3,11},{11,3},{4,12},{12,4},... | collective-permute-start | bytes 774152 | tf_op jit(solution)/shard_map/ppermute | solution.py:310
  34.3 0.0 copy-start.7
  34.3 0.0 copy-start.8
  34.3 0.0 copy-done.3
  34.3 0.0 copy-done.4
  34.3 0.6 copy-done.7
  34.9 0.0 copy-done.8
  35.0 0.9 dynamic-slice_bitcast_fusion.table_ref
  35.8 0.0 collective-permute-done.1.refs_2_
  35.8 0.0 collective-permute-done.2.refs_3_
  35.8 0.9 shard_map.112
  36.8 9.9 %all-to-all-done.wake_ref = bf16[32,8,896]{2,1,0:T(8,128)(2,1)S(1)} async-done(((bf16[32,8,896]{2,1,0:T(8,128)(2,1)}), bf16[32,8,896]{2,1,0:T(8,128)(2,1)S(1)}, u32[]{:S(2)}, u32[]{:S(2)}) %all-to-all-start) | async-done | bytes 458784 | tf_op jit(solution)/shard_map/all_to_all | solution.py:296
  46.7 1.5 %shard_map.113 = bf16[32,32,128]{2,1,0:T(8,128)(2,1)} custom-call(bf16[32,8,896]{2,1,0:T(8,128)(2,1)S(1)} %all-to-all-done.wake_ref, bf16[512,896]{1,0:T(8,128)(2,1)S(1)} %get-tuple-element.23.basis_ref, bf16[4,256,256]{2,1,0:T(8,128)(2,1)S(1)} %get-tuple-element.24.onehot_ref), custom_call_target="tpu_custom_call" | custom-call | tf_op jit(solution)/shard_map/pallas_call | solution.py:262
  48.1 0.0 copy-start
  48.1 8.6 %all-to-all-start.1 = ((bf16[32,32,128]{2,1,0:T(8,128)(2,1)}), bf16[32,32,128]{2,1,0:T(8,128)(2,1)S(1)}, u32[]{:S(2)}, u32[]{:S(2)}) async-start(bf16[32,32,128]{2,1,0:T(8,128)(2,1)} %shard_map.113), calls=%async_computation.1 | async-start | bytes 524288 | tf_op jit(solution)/shard_map/all_to_all | solution.py:327
  56.7 0.7 collective-permute-start.3
  57.4 0.0 collective-permute-done.3.kept_ref.first_ref
  57.4 8.5 %all-to-all-done.1.in_ref = bf16[32,32,128]{2,1,0:T(8,128)(2,1)S(1)} async-done(((bf16[32,32,128]{2,1,0:T(8,128)(2,1)}), bf16[32,32,128]{2,1,0:T(8,128)(2,1)S(1)}, u32[]{:S(2)}, u32[]{:S(2)}) %all-to-all-start.1) | async-done | bytes 262176 | tf_op jit(solution)/shard_map/all_to_all | solution.py:327
  65.9 0.7 shard_map.114
  66.6 4.4 %all-to-all-start.2 = ((bf16[16,32,128]{2,1,0:T(8,128)(2,1)}), bf16[16,32,128]{2,1,0:T(8,128)(2,1)S(1)}, u32[]{:S(2)}, u32[]{:S(2)}) async-start(bf16[16,32,128]{2,1,0:T(8,128)(2,1)} %shard_map.114), calls=%async_computation.2 | async-start | bytes 262144 | tf_op jit(solution)/shard_map/all_to_all | solution.py:334
  71.0 12.0 %collective-permute-start.4 = (bf16[176,128]{1,0:T(8,128)(2,1)S(1)}, bf16[176,128]{1,0:T(8,128)(2,1)S(1)}, u32[]{:S(2)}, u32[]{:S(2)}) collective-permute-start(bf16[176,128]{1,0:T(8,128)(2,1)S(1)} %shard_map.110), channel_id=1, source_target_pairs={{0,128},{1,113},{2,146},{3,99},{4,164},{5,85},{6,182},{7,71},{16,1... | collective-permute-start | bytes 135176 | tf_op jit(solution)/shard_map/ppermute | solution.py:330
  83.0 7.4 %collective-permute-done.4.second_ref = bf16[176,128]{1,0:T(8,128)(2,1)S(1)} collective-permute-done((bf16[176,128]{1,0:T(8,128)(2,1)S(1)}, bf16[176,128]{1,0:T(8,128)(2,1)S(1)}, u32[]{:S(2)}, u32[]{:S(2)}) %collective-permute-start.4) | collective-permute-done | bytes 45088 | tf_op jit(solution)/shard_map/ppermute | solution.py:330
  90.4 0.1 shard_map.115
  90.5 0.0 all-to-all-done.2.in_ref
  90.5 0.0 copy-done
  90.5 1.0 shard_map.116
  91.5 13.7 %all_to_all.30.in_ref = bf16[32,16,128]{2,1,0:T(8,128)(2,1)S(1)} all-to-all(bf16[32,16,128]{2,1,0:T(8,128)(2,1)S(1)} %shard_map.116), channel_id=1, replica_groups=mesh['yl'=2,'z'=16,'c'=2,'x'=4,'yh'=2] {'yl','c','x','yh'}, dimensions={0} | all-to-all | bytes 262144 | tf_op jit(solution)/shard_map/all_to_all | solution.py:345
  105.2 0.0 copy-start.1
  105.2 0.6 shard_map.117
  105.9 11.4 %all_to_all.31.in_ref = bf16[32,16,128]{2,1,0:T(8,128)(2,1)S(1)} all-to-all(bf16[32,16,128]{2,1,0:T(8,128)(2,1)S(1)} %shard_map.117), channel_id=1, replica_groups=mesh['yl'=2,'z'=16,'c'=2,'x'=4,'yh'=2] {'yl','c','x','yh'}, dimensions={0} | all-to-all | bytes 262144 | tf_op jit(solution)/shard_map/all_to_all | solution.py:356
  117.3 0.2 shard_map.118
  117.4 10.9 %all_to_all.32.in_ref = bf16[32,8,128]{2,1,0:T(8,128)(2,1)S(1)} all-to-all(bf16[32,8,128]{2,1,0:T(8,128)(2,1)S(1)} %shard_map.118), channel_id=1, replica_groups=mesh['yl'=2,'z'=16,'c'=2,'x'=4,'yh'=2] {'yl','c','x','yh'}, dimensions={0} | all-to-all | bytes 131072 | tf_op jit(solution)/shard_map/all_to_all | solution.py:358
  128.4 0.0 copy-done.1
  128.4 1.3 shard_map.119
  (1 shorter events, 0.0 us)
Async XLA Ops:
  1.6 17.3 %copy-start.2 = (bf16[1,128,1792]{2,1,0:T(8,128)(2,1)S(1)}, bf16[1,128,1792]{2,1,0:T(8,128)(2,1)}, u32[]{:S(2)}) copy-start(bf16[1,128,1792]{2,1,0:T(8,128)(2,1)} %param.12) | copy-start | bytes 1376260
  1.6 45.1 %all-to-all-start = ((bf16[32,8,896]{2,1,0:T(8,128)(2,1)}), bf16[32,8,896]{2,1,0:T(8,128)(2,1)S(1)}, u32[]{:S(2)}, u32[]{:S(2)}) async-start(bf16[32,8,896]{2,1,0:T(8,128)(2,1)} %shard_map.111), calls=%async_computation | async-start | bytes 917504 | tf_op jit(solution)/shard_map/all_to_all | solution.py:296
  18.8 0.7 copy-start.6
  18.9 0.7 copy-start.5
  19.5 14.8 %copy-start.3 = (bf16[1,128,128]{2,1,0:T(8,128)(2,1)S(1)}, bf16[1,128,128]{2,1,0:T(8,128)(2,1)}, u32[]{:S(2)}) copy-start(bf16[1,128,128]{2,1,0:T(8,128)(2,1)} %param.16) | copy-start | bytes 98308
  20.1 14.2 %copy-start.4 = (bf16[1,40,128]{2,1,0:T(8,128)(2,1)S(1)}, bf16[1,40,128]{2,1,0:T(8,128)(2,1)}, u32[]{:S(2)}) copy-start(bf16[1,40,128]{2,1,0:T(8,128)(2,1)} %param.15) | copy-start | bytes 30724
  20.1 9.5 %collective-permute-start = (bf16[144,896]{1,0:T(8,128)(2,1)S(1)}, bf16[144,896]{1,0:T(8,128)(2,1)S(1)}, u32[]{:S(2)}, u32[]{:S(2)}) collective-permute-start(bf16[144,896]{1,0:T(8,128)(2,1)S(1)} %get-tuple-element.22), channel_id=1, source_target_pairs={{0,256},{256,0},{1,257},{257,1},{2,258},{258,2},{3,259},{259,3},{4... | collective-permute-start | bytes 774152 | tf_op jit(solution)/shard_map/ppermute | solution.py:308
  23.3 12.5 %collective-permute-start.1 = (bf16[144,896]{1,0:T(8,128)(2,1)S(1)}, bf16[144,896]{1,0:T(8,128)(2,1)S(1)}, u32[]{:S(2)}, u32[]{:S(2)}) collective-permute-start(bf16[144,896]{1,0:T(8,128)(2,1)S(1)} %get-tuple-element.21.refs_0_), channel_id=1, source_target_pairs={{0,8},{8,0},{1,9},{9,1},{2,10},{10,2},{3,11},{11,3},{4,12},{12,4},... | collective-permute-start | bytes 774152 | tf_op jit(solution)/shard_map/ppermute | solution.py:309
  29.7 6.1 %collective-permute-start.2 = (bf16[144,896]{1,0:T(8,128)(2,1)S(1)}, bf16[144,896]{1,0:T(8,128)(2,1)S(1)}, u32[]{:S(2)}, u32[]{:S(2)}) collective-permute-start(bf16[144,896]{1,0:T(8,128)(2,1)S(1)} %collective-permute-done.refs_1_), channel_id=1, source_target_pairs={{0,8},{8,0},{1,9},{9,1},{2,10},{10,2},{3,11},{11,3},{4,12},{12,4},... | collective-permute-start | bytes 774152 | tf_op jit(solution)/shard_map/ppermute | solution.py:310
  34.3 0.7 copy-start.7
  34.3 0.7 copy-start.8
  48.1 42.4 %copy-start = (bf16[2,512,512]{2,1,0:T(8,128)(2,1)S(1)}, bf16[2,512,512]{2,1,0:T(8,128)(2,1)}, u32[]{:S(2)}) copy-start(bf16[2,512,512]{2,1,0:T(8,128)(2,1)} %constant.24.clone.table_ref) | copy-start | bytes 3145732
  48.1 17.8 %all-to-all-start.1 = ((bf16[32,32,128]{2,1,0:T(8,128)(2,1)}), bf16[32,32,128]{2,1,0:T(8,128)(2,1)S(1)}, u32[]{:S(2)}, u32[]{:S(2)}) async-start(bf16[32,32,128]{2,1,0:T(8,128)(2,1)} %shard_map.113), calls=%async_computation.1 | async-start | bytes 524288 | tf_op jit(solution)/shard_map/all_to_all | solution.py:327
  56.7 0.7 collective-permute-start.3
  66.6 23.9 %all-to-all-start.2 = ((bf16[16,32,128]{2,1,0:T(8,128)(2,1)}), bf16[16,32,128]{2,1,0:T(8,128)(2,1)S(1)}, u32[]{:S(2)}, u32[]{:S(2)}) async-start(bf16[16,32,128]{2,1,0:T(8,128)(2,1)} %shard_map.114), calls=%async_computation.2 | async-start | bytes 262144 | tf_op jit(solution)/shard_map/all_to_all | solution.py:334
  71.0 19.4 %collective-permute-start.4 = (bf16[176,128]{1,0:T(8,128)(2,1)S(1)}, bf16[176,128]{1,0:T(8,128)(2,1)S(1)}, u32[]{:S(2)}, u32[]{:S(2)}) collective-permute-start(bf16[176,128]{1,0:T(8,128)(2,1)S(1)} %shard_map.110), channel_id=1, source_target_pairs={{0,128},{1,113},{2,146},{3,99},{4,164},{5,85},{6,182},{7,71},{16,1... | collective-permute-start | bytes 135176 | tf_op jit(solution)/shard_map/ppermute | solution.py:330
  105.2 23.1 %copy-start.1 = (bf16[1,2048,128]{2,1,0:T(8,128)(2,1)S(1)}, bf16[1,2048,128]{2,1,0:T(8,128)(2,1)}, u32[]{:S(2)}) copy-start(bf16[1,2048,128]{2,1,0:T(8,128)(2,1)} %param.19) | copy-start | bytes 1572868

commit v10 on v9

--- a/solution.py
+++ b/solution.py
@@ -34,6 +34,7 @@
 
 
 SHIFT = ((0, 1, -1, 2, -2, 3, -3, 4), (8, -7, 7, -6, 6, -5, 5, -4))
+HOPS = (SHIFT[0], (4, -3, 3, -2, 2, -1, 1, 0), (4, -4, 4, -4, 4, -4, 4, -4))
 PACK = 48 + NB
 
 
@@ -122,7 +123,7 @@
     out_ref[...] = jnp.concatenate(picks, axis=1).astype(BF)
 
 
-def gather_sum_kernel(in_ref, kept_ref, out_ref):
+def gather_sum_kernel(in_ref, first_ref, middle_ref, out_ref):
     sums = {}
     for yl in range(YL):
         for c in range(C):
@@ -276,8 +277,8 @@
     inverse = lax.dynamic_slice(jnp.asarray(INVERSE), (z, 0, 0, 0), (1,) + INVERSE.shape[1:])[0]
     pack = call(parameter_kernel, [(PACK, NB)], [VMEM] * 4, shapes[0], flex[0], omega, zeta)
     route = [
-        [(i * D + k, (i - SHIFT[e][k]) % Z * D + k) for i in range(Z) for k in range(D)]
-        for e in range(2)
+        [(i * D + k, (i - hops[k]) % Z * D + k) for i in range(Z) for k in range(D)]
+        for hops in HOPS
     ]
 
     spread = call(
@@ -324,10 +325,11 @@
     column = ("z", "x", "yh")
     pack, picked = lax.optimization_barrier((pack, picked))
     first = lax.ppermute(pack, column, route[0])
+    middle = lax.ppermute(pack, column, route[1])
     parts = lax.all_to_all(picked, PLANE, 0, 0, tiled=True)
-    forcing = call(gather_sum_kernel, [(Z, 4 * TS, NB)], [VMEM, HBM], parts, first)
-    pack, forcing = lax.optimization_barrier((pack, forcing))
-    second = lax.ppermute(pack, column, route[1])
+    forcing = call(gather_sum_kernel, [(Z, 4 * TS, NB)], [VMEM, HBM, HBM], parts, first, middle)
+    middle, forcing = lax.optimization_barrier((middle, forcing))
+    second = lax.ppermute(middle, column, route[2])
     spreads, powers = call(
         prepare_kernel, [(2, NB, NB), (16, NB)], [VMEM] * 2, first, second, dtypes=(BF, F32)
     )

time: 130 us -> 132 us (1.015)
  blocking collectives: 36 us -> 41 us
  waiting for transfers between devices: 28.7 us -> 24.5 us
    all_to_all x1, waiting for transfers between devices: 8.46 us -> 0.34 us  [local(): parts = lax.all_to_all(picked, PLANE, 0, 0, tiled=True)]
    all_to_all x1, blocking collectives: 13.7 us -> 18.7 us  [local(): harmonic = lax.all_to_all(harmonic, PLANE, 0, 0, tiled=True)]
    ppermute x1 -> x2, waiting for transfers between devices: 7.39 us -> 11.3 us  [the longest x1 7.16 us: local(): second = lax.ppermute(middle, column, route[2])]
    all_to_all x1, starting transfers between devices: 4.39 us -> 6.31 us  [local(): forcing = lax.all_to_all(forcing, 'z', 0, 0, tiled=True)]
    ppermute x1 -> x2, starting transfers between devices: 12 us -> 11.2 us  [the longest x1 7.18 us: local(): second = lax.ppermute(middle, column, route[2])]
  transfers between devices with their start and end apart: 8 -> 9, of which waited for: 4 -> 5; matrix products, arithmetic and copies ran while one was open for 1% -> 1% of each run, Pallas kernels for 1% -> 1%
where the time goes in v10:
time: 132 us; the launch traced here: 131 us
  starting transfers between devices  55.1 us (42%)
  blocking collectives  41 us (31%)
  waiting for transfers between devices  24.5 us (19%)
  Pallas kernels  8.42 us (6%)
  local copies, waits for them, and re-layouts  2.19 us (2%)
    all_to_all x1, blocking collectives, local(): harmonic = lax.all_to_all(harmonic, PLANE, 0, 0, tiled=True)  18.7 us
    all_to_all x1, starting transfers between devices, local(): blocks = lax.all_to_all(spread, ('yl', 'z'), 0, 0, tiled=True)  17.2 us
    all_to_all x1, blocking collectives, local(): physical = lax.all_to_all(physical, PLANE, 0, 0, tiled=True)  11.4 us
    all_to_all x1, blocking collectives, local(): sectoral = lax.all_to_all(sectoral, PLANE, 0, 0, tiled=True)  10.9 us
    all_to_all x1, waiting for transfers between devices, local(): blocks = lax.all_to_all(spread, ('yl', 'z'), 0, 0, tiled=True)  9.9 us
    all_to_all x1, starting transfers between devices, local(): parts = lax.all_to_all(picked, PLANE, 0, 0, tiled=True)  8.61 us
    pallas_call x11, Pallas kernels, call(): pl.pallas_call(kernel, out_shape=outs, in_specs=specs, out_specs=out_spec...  8.42 us
    ppermute x1, starting transfers between devices, local(): second = lax.ppermute(middle, column, route[2])  7.18 us
  transfers between devices with their start and end apart: 9, of which 5 were waited for; matrix products, arithmetic and copies ran while one was open for 1% of the time, Pallas kernels for 1%

profile of v10, /device:TPU:1, one launch (start us, length us, event | category | flops | bytes accessed | tf_op | source)
XLA Modules:
  0.0 131.5 jit_solution(7730771700082579102)
XLA Ops:
  0.0 1.6 %shard_map.111 = bf16[32,8,896]{2,1,0:T(8,128)(2,1)} custom-call(bf16[8,1792]{1,0:T(8,128)(2,1)} %bitcast.15), custom_call_target="tpu_custom_call" | custom-call | tf_op jit(solution)/shard_map/pallas_call | solution.py:263
  1.6 0.0 copy-start.2
  1.6 17.2 %all-to-all-start = ((bf16[32,8,896]{2,1,0:T(8,128)(2,1)}), bf16[32,8,896]{2,1,0:T(8,128)(2,1)S(1)}, u32[]{:S(2)}, u32[]{:S(2)}) async-start(bf16[32,8,896]{2,1,0:T(8,128)(2,1)} %shard_map.111), calls=%async_computation | async-start | bytes 917504 | tf_op jit(solution)/shard_map/all_to_all | solution.py:297
  18.8 0.0 copy-start.6
  18.8 0.1 pad_add_fusion.pos
  18.9 0.0 copy-start.5
  18.9 0.0 copy-done.2
  18.9 0.6 copy-done.6
  19.5 0.1 copy-done.5
  19.5 0.0 copy-start.3
  19.5 0.6 shard_map.109
  20.1 0.0 copy-start.4
  20.1 3.1 %collective-permute-start = (bf16[144,896]{1,0:T(8,128)(2,1)S(1)}, bf16[144,896]{1,0:T(8,128)(2,1)S(1)}, u32[]{:S(2)}, u32[]{:S(2)}) collective-permute-start(bf16[144,896]{1,0:T(8,128)(2,1)S(1)} %get-tuple-element.22), channel_id=1, source_target_pairs={{0,256},{256,0},{1,257},{257,1},{2,258},{258,2},{3,259},{259,3},{4... | collective-permute-start | bytes 774152 | tf_op jit(solution)/shard_map/ppermute | solution.py:309
  23.3 3.4 %collective-permute-start.1 = (bf16[144,896]{1,0:T(8,128)(2,1)S(1)}, bf16[144,896]{1,0:T(8,128)(2,1)S(1)}, u32[]{:S(2)}, u32[]{:S(2)}) collective-permute-start(bf16[144,896]{1,0:T(8,128)(2,1)S(1)} %get-tuple-element.21.refs_0_), channel_id=1, source_target_pairs={{0,8},{8,0},{1,9},{9,1},{2,10},{10,2},{3,11},{11,3},{4,12},{12,4},... | collective-permute-start | bytes 774152 | tf_op jit(solution)/shard_map/ppermute | solution.py:310
  26.7 2.9 %collective-permute-done.refs_1_ = bf16[144,896]{1,0:T(8,128)(2,1)S(1)} collective-permute-done((bf16[144,896]{1,0:T(8,128)(2,1)S(1)}, bf16[144,896]{1,0:T(8,128)(2,1)S(1)}, u32[]{:S(2)}, u32[]{:S(2)}) %collective-permute-start) | collective-permute-done | bytes 258080 | tf_op jit(solution)/shard_map/ppermute | solution.py:309
  29.7 4.6 %collective-permute-start.2 = (bf16[144,896]{1,0:T(8,128)(2,1)S(1)}, bf16[144,896]{1,0:T(8,128)(2,1)S(1)}, u32[]{:S(2)}, u32[]{:S(2)}) collective-permute-start(bf16[144,896]{1,0:T(8,128)(2,1)S(1)} %collective-permute-done.refs_1_), channel_id=1, source_target_pairs={{0,8},{8,0},{1,9},{9,1},{2,10},{10,2},{3,11},{11,3},{4,12},{12,4},... | collective-permute-start | bytes 774152 | tf_op jit(solution)/shard_map/ppermute | solution.py:311
  34.3 0.0 copy-start.7
  34.3 0.0 copy-start.8
  34.3 0.0 copy-done.3
  34.3 0.0 copy-done.4
  34.3 0.6 copy-done.7
  34.9 0.0 copy-done.8
  35.0 0.9 dynamic-slice_bitcast_fusion.table_ref
  35.8 0.0 collective-permute-done.1.refs_2_
  35.8 0.0 collective-permute-done.2.refs_3_
  35.8 0.9 shard_map.112
  36.8 9.9 %all-to-all-done.wake_ref = bf16[32,8,896]{2,1,0:T(8,128)(2,1)S(1)} async-done(((bf16[32,8,896]{2,1,0:T(8,128)(2,1)}), bf16[32,8,896]{2,1,0:T(8,128)(2,1)S(1)}, u32[]{:S(2)}, u32[]{:S(2)}) %all-to-all-start) | async-done | bytes 458784 | tf_op jit(solution)/shard_map/all_to_all | solution.py:297
  46.7 1.5 %shard_map.113 = bf16[32,32,128]{2,1,0:T(8,128)(2,1)} custom-call(bf16[32,8,896]{2,1,0:T(8,128)(2,1)S(1)} %all-to-all-done.wake_ref, bf16[512,896]{1,0:T(8,128)(2,1)S(1)} %get-tuple-element.23.basis_ref, bf16[4,256,256]{2,1,0:T(8,128)(2,1)S(1)} %get-tuple-element.24.onehot_ref), custom_call_target="tpu_custom_call" | custom-call | tf_op jit(solution)/shard_map/pallas_call | solution.py:263
  48.1 0.0 copy-start
  48.1 8.6 %all-to-all-start.1 = ((bf16[32,32,128]{2,1,0:T(8,128)(2,1)}), bf16[32,32,128]{2,1,0:T(8,128)(2,1)S(1)}, u32[]{:S(2)}, u32[]{:S(2)}) async-start(bf16[32,32,128]{2,1,0:T(8,128)(2,1)} %shard_map.113), calls=%async_computation.1 | async-start | bytes 524288 | tf_op jit(solution)/shard_map/all_to_all | solution.py:329
  56.7 4.0 %collective-permute-start.3 = (bf16[176,128]{1,0:T(8,128)(2,1)S(1)}, bf16[176,128]{1,0:T(8,128)(2,1)S(1)}, u32[]{:S(2)}, u32[]{:S(2)}) collective-permute-start(bf16[176,128]{1,0:T(8,128)(2,1)S(1)} %shard_map.110), channel_id=1, source_target_pairs={{0,192},{1,49},{2,210},{3,35},{4,228},{5,21},{6,246},{7,7},{16,208... | collective-permute-start | bytes 135176 | tf_op jit(solution)/shard_map/ppermute | solution.py:328
  60.8 0.7 collective-permute-start.4
  61.5 4.1 %collective-permute-done.3.middle_ref = bf16[176,128]{1,0:T(8,128)(2,1)S(1)} collective-permute-done((bf16[176,128]{1,0:T(8,128)(2,1)S(1)}, bf16[176,128]{1,0:T(8,128)(2,1)S(1)}, u32[]{:S(2)}, u32[]{:S(2)}) %collective-permute-start.3) | collective-permute-done | bytes 45088 | tf_op jit(solution)/shard_map/ppermute | solution.py:328
  65.5 0.0 collective-permute-done.4.first_ref
  65.5 0.3 all-to-all-done.1.in_ref
  65.9 0.7 shard_map.114
  66.6 6.3 %all-to-all-start.2 = ((bf16[16,32,128]{2,1,0:T(8,128)(2,1)}), bf16[16,32,128]{2,1,0:T(8,128)(2,1)S(1)}, u32[]{:S(2)}, u32[]{:S(2)}) async-start(bf16[16,32,128]{2,1,0:T(8,128)(2,1)} %shard_map.114), calls=%async_computation.2 | async-start | bytes 262144 | tf_op jit(solution)/shard_map/all_to_all | solution.py:336
  72.9 7.2 %collective-permute-start.5 = (bf16[176,128]{1,0:T(8,128)(2,1)S(1)}, bf16[176,128]{1,0:T(8,128)(2,1)S(1)}, u32[]{:S(2)}, u32[]{:S(2)}) collective-permute-start(bf16[176,128]{1,0:T(8,128)(2,1)S(1)} %collective-permute-done.3.middle_ref), channel_id=1, source_target_pairs={{0,192},{1,65},{2,194},{3,67},{4,196},{5,69},{6,198},{7,71},{16,20... | collective-permute-start | bytes 135176 | tf_op jit(solution)/shard_map/ppermute | solution.py:332
  80.1 7.2 %collective-permute-done.5.second_ref = bf16[176,128]{1,0:T(8,128)(2,1)S(1)} collective-permute-done((bf16[176,128]{1,0:T(8,128)(2,1)S(1)}, bf16[176,128]{1,0:T(8,128)(2,1)S(1)}, u32[]{:S(2)}, u32[]{:S(2)}) %collective-permute-start.5) | collective-permute-done | bytes 45088 | tf_op jit(solution)/shard_map/ppermute | solution.py:332
  87.3 0.1 shard_map.115
  87.4 0.0 all-to-all-done.2.in_ref
  87.4 0.0 copy-done
  87.4 1.0 shard_map.116
  88.4 18.7 %all_to_all.30.in_ref = bf16[32,16,128]{2,1,0:T(8,128)(2,1)S(1)} all-to-all(bf16[32,16,128]{2,1,0:T(8,128)(2,1)S(1)} %shard_map.116), channel_id=1, replica_groups=mesh['yl'=2,'z'=16,'c'=2,'x'=4,'yh'=2] {'yl','c','x','yh'}, dimensions={0} | all-to-all | bytes 262144 | tf_op jit(solution)/shard_map/all_to_all | solution.py:347
  107.1 0.0 copy-start.1
  107.1 0.6 shard_map.117
  107.7 11.4 %all_to_all.31.in_ref = bf16[32,16,128]{2,1,0:T(8,128)(2,1)S(1)} all-to-all(bf16[32,16,128]{2,1,0:T(8,128)(2,1)S(1)} %shard_map.117), channel_id=1, replica_groups=mesh['yl'=2,'z'=16,'c'=2,'x'=4,'yh'=2] {'yl','c','x','yh'}, dimensions={0} | all-to-all | bytes 262144 | tf_op jit(solution)/shard_map/all_to_all | solution.py:358
  119.1 0.2 shard_map.118
  119.3 10.9 %all_to_all.32.in_ref = bf16[32,8,128]{2,1,0:T(8,128)(2,1)S(1)} all-to-all(bf16[32,8,128]{2,1,0:T(8,128)(2,1)S(1)} %shard_map.118), channel_id=1, replica_groups=mesh['yl'=2,'z'=16,'c'=2,'x'=4,'yh'=2] {'yl','c','x','yh'}, dimensions={0} | all-to-all | bytes 131072 | tf_op jit(solution)/shard_map/all_to_all | solution.py:360
  130.2 0.0 copy-done.1
  130.2 1.3 shard_map.119
  (1 shorter events, 0.0 us)
Async XLA Ops:
  1.6 17.3 %copy-start.2 = (bf16[1,128,1792]{2,1,0:T(8,128)(2,1)S(1)}, bf16[1,128,1792]{2,1,0:T(8,128)(2,1)}, u32[]{:S(2)}) copy-start(bf16[1,128,1792]{2,1,0:T(8,128)(2,1)} %param.12) | copy-start | bytes 1376260
  1.6 45.1 %all-to-all-start = ((bf16[32,8,896]{2,1,0:T(8,128)(2,1)}), bf16[32,8,896]{2,1,0:T(8,128)(2,1)S(1)}, u32[]{:S(2)}, u32[]{:S(2)}) async-start(bf16[32,8,896]{2,1,0:T(8,128)(2,1)} %shard_map.111), calls=%async_computation | async-start | bytes 917504 | tf_op jit(solution)/shard_map/all_to_all | solution.py:297
  18.8 0.7 copy-start.6
  18.9 0.7 copy-start.5
  19.5 14.8 %copy-start.3 = (bf16[1,128,128]{2,1,0:T(8,128)(2,1)S(1)}, bf16[1,128,128]{2,1,0:T(8,128)(2,1)}, u32[]{:S(2)}) copy-start(bf16[1,128,128]{2,1,0:T(8,128)(2,1)} %param.16) | copy-start | bytes 98308
  20.1 14.2 %copy-start.4 = (bf16[1,40,128]{2,1,0:T(8,128)(2,1)S(1)}, bf16[1,40,128]{2,1,0:T(8,128)(2,1)}, u32[]{:S(2)}) copy-start(bf16[1,40,128]{2,1,0:T(8,128)(2,1)} %param.15) | copy-start | bytes 30724
  20.1 9.5 %collective-permute-start = (bf16[144,896]{1,0:T(8,128)(2,1)S(1)}, bf16[144,896]{1,0:T(8,128)(2,1)S(1)}, u32[]{:S(2)}, u32[]{:S(2)}) collective-permute-start(bf16[144,896]{1,0:T(8,128)(2,1)S(1)} %get-tuple-element.22), channel_id=1, source_target_pairs={{0,256},{256,0},{1,257},{257,1},{2,258},{258,2},{3,259},{259,3},{4... | collective-permute-start | bytes 774152 | tf_op jit(solution)/shard_map/ppermute | solution.py:309
  23.3 12.5 %collective-permute-start.1 = (bf16[144,896]{1,0:T(8,128)(2,1)S(1)}, bf16[144,896]{1,0:T(8,128)(2,1)S(1)}, u32[]{:S(2)}, u32[]{:S(2)}) collective-permute-start(bf16[144,896]{1,0:T(8,128)(2,1)S(1)} %get-tuple-element.21.refs_0_), channel_id=1, source_target_pairs={{0,8},{8,0},{1,9},{9,1},{2,10},{10,2},{3,11},{11,3},{4,12},{12,4},... | collective-permute-start | bytes 774152 | tf_op jit(solution)/shard_map/ppermute | solution.py:310
  29.7 6.1 %collective-permute-start.2 = (bf16[144,896]{1,0:T(8,128)(2,1)S(1)}, bf16[144,896]{1,0:T(8,128)(2,1)S(1)}, u32[]{:S(2)}, u32[]{:S(2)}) collective-permute-start(bf16[144,896]{1,0:T(8,128)(2,1)S(1)} %collective-permute-done.refs_1_), channel_id=1, source_target_pairs={{0,8},{8,0},{1,9},{9,1},{2,10},{10,2},{3,11},{11,3},{4,12},{12,4},... | collective-permute-start | bytes 774152 | tf_op jit(solution)/shard_map/ppermute | solution.py:311
  34.3 0.7 copy-start.7
  34.3 0.7 copy-start.8
  48.1 39.3 %copy-start = (bf16[2,512,512]{2,1,0:T(8,128)(2,1)S(1)}, bf16[2,512,512]{2,1,0:T(8,128)(2,1)}, u32[]{:S(2)}) copy-start(bf16[2,512,512]{2,1,0:T(8,128)(2,1)} %constant.24.clone.table_ref) | copy-start | bytes 3145732
  48.1 17.8 %all-to-all-start.1 = ((bf16[32,32,128]{2,1,0:T(8,128)(2,1)}), bf16[32,32,128]{2,1,0:T(8,128)(2,1)S(1)}, u32[]{:S(2)}, u32[]{:S(2)}) async-start(bf16[32,32,128]{2,1,0:T(8,128)(2,1)} %shard_map.113), calls=%async_computation.1 | async-start | bytes 524288 | tf_op jit(solution)/shard_map/all_to_all | solution.py:329
  56.7 8.8 %collective-permute-start.3 = (bf16[176,128]{1,0:T(8,128)(2,1)S(1)}, bf16[176,128]{1,0:T(8,128)(2,1)S(1)}, u32[]{:S(2)}, u32[]{:S(2)}) collective-permute-start(bf16[176,128]{1,0:T(8,128)(2,1)S(1)} %shard_map.110), channel_id=1, source_target_pairs={{0,192},{1,49},{2,210},{3,35},{4,228},{5,21},{6,246},{7,7},{16,208... | collective-permute-start | bytes 135176 | tf_op jit(solution)/shard_map/ppermute | solution.py:328
  60.8 4.8 %collective-permute-start.4 = (bf16[176,128]{1,0:T(8,128)(2,1)S(1)}, bf16[176,128]{1,0:T(8,128)(2,1)S(1)}, u32[]{:S(2)}, u32[]{:S(2)}) collective-permute-start(bf16[176,128]{1,0:T(8,128)(2,1)S(1)} %shard_map.110), channel_id=1, source_target_pairs={{0,0},{1,241},{2,18},{3,227},{4,36},{5,213},{6,54},{7,199},{16,16}... | collective-permute-start | bytes 135176 | tf_op jit(solution)/shard_map/ppermute | solution.py:327
  66.6 20.8 %all-to-all-start.2 = ((bf16[16,32,128]{2,1,0:T(8,128)(2,1)}), bf16[16,32,128]{2,1,0:T(8,128)(2,1)S(1)}, u32[]{:S(2)}, u32[]{:S(2)}) async-start(bf16[16,32,128]{2,1,0:T(8,128)(2,1)} %shard_map.114), calls=%async_computation.2 | async-start | bytes 262144 | tf_op jit(solution)/shard_map/all_to_all | solution.py:336
  72.9 14.3 %collective-permute-start.5 = (bf16[176,128]{1,0:T(8,128)(2,1)S(1)}, bf16[176,128]{1,0:T(8,128)(2,1)S(1)}, u32[]{:S(2)}, u32[]{:S(2)}) collective-permute-start(bf16[176,128]{1,0:T(8,128)(2,1)S(1)} %collective-permute-done.3.middle_ref), channel_id=1, source_target_pairs={{0,192},{1,65},{2,194},{3,67},{4,196},{5,69},{6,198},{7,71},{16,20... | collective-permute-start | bytes 135176 | tf_op jit(solution)/shard_map/ppermute | solution.py:332
  107.1 23.1 %copy-start.1 = (bf16[1,2048,128]{2,1,0:T(8,128)(2,1)S(1)}, bf16[1,2048,128]{2,1,0:T(8,128)(2,1)}, u32[]{:S(2)}) copy-start(bf16[1,2048,128]{2,1,0:T(8,128)(2,1)} %param.19) | copy-start | bytes 1572868

commit v11 on v8

--- a/solution.py
+++ b/solution.py
@@ -12,7 +12,7 @@
 YL, Z, C, D = 2, 16, 2, 8
 PEERS = YL * C * D
 BLADES, PH, NT, NB, MODES = YL * Z * C, 8, 256, 128, 40
-HALF = 896
+COLS = 1792
 TS = NT // PEERS
 TD = NT // D
 BF = jnp.bfloat16
@@ -62,29 +62,26 @@
 
 
 def spread_kernel(in_ref, out_ref, wake_ref, hold_ref, sems):
-    copy = pltpu.make_async_copy(in_ref, wake_ref, sems.at[YL])
+    copy = pltpu.make_async_copy(in_ref, wake_ref, sems.at[2])
     copy.start()
     copy.wait()
     copies = []
-    for half in range(YL):
-        rows = pl.ds(half * Z, Z)
-        part = wake_ref[:, half * HALF : (half + 1) * HALF]
-        hold_ref[rows] = jnp.broadcast_to(part[None], (Z, PH, HALF))
-        copies.append(pltpu.make_async_copy(hold_ref.at[rows], out_ref.at[rows], sems.at[half]))
+    for k in range(2):
+        rows = pl.ds(k * Z // 2, Z // 2)
+        hold_ref[rows] = jnp.broadcast_to(wake_ref[...][None], (Z // 2, PH, COLS))
+        copies.append(pltpu.make_async_copy(hold_ref.at[rows], out_ref.at[rows], sems.at[k]))
         copies[-1].start()
     for copy in copies:
         copy.wait()
 
 
-def pack_kernel(pos, basis_ref, block_ref, phase_ref, near_ref, far_ref):
+def pack_kernel(basis_ref, block_ref, phase_ref, out_ref):
     index = jnp.concatenate(
         [block_ref[...].astype(F32), phase_ref[...].astype(F32), jnp.zeros((14, NT), F32)], axis=0
     )
-    index = jnp.concatenate([index, jnp.zeros((16, HALF - NT), F32)], axis=1).astype(BF)
-    for k, ref in enumerate((near_ref, far_ref)):
-        half = (pos[0] + k) & 1
-        ref[0:NB] = basis_ref[:, pl.ds(pl.multiple_of(half * HALF, 128), HALF)]
-        ref[NB : NB + 16] = index
+    index = jnp.concatenate([index, jnp.zeros((16, COLS - NT), F32)], axis=1).astype(BF)
+    out_ref[0:NB] = basis_ref[...]
+    out_ref[NB : NB + 16] = index
 
 
 def select_kernel(pos, *refs):
@@ -94,16 +91,17 @@
         basis_ref[r * NB : (r + 1) * NB] = ref[0:NB]
         index = ref[NB : NB + 16, 0:NT].astype(F32)
         block, phase = index[0:1].astype(jnp.int32), index[1:2].astype(jnp.int32)
-        code = ((block >> 1) * PH + phase).astype(F32)
-        codes.append(jnp.where((block & 1) == pos[1], code, -1.0))
+        code = (((block >> 1) & (Z - 1)) * PH + phase).astype(F32)
+        here = ((block & 1) == pos[1]) & ((block >> 5) == pos[0])
+        codes.append(jnp.where(here, code, -1.0))
     codes = jnp.concatenate(codes + [jnp.zeros((4, NT), F32)], axis=0).T
-    pair = lax.broadcasted_iota(jnp.int32, (NT, YL * Z * PH), 1).astype(F32)
+    pair = lax.broadcasted_iota(jnp.int32, (NT, Z * PH), 1).astype(F32)
     for r in range(4):
         onehot_ref[r] = jnp.where(codes[:, r : r + 1] == pair, 1.0, 0.0).astype(BF)
 
 
 def project_kernel(wake_ref, basis_ref, onehot_ref, out_ref):
-    table = dot_nt(wake_ref[...].reshape(YL * Z * PH, HALF), basis_ref[...]).astype(BF)
+    table = dot_nt(wake_ref[...].reshape(Z * PH, COLS), basis_ref[...]).astype(BF)
     picks = []
     for r in range(4):
         part = jnp.dot(
@@ -253,37 +251,29 @@
 
     spread = call(
         spread_kernel,
-        [(YL * Z, PH, HALF)],
+        [(Z, PH, COLS)],
         [HBM],
         wake[0],
         out_specs=[HBM],
         vmem=60,
         scratch=[
-            pltpu.VMEM((PH, YL * HALF), BF),
-            pltpu.VMEM((YL * Z, PH, HALF), BF),
-            pltpu.SemaphoreType.DMA((YL + 1,)),
+            pltpu.VMEM((PH, COLS), BF),
+            pltpu.VMEM((Z, PH, COLS), BF),
+            pltpu.SemaphoreType.DMA((3,)),
         ],
     )
-    blocks = lax.all_to_all(spread, ("yl", "z"), 0, 0, tiled=True)
-
-    near, far = call(
-        pack_kernel,
-        [(NB + 16, HALF)] * 2,
-        [SMEM, VMEM, VMEM, VMEM],
-        pos,
-        basis[0],
-        block_index,
-        phase_index,
-    )
+    blocks = lax.all_to_all(spread, "z", 0, 0, tiled=True)
+
+    near = call(pack_kernel, [(NB + 16, COLS)], [VMEM] * 3, basis[0], block_index, phase_index)
     swap = [(0, 1), (1, 0)]
-    by_yl = lax.ppermute(far, "yl", swap)
+    by_yl = lax.ppermute(near, "yl", swap)
     by_c = lax.ppermute(near, "c", swap)
     by_both = lax.ppermute(by_yl, "c", swap)
     near, forward, inverse, powers = lax.optimization_barrier((near, forward, inverse, powers))
 
     joined, onehot = call(
         select_kernel,
-        [(4 * NB, HALF), (4, NT, YL * Z * PH)],
+        [(4 * NB, COLS), (4, NT, Z * PH)],
         [SMEM] + [VMEM] * 4,
         pos,
         near,

time: 130 us -> 135 us (1.038)
  local copies, waits for them, and re-layouts: 2.93 us -> 9.27 us
  blocking collectives: 78.7 us -> 84.6 us
  waiting for transfers between devices: 12 us -> 7.84 us
  starting transfers between devices: 28.4 us -> 25.9 us
    all_to_all x1, waiting for transfers between devices: 9.13 us -> 0.01 us  [local(): blocks = lax.all_to_all(spread, 'z', 0, 0, tiled=True)]
    all_to_all x1, blocking collectives: 16.7 us -> 23.7 us  [local(): forcing = lax.all_to_all(forcing, 'z', 0, 0, tiled=True)]
    unnamed x16 -> x28, local copies, waits for them, and re-layouts: 1.36 us -> 7.7 us
    ppermute x1, waiting for transfers between devices: 2.87 us -> 7.83 us  [local(): by_yl = lax.ppermute(near, 'yl', swap)]
    all_to_all x1, starting transfers between devices: 17.2 us -> 15.8 us  [local(): blocks = lax.all_to_all(spread, 'z', 0, 0, tiled=True)]
  transfers between devices with their start and end apart: 4 -> 4, of which waited for: 2 -> 1; matrix products, arithmetic and copies ran while one was open for 1% -> 1% of each run, Pallas kernels for 1% -> 1%
where the time goes in v11:
time: 135 us; the launch traced here: 134 us
  blocking collectives  84.6 us (63%)
  starting transfers between devices  25.9 us (19%)
  local copies, waits for them, and re-layouts  9.27 us (7%)
  waiting for transfers between devices  7.84 us (6%)
  Pallas kernels  6.29 us (5%)
    all_to_all x1, blocking collectives, local(): forcing = lax.all_to_all(forcing, 'z', 0, 0, tiled=True)  23.7 us
    all_to_all x1, blocking collectives, local(): parts = lax.all_to_all(picked, PLANE, 0, 0, tiled=True)  16.4 us
    all_to_all x1, blocking collectives, local(): physical = lax.all_to_all(physical, 'z', 0, 0, tiled=True)  15.8 us
    all_to_all x1, starting transfers between devices, local(): blocks = lax.all_to_all(spread, 'z', 0, 0, tiled=True)  15.8 us
    all_to_all x1, blocking collectives, local(): sectoral = lax.all_to_all(sectoral, PLANE, 0, 0, tiled=True)  15.6 us
    all_to_all x1, blocking collectives, local(): harmonic = lax.all_to_all(harmonic, PLANE, 0, 0, tiled=True)  13.2 us
    ppermute x1, waiting for transfers between devices, local(): by_yl = lax.ppermute(near, 'yl', swap)  7.83 us
    unnamed x28, local copies, waits for them, and re-layouts  7.7 us
  transfers between devices with their start and end apart: 4, of which 1 were waited for; matrix products, arithmetic and copies ran while one was open for 1% of the time, Pallas kernels for 1%

profile of v11, /device:TPU:1, one launch (start us, length us, event | category | flops | bytes accessed | tf_op | source)
XLA Modules:
  0.0 134.1 jit_solution(793228301505884802)
XLA Ops:
  0.0 0.0 copy-start.12
  0.0 0.0 copy-start.13
  0.0 1.6 %shard_map.111 = bf16[16,8,1792]{2,1,0:T(8,128)(2,1)} custom-call(bf16[8,1792]{1,0:T(8,128)(2,1)} %bitcast.17), custom_call_target="tpu_custom_call" | custom-call | tf_op jit(solution)/shard_map/pallas_call | solution.py:231
  1.6 15.8 %all-to-all-start = ((bf16[16,8,1792]{2,1,0:T(8,128)(2,1)}), bf16[16,8,1792]{2,1,0:T(8,128)(2,1)S(1)}, u32[]{:S(2)}, u32[]{:S(2)}) async-start(bf16[16,8,1792]{2,1,0:T(8,128)(2,1)} %shard_map.111), calls=%async_computation | async-start | bytes 917504 | tf_op jit(solution)/shard_map/all_to_all | solution.py:265
  17.4 0.0 copy-start.5
  17.4 1.0 copy-done.5
  18.4 0.0 copy-start.10
  18.4 0.7 copy-done.10
  19.1 0.0 copy-start.11
  19.1 0.7 copy-done.11
  19.8 3.2 %collective-permute-start = (bf16[144,1792]{1,0:T(8,128)(2,1)S(1)}, bf16[144,1792]{1,0:T(8,128)(2,1)S(1)}, u32[]{:S(2)}, u32[]{:S(2)}) collective-permute-start(bf16[144,1792]{1,0:T(8,128)(2,1)S(1)} %shard_map.109.refs_0_), channel_id=1, source_target_pairs={{0,256},{256,0},{1,257},{257,1},{2,258},{258,2},{3,259},{259,3},{4... | collective-permute-start | bytes 1548296 | tf_op jit(solution)/shard_map/ppermute | solution.py:269
  23.0 3.1 %collective-permute-start.1 = (bf16[144,1792]{1,0:T(8,128)(2,1)S(1)}, bf16[144,1792]{1,0:T(8,128)(2,1)S(1)}, u32[]{:S(2)}, u32[]{:S(2)}) collective-permute-start(bf16[144,1792]{1,0:T(8,128)(2,1)S(1)} %shard_map.109.refs_0_), channel_id=1, source_target_pairs={{0,8},{8,0},{1,9},{9,1},{2,10},{10,2},{3,11},{11,3},{4,12},{12,4},... | collective-permute-start | bytes 1548296 | tf_op jit(solution)/shard_map/ppermute | solution.py:270
  26.1 7.8 %collective-permute-done.refs_1_ = bf16[144,1792]{1,0:T(8,128)(2,1)S(1)} collective-permute-done((bf16[144,1792]{1,0:T(8,128)(2,1)S(1)}, bf16[144,1792]{1,0:T(8,128)(2,1)S(1)}, u32[]{:S(2)}, u32[]{:S(2)}) %collective-permute-start) | collective-permute-done | bytes 516128 | tf_op jit(solution)/shard_map/ppermute | solution.py:269
  34.0 3.8 %collective-permute-start.2 = (bf16[144,1792]{1,0:T(8,128)(2,1)S(1)}, bf16[144,1792]{1,0:T(8,128)(2,1)S(1)}, u32[]{:S(2)}, u32[]{:S(2)}) collective-permute-start(bf16[144,1792]{1,0:T(8,128)(2,1)S(1)} %collective-permute-done.refs_1_), channel_id=1, source_target_pairs={{0,8},{8,0},{1,9},{9,1},{2,10},{10,2},{3,11},{11,3},{4,12},{12,4},... | collective-permute-start | bytes 1548296 | tf_op jit(solution)/shard_map/ppermute | solution.py:271
  37.8 0.0 copy-done.12
  37.8 0.0 copy-done.13
  37.8 0.1 shard_map.110.powers_ref
  37.8 0.7 dynamic-slice_bitcast_fusion.1.table_ref
  38.6 0.8 dynamic-slice_bitcast_fusion.table_ref
  39.4 0.1 pad_add_fusion.pos
  39.5 0.0 collective-permute-done.1.refs_2_
  39.5 0.0 copy-start.1
  39.5 0.8 copy-done.1
  40.3 0.0 collective-permute-done.2.refs_3_
  40.3 0.0 copy-start.3
  40.3 0.8 copy-done.3
  41.1 0.0 copy-start.2
  41.1 1.0 copy-done.2
  42.1 0.0 copy-start.4
  42.1 1.0 copy-done.4
  43.2 1.0 shard_map.112
  44.1 0.0 copy-start.6
  44.1 0.7 copy-done.6
  44.8 0.0 all-to-all-done.wake_ref
  44.8 0.0 copy-start.7
  44.8 0.9 copy-done.7
  45.8 0.0 copy-start.8
  45.8 0.0 copy-start.9
  45.8 0.9 shard_map.113
  46.7 0.0 copy-start
  46.7 16.4 %all_to_all.30.in_ref = bf16[32,32,128]{2,1,0:T(8,128)(2,1)S(1)} all-to-all(bf16[32,32,128]{2,1,0:T(8,128)(2,1)S(1)} %shard_map.113), channel_id=1, replica_groups=mesh['yl'=2,'z'=16,'c'=2,'x'=4,'yh'=2] {'yl','c','x','yh'}, dimensions={0} | all-to-all | bytes 524288 | tf_op jit(solution)/shard_map/all_to_all | solution.py:285
  63.2 23.7 %all_to_all.31.in_ref = bf16[16,32,128]{2,1,0:T(8,128)(2,1)S(1)} all-to-all(bf16[16,32,128]{2,1,0:T(8,128)(2,1)S(1)} %shard_map.114), channel_id=1, replica_groups=mesh['yl'=2,'z'=16,'c'=2,'x'=4,'yh'=2] {'z'}, dimensions={0} | all-to-all | bytes 262144 | tf_op jit(solution)/shard_map/all_to_all | solution.py:287
  86.9 0.2 shard_map.115
  87.0 13.2 %all_to_all.32.in_ref = bf16[32,8,128]{2,1,0:T(8,128)(2,1)S(1)} all-to-all(bf16[32,8,128]{2,1,0:T(8,128)(2,1)S(1)} %shard_map.115), channel_id=1, replica_groups=mesh['yl'=2,'z'=16,'c'=2,'x'=4,'yh'=2] {'yl','c','x','yh'}, dimensions={0} | all-to-all | bytes 131072 | tf_op jit(solution)/shard_map/all_to_all | solution.py:289
  100.2 0.0 copy-done.8
  100.2 0.0 copy-done.9
  100.2 1.1 shard_map.116
  101.3 15.8 %all_to_all.33.in_ref = bf16[16,32,128]{2,1,0:T(8,128)(2,1)S(1)} all-to-all(bf16[16,32,128]{2,1,0:T(8,128)(2,1)S(1)} %shard_map.116), channel_id=1, replica_groups=mesh['yl'=2,'z'=16,'c'=2,'x'=4,'yh'=2] {'z'}, dimensions={0} | all-to-all | bytes 262144 | tf_op jit(solution)/shard_map/all_to_all | solution.py:301
  117.1 0.2 shard_map.117
  117.3 15.6 %all_to_all.34.in_ref = bf16[32,32,128]{2,1,0:T(8,128)(2,1)S(1)} all-to-all(bf16[32,32,128]{2,1,0:T(8,128)(2,1)S(1)} %shard_map.117), channel_id=1, replica_groups=mesh['yl'=2,'z'=16,'c'=2,'x'=4,'yh'=2] {'yl','c','x','yh'}, dimensions={0} | all-to-all | bytes 524288 | tf_op jit(solution)/shard_map/all_to_all | solution.py:303
  132.9 0.0 copy-done
  132.9 1.3 shard_map.118
  (2 shorter events, 0.1 us)
Async XLA Ops:
  0.0 37.8 %copy-start.12 = (f32[1,40]{1,0:T(1,128)S(1)}, f32[1,40]{1,0:T(1,128)}, u32[]{:S(2)}) copy-start(f32[1,40]{1,0:T(1,128)} %omega_ref.1) | copy-start | bytes 484
  0.0 37.8 %copy-start.13 = (f32[1,40]{1,0:T(1,128)S(1)}, f32[1,40]{1,0:T(1,128)}, u32[]{:S(2)}) copy-start(f32[1,40]{1,0:T(1,128)} %zeta_ref.1) | copy-start | bytes 484
  1.6 43.3 %all-to-all-start = ((bf16[16,8,1792]{2,1,0:T(8,128)(2,1)}), bf16[16,8,1792]{2,1,0:T(8,128)(2,1)S(1)}, u32[]{:S(2)}, u32[]{:S(2)}) async-start(bf16[16,8,1792]{2,1,0:T(8,128)(2,1)} %shard_map.111), calls=%async_computation | async-start | bytes 917504 | tf_op jit(solution)/shard_map/all_to_all | solution.py:265
  17.4 1.0 copy-start.5
  18.4 0.7 copy-start.10
  19.1 0.7 copy-start.11
  19.8 14.2 %collective-permute-start = (bf16[144,1792]{1,0:T(8,128)(2,1)S(1)}, bf16[144,1792]{1,0:T(8,128)(2,1)S(1)}, u32[]{:S(2)}, u32[]{:S(2)}) collective-permute-start(bf16[144,1792]{1,0:T(8,128)(2,1)S(1)} %shard_map.109.refs_0_), channel_id=1, source_target_pairs={{0,256},{256,0},{1,257},{257,1},{2,258},{258,2},{3,259},{259,3},{4... | collective-permute-start | bytes 1548296 | tf_op jit(solution)/shard_map/ppermute | solution.py:269
  23.0 16.5 %collective-permute-start.1 = (bf16[144,1792]{1,0:T(8,128)(2,1)S(1)}, bf16[144,1792]{1,0:T(8,128)(2,1)S(1)}, u32[]{:S(2)}, u32[]{:S(2)}) collective-permute-start(bf16[144,1792]{1,0:T(8,128)(2,1)S(1)} %shard_map.109.refs_0_), channel_id=1, source_target_pairs={{0,8},{8,0},{1,9},{9,1},{2,10},{10,2},{3,11},{11,3},{4,12},{12,4},... | collective-permute-start | bytes 1548296 | tf_op jit(solution)/shard_map/ppermute | solution.py:270
  34.0 6.3 %collective-permute-start.2 = (bf16[144,1792]{1,0:T(8,128)(2,1)S(1)}, bf16[144,1792]{1,0:T(8,128)(2,1)S(1)}, u32[]{:S(2)}, u32[]{:S(2)}) collective-permute-start(bf16[144,1792]{1,0:T(8,128)(2,1)S(1)} %collective-permute-done.refs_1_), channel_id=1, source_target_pairs={{0,8},{8,0},{1,9},{9,1},{2,10},{10,2},{3,11},{11,3},{4,12},{12,4},... | collective-permute-start | bytes 1548296 | tf_op jit(solution)/shard_map/ppermute | solution.py:271
  39.5 0.8 copy-start.1
  40.3 0.8 copy-start.3
  41.1 1.0 copy-start.2
  42.1 1.0 copy-start.4
  44.1 0.7 copy-start.6
  44.8 1.0 copy-start.7
  45.8 54.4 %copy-start.8 = (bf16[1,128,128]{2,1,0:T(8,128)(2,1)S(1)}, bf16[1,128,128]{2,1,0:T(8,128)(2,1)}, u32[]{:S(2)}) copy-start(bf16[1,128,128]{2,1,0:T(8,128)(2,1)} %param.16) | copy-start | bytes 98308
  45.8 54.4 %copy-start.9 = (bf16[1,40,128]{2,1,0:T(8,128)(2,1)S(1)}, bf16[1,40,128]{2,1,0:T(8,128)(2,1)}, u32[]{:S(2)}) copy-start(bf16[1,40,128]{2,1,0:T(8,128)(2,1)} %param.15) | copy-start | bytes 30724
  46.7 86.1 %copy-start = (bf16[1,2048,128]{2,1,0:T(8,128)(2,1)S(1)}, bf16[1,2048,128]{2,1,0:T(8,128)(2,1)}, u32[]{:S(2)}) copy-start(bf16[1,2048,128]{2,1,0:T(8,128)(2,1)} %param.19) | copy-start | bytes 1572868

commit v12 on v11

--- a/solution.py
+++ b/solution.py
@@ -84,11 +84,11 @@
     out_ref[NB : NB + 16] = index
 
 
-def select_kernel(pos, *refs):
-    basis_ref, onehot_ref = refs[4:]
+def project_kernel(pos, wake_ref, *refs):
+    out_ref = refs[4]
+    wake = wake_ref[...].reshape(Z * PH, COLS)
     codes = []
-    for r, ref in enumerate(refs[:4]):
-        basis_ref[r * NB : (r + 1) * NB] = ref[0:NB]
+    for ref in refs[:4]:
         index = ref[NB : NB + 16, 0:NT].astype(F32)
         block, phase = index[0:1].astype(jnp.int32), index[1:2].astype(jnp.int32)
         code = (((block >> 1) & (Z - 1)) * PH + phase).astype(F32)
@@ -96,17 +96,11 @@
         codes.append(jnp.where(here, code, -1.0))
     codes = jnp.concatenate(codes + [jnp.zeros((4, NT), F32)], axis=0).T
     pair = lax.broadcasted_iota(jnp.int32, (NT, Z * PH), 1).astype(F32)
-    for r in range(4):
-        onehot_ref[r] = jnp.where(codes[:, r : r + 1] == pair, 1.0, 0.0).astype(BF)
-
-
-def project_kernel(wake_ref, basis_ref, onehot_ref, out_ref):
-    table = dot_nt(wake_ref[...].reshape(Z * PH, COLS), basis_ref[...]).astype(BF)
     picks = []
-    for r in range(4):
-        part = jnp.dot(
-            onehot_ref[r], table[:, r * NB : (r + 1) * NB], preferred_element_type=F32
-        )
+    for r, ref in enumerate(refs[:4]):
+        table = dot_nt(wake, ref[0:NB]).astype(BF)
+        onehot = jnp.where(codes[:, r : r + 1] == pair, 1.0, 0.0).astype(BF)
+        part = jnp.dot(onehot, table, preferred_element_type=F32)
         picks.append(part.reshape(PEERS, TS, NB))
     out_ref[...] = jnp.concatenate(picks, axis=1).astype(BF)
 
@@ -271,17 +265,17 @@
     by_both = lax.ppermute(by_yl, "c", swap)
     near, forward, inverse, powers = lax.optimization_barrier((near, forward, inverse, powers))
 
-    joined, onehot = call(
-        select_kernel,
-        [(4 * NB, COLS), (4, NT, Z * PH)],
-        [SMEM] + [VMEM] * 4,
+    picked = call(
+        project_kernel,
+        [(PEERS, 4 * TS, NB)],
+        [SMEM] + [VMEM] * 5,
         pos,
+        blocks,
         near,
         by_yl,
         by_c,
         by_both,
     )
-    picked = call(project_kernel, [(PEERS, 4 * TS, NB)], [VMEM] * 3, blocks, joined, onehot)
     parts = lax.all_to_all(picked, PLANE, 0, 0, tiled=True)
     forcing = call(gather_sum_kernel, [(Z, 4 * TS, NB)], [VMEM], parts)
     forcing = lax.all_to_all(forcing, "z", 0, 0, tiled=True)

time: 135 us -> 129 us (0.956)
  local copies, waits for them, and re-layouts: 9.27 us -> 2.91 us
    unnamed x28 -> x16, local copies, waits for them, and re-layouts: 7.7 us -> 1.34 us
    all_to_all x1, blocking collectives: 16.4 us -> 22.7 us  [local(): parts = lax.all_to_all(picked, PLANE, 0, 0, tiled=True)]
    all_to_all x1, blocking collectives: 23.7 us -> 17.8 us  [local(): forcing = lax.all_to_all(forcing, 'z', 0, 0, tiled=True)]
    pallas_call x10 -> x9, Pallas kernels: 6.29 us -> 6.51 us  [call(): pl.pallas_call(kernel, out_shape=outs, in_specs=specs, out_specs=out_spec...]
  transfers between devices with their start and end apart: 4 -> 4, of which waited for: 1 -> 1; matrix products, arithmetic and copies ran while one was open for 1% -> 1% of each run, Pallas kernels for 1% -> 0%
where the time goes in v12:
time: 129 us
  blocking collectives  85 us (66%)
  starting transfers between devices  26 us (20%)
  waiting for transfers between devices  7.84 us (6%)
  Pallas kernels  6.51 us (5%)
  local copies, waits for them, and re-layouts  2.91 us (2%)
    all_to_all x1, blocking collectives, local(): parts = lax.all_to_all(picked, PLANE, 0, 0, tiled=True)  22.7 us
    all_to_all x1, blocking collectives, local(): forcing = lax.all_to_all(forcing, 'z', 0, 0, tiled=True)  17.8 us
    all_to_all x1, starting transfers between devices, local(): blocks = lax.all_to_all(spread, 'z', 0, 0, tiled=True)  15.9 us
    all_to_all x1, blocking collectives, local(): physical = lax.all_to_all(physical, 'z', 0, 0, tiled=True)  15.8 us
    all_to_all x1, blocking collectives, local(): sectoral = lax.all_to_all(sectoral, PLANE, 0, 0, tiled=True)  15.6 us
    all_to_all x1, blocking collectives, local(): harmonic = lax.all_to_all(harmonic, PLANE, 0, 0, tiled=True)  13.2 us
    ppermute x1, waiting for transfers between devices, local(): by_yl = lax.ppermute(near, 'yl', swap)  7.83 us
    pallas_call x9, Pallas kernels, call(): pl.pallas_call(kernel, out_shape=outs, in_specs=specs, out_specs=out_spec...  6.51 us
  transfers between devices with their start and end apart: 4, of which 1 were waited for; matrix products, arithmetic and copies ran while one was open for 1% of the time, Pallas kernels for 0%

profile of v12, /device:TPU:1, one launch (start us, length us, event | category | flops | bytes accessed | tf_op | source)
XLA Modules:
  0.0 128.6 jit_solution(8888209499596906468)
XLA Ops:
  0.0 1.5 %shard_map.111 = bf16[16,8,1792]{2,1,0:T(8,128)(2,1)} custom-call(bf16[8,1792]{1,0:T(8,128)(2,1)} %bitcast.17), custom_call_target="tpu_custom_call" | custom-call | tf_op jit(solution)/shard_map/pallas_call | solution.py:225
  1.6 0.0 copy-start.1
  1.6 0.0 copy-start.5
  1.6 15.9 %all-to-all-start = ((bf16[16,8,1792]{2,1,0:T(8,128)(2,1)}), bf16[16,8,1792]{2,1,0:T(8,128)(2,1)S(1)}, u32[]{:S(2)}, u32[]{:S(2)}) async-start(bf16[16,8,1792]{2,1,0:T(8,128)(2,1)} %shard_map.111), calls=%async_computation | async-start | bytes 917504 | tf_op jit(solution)/shard_map/all_to_all | solution.py:259
  17.5 0.0 copy-start.4
  17.5 0.0 copy-done.1
  17.5 0.0 copy-done.5
  17.5 0.7 copy-done.4
  18.2 3.2 %collective-permute-start = (bf16[144,1792]{1,0:T(8,128)(2,1)S(1)}, bf16[144,1792]{1,0:T(8,128)(2,1)S(1)}, u32[]{:S(2)}, u32[]{:S(2)}) collective-permute-start(bf16[144,1792]{1,0:T(8,128)(2,1)S(1)} %shard_map.109.refs_0_), channel_id=1, source_target_pairs={{0,256},{256,0},{1,257},{257,1},{2,258},{258,2},{3,259},{259,3},{4... | collective-permute-start | bytes 1548296 | tf_op jit(solution)/shard_map/ppermute | solution.py:263
  21.4 3.1 %collective-permute-start.1 = (bf16[144,1792]{1,0:T(8,128)(2,1)S(1)}, bf16[144,1792]{1,0:T(8,128)(2,1)S(1)}, u32[]{:S(2)}, u32[]{:S(2)}) collective-permute-start(bf16[144,1792]{1,0:T(8,128)(2,1)S(1)} %shard_map.109.refs_0_), channel_id=1, source_target_pairs={{0,8},{8,0},{1,9},{9,1},{2,10},{10,2},{3,11},{11,3},{4,12},{12,4},... | collective-permute-start | bytes 1548296 | tf_op jit(solution)/shard_map/ppermute | solution.py:264
  24.6 7.8 %collective-permute-done.refs_1_ = bf16[144,1792]{1,0:T(8,128)(2,1)S(1)} collective-permute-done((bf16[144,1792]{1,0:T(8,128)(2,1)S(1)}, bf16[144,1792]{1,0:T(8,128)(2,1)S(1)}, u32[]{:S(2)}, u32[]{:S(2)}) %collective-permute-start) | collective-permute-done | bytes 516128 | tf_op jit(solution)/shard_map/ppermute | solution.py:263
  32.4 3.8 %collective-permute-start.2 = (bf16[144,1792]{1,0:T(8,128)(2,1)S(1)}, bf16[144,1792]{1,0:T(8,128)(2,1)S(1)}, u32[]{:S(2)}, u32[]{:S(2)}) collective-permute-start(bf16[144,1792]{1,0:T(8,128)(2,1)S(1)} %collective-permute-done.refs_1_), channel_id=1, source_target_pairs={{0,8},{8,0},{1,9},{9,1},{2,10},{10,2},{3,11},{11,3},{4,12},{12,4},... | collective-permute-start | bytes 1548296 | tf_op jit(solution)/shard_map/ppermute | solution.py:265
  36.2 0.0 copy-start.6
  36.2 0.0 copy-start.7
  36.2 0.6 copy-done.6
  36.8 0.0 copy-done.7
  36.9 0.1 shard_map.110.powers_ref
  36.9 0.7 dynamic-slice_bitcast_fusion.1.table_ref
  37.6 0.8 dynamic-slice_bitcast_fusion.table_ref
  38.5 0.1 pad_add_fusion.pos
  38.6 0.0 collective-permute-done.1.refs_2_
  38.6 0.0 collective-permute-done.2.refs_3_
  38.6 0.0 all-to-all-done.wake_ref
  38.6 2.1 %shard_map.112 = bf16[32,32,128]{2,1,0:T(8,128)(2,1)S(1)} custom-call(s32[3]{0:T(128)S(1)} %pad_add_fusion.pos, bf16[16,8,1792]{2,1,0:T(8,128)(2,1)S(1)} %all-to-all-done.wake_ref, bf16[144,1792]{1,0:T(8,128)(2,1)S(1)} %shard_map.109.refs_0_, bf16[144,1792]{1,0:T(8,128)(2,1)S(1)} %collective-permute-done.refs_1_, ...), custom_call_target="tpu_custom_call" | custom-call | tf_op jit(solution)/shard_map/pallas_call | solution.py:225
  40.7 22.7 %all_to_all.30.in_ref = bf16[32,32,128]{2,1,0:T(8,128)(2,1)S(1)} all-to-all(bf16[32,32,128]{2,1,0:T(8,128)(2,1)S(1)} %shard_map.112), channel_id=1, replica_groups=mesh['yl'=2,'z'=16,'c'=2,'x'=4,'yh'=2] {'yl','c','x','yh'}, dimensions={0} | all-to-all | bytes 524288 | tf_op jit(solution)/shard_map/all_to_all | solution.py:279
  63.4 17.8 %all_to_all.31.in_ref = bf16[16,32,128]{2,1,0:T(8,128)(2,1)S(1)} all-to-all(bf16[16,32,128]{2,1,0:T(8,128)(2,1)S(1)} %shard_map.113), channel_id=1, replica_groups=mesh['yl'=2,'z'=16,'c'=2,'x'=4,'yh'=2] {'z'}, dimensions={0} | all-to-all | bytes 262144 | tf_op jit(solution)/shard_map/all_to_all | solution.py:281
  81.3 0.2 shard_map.114
  81.4 0.0 copy-start.2
  81.4 0.0 copy-start.3
  81.5 13.2 %all_to_all.32.in_ref = bf16[32,8,128]{2,1,0:T(8,128)(2,1)S(1)} all-to-all(bf16[32,8,128]{2,1,0:T(8,128)(2,1)S(1)} %shard_map.114), channel_id=1, replica_groups=mesh['yl'=2,'z'=16,'c'=2,'x'=4,'yh'=2] {'yl','c','x','yh'}, dimensions={0} | all-to-all | bytes 131072 | tf_op jit(solution)/shard_map/all_to_all | solution.py:283
  94.6 0.0 copy-done.2
  94.6 0.0 copy-done.3
  94.6 1.1 shard_map.115
  95.7 15.8 %all_to_all.33.in_ref = bf16[16,32,128]{2,1,0:T(8,128)(2,1)S(1)} all-to-all(bf16[16,32,128]{2,1,0:T(8,128)(2,1)S(1)} %shard_map.115), channel_id=1, replica_groups=mesh['yl'=2,'z'=16,'c'=2,'x'=4,'yh'=2] {'z'}, dimensions={0} | all-to-all | bytes 262144 | tf_op jit(solution)/shard_map/all_to_all | solution.py:295
  111.5 0.0 copy-start
  111.5 0.2 shard_map.116
  111.7 15.6 %all_to_all.34.in_ref = bf16[32,32,128]{2,1,0:T(8,128)(2,1)S(1)} all-to-all(bf16[32,32,128]{2,1,0:T(8,128)(2,1)S(1)} %shard_map.116), channel_id=1, replica_groups=mesh['yl'=2,'z'=16,'c'=2,'x'=4,'yh'=2] {'yl','c','x','yh'}, dimensions={0} | all-to-all | bytes 524288 | tf_op jit(solution)/shard_map/all_to_all | solution.py:297
  127.3 0.0 copy-done
  127.3 1.3 shard_map.117
  (2 shorter events, 0.1 us)
Async XLA Ops:
  1.6 15.9 %copy-start.1 = (bf16[1,128,1792]{2,1,0:T(8,128)(2,1)S(1)}, bf16[1,128,1792]{2,1,0:T(8,128)(2,1)}, u32[]{:S(2)}) copy-start(bf16[1,128,1792]{2,1,0:T(8,128)(2,1)} %param.12) | copy-start | bytes 1376260
  1.6 15.9 %copy-start.5 = (s32[1,256]{1,0:T(1,128)S(1)}, s32[1,256]{1,0:T(1,128)}, u32[]{:S(2)}) copy-start(s32[1,256]{1,0:T(1,128)} %phase_ref.1) | copy-start | bytes 3076
  1.6 37.0 %all-to-all-start = ((bf16[16,8,1792]{2,1,0:T(8,128)(2,1)}), bf16[16,8,1792]{2,1,0:T(8,128)(2,1)S(1)}, u32[]{:S(2)}, u32[]{:S(2)}) async-start(bf16[16,8,1792]{2,1,0:T(8,128)(2,1)} %shard_map.111), calls=%async_computation | async-start | bytes 917504 | tf_op jit(solution)/shard_map/all_to_all | solution.py:259
  17.5 0.7 copy-start.4
  18.2 14.2 %collective-permute-start = (bf16[144,1792]{1,0:T(8,128)(2,1)S(1)}, bf16[144,1792]{1,0:T(8,128)(2,1)S(1)}, u32[]{:S(2)}, u32[]{:S(2)}) collective-permute-start(bf16[144,1792]{1,0:T(8,128)(2,1)S(1)} %shard_map.109.refs_0_), channel_id=1, source_target_pairs={{0,256},{256,0},{1,257},{257,1},{2,258},{258,2},{3,259},{259,3},{4... | collective-permute-start | bytes 1548296 | tf_op jit(solution)/shard_map/ppermute | solution.py:263
  21.4 17.2 %collective-permute-start.1 = (bf16[144,1792]{1,0:T(8,128)(2,1)S(1)}, bf16[144,1792]{1,0:T(8,128)(2,1)S(1)}, u32[]{:S(2)}, u32[]{:S(2)}) collective-permute-start(bf16[144,1792]{1,0:T(8,128)(2,1)S(1)} %shard_map.109.refs_0_), channel_id=1, source_target_pairs={{0,8},{8,0},{1,9},{9,1},{2,10},{10,2},{3,11},{11,3},{4,12},{12,4},... | collective-permute-start | bytes 1548296 | tf_op jit(solution)/shard_map/ppermute | solution.py:264
  32.4 6.2 %collective-permute-start.2 = (bf16[144,1792]{1,0:T(8,128)(2,1)S(1)}, bf16[144,1792]{1,0:T(8,128)(2,1)S(1)}, u32[]{:S(2)}, u32[]{:S(2)}) collective-permute-start(bf16[144,1792]{1,0:T(8,128)(2,1)S(1)} %collective-permute-done.refs_1_), channel_id=1, source_target_pairs={{0,8},{8,0},{1,9},{9,1},{2,10},{10,2},{3,11},{11,3},{4,12},{12,4},... | collective-permute-start | bytes 1548296 | tf_op jit(solution)/shard_map/ppermute | solution.py:265
  36.2 0.7 copy-start.6
  36.2 0.7 copy-start.7
  81.4 13.2 %copy-start.2 = (bf16[1,128,128]{2,1,0:T(8,128)(2,1)S(1)}, bf16[1,128,128]{2,1,0:T(8,128)(2,1)}, u32[]{:S(2)}) copy-start(bf16[1,128,128]{2,1,0:T(8,128)(2,1)} %param.16) | copy-start | bytes 98308
  81.4 13.2 %copy-start.3 = (bf16[1,40,128]{2,1,0:T(8,128)(2,1)S(1)}, bf16[1,40,128]{2,1,0:T(8,128)(2,1)}, u32[]{:S(2)}) copy-start(bf16[1,40,128]{2,1,0:T(8,128)(2,1)} %param.15) | copy-start | bytes 30724
  111.5 15.8 %copy-start = (bf16[1,2048,128]{2,1,0:T(8,128)(2,1)S(1)}, bf16[1,2048,128]{2,1,0:T(8,128)(2,1)}, u32[]{:S(2)}) copy-start(bf16[1,2048,128]{2,1,0:T(8,128)(2,1)} %param.19) | copy-start | bytes 1572868

commit v13 on v12

--- a/solution.py
+++ b/solution.py
@@ -84,9 +84,8 @@
     out_ref[NB : NB + 16] = index
 
 
-def project_kernel(pos, wake_ref, *refs):
-    out_ref = refs[4]
-    wake = wake_ref[...].reshape(Z * PH, COLS)
+def select_kernel(pos, *refs):
+    onehot_ref = refs[4]
     codes = []
     for ref in refs[:4]:
         index = ref[NB : NB + 16, 0:NT].astype(F32)
@@ -96,11 +95,17 @@
         codes.append(jnp.where(here, code, -1.0))
     codes = jnp.concatenate(codes + [jnp.zeros((4, NT), F32)], axis=0).T
     pair = lax.broadcasted_iota(jnp.int32, (NT, Z * PH), 1).astype(F32)
+    for r in range(4):
+        onehot_ref[r] = jnp.where(codes[:, r : r + 1] == pair, 1.0, 0.0).astype(BF)
+
+
+def project_kernel(wake_ref, onehot_ref, *refs):
+    out_ref = refs[4]
+    wake = wake_ref[...].reshape(Z * PH, COLS)
     picks = []
     for r, ref in enumerate(refs[:4]):
         table = dot_nt(wake, ref[0:NB]).astype(BF)
-        onehot = jnp.where(codes[:, r : r + 1] == pair, 1.0, 0.0).astype(BF)
-        part = jnp.dot(onehot, table, preferred_element_type=F32)
+        part = jnp.dot(onehot_ref[r], table, preferred_element_type=F32)
         picks.append(part.reshape(PEERS, TS, NB))
     out_ref[...] = jnp.concatenate(picks, axis=1).astype(BF)
 
@@ -265,16 +270,10 @@
     by_both = lax.ppermute(by_yl, "c", swap)
     near, forward, inverse, powers = lax.optimization_barrier((near, forward, inverse, powers))
 
+    sectors = (near, by_yl, by_c, by_both)
+    onehot = call(select_kernel, [(4, NT, Z * PH)], [SMEM] + [VMEM] * 4, pos, *sectors)
     picked = call(
-        project_kernel,
-        [(PEERS, 4 * TS, NB)],
-        [SMEM] + [VMEM] * 5,
-        pos,
-        blocks,
-        near,
-        by_yl,
-        by_c,
-        by_both,
+        project_kernel, [(PEERS, 4 * TS, NB)], [VMEM] * 6, blocks, onehot, *sectors
     )
     parts = lax.all_to_all(picked, PLANE, 0, 0, tiled=True)
     forcing = call(gather_sum_kernel, [(Z, 4 * TS, NB)], [VMEM], parts)

time: 129 us -> 129 us (level)
    pallas_call x9 -> x10, Pallas kernels: 6.51 us -> 6.88 us  [call(): pl.pallas_call(kernel, out_shape=outs, in_specs=specs, out_specs=out_spec...]
  transfers between devices with their start and end apart: 4 -> 4, of which waited for: 1 -> 1; matrix products, arithmetic and copies ran while one was open for 1% -> 1% of each run, Pallas kernels for 0% -> 1%
where the time goes in v13:
time: 129 us; the launch traced here: 128 us
  blocking collectives  84.5 us (66%)
  starting transfers between devices  26 us (20%)
  waiting for transfers between devices  7.84 us (6%)
  Pallas kernels  6.88 us (5%)
  local copies, waits for them, and re-layouts  2.91 us (2%)
    all_to_all x1, blocking collectives, local(): parts = lax.all_to_all(picked, PLANE, 0, 0, tiled=True)  21.7 us
    all_to_all x1, blocking collectives, local(): forcing = lax.all_to_all(forcing, 'z', 0, 0, tiled=True)  18.2 us
    all_to_all x1, starting transfers between devices, local(): blocks = lax.all_to_all(spread, 'z', 0, 0, tiled=True)  15.9 us
    all_to_all x1, blocking collectives, local(): physical = lax.all_to_all(physical, 'z', 0, 0, tiled=True)  15.8 us
    all_to_all x1, blocking collectives, local(): sectoral = lax.all_to_all(sectoral, PLANE, 0, 0, tiled=True)  15.6 us
    all_to_all x1, blocking collectives, local(): harmonic = lax.all_to_all(harmonic, PLANE, 0, 0, tiled=True)  13.2 us
    ppermute x1, waiting for transfers between devices, local(): by_yl = lax.ppermute(near, 'yl', swap)  7.83 us
    pallas_call x10, Pallas kernels, call(): pl.pallas_call(kernel, out_shape=outs, in_specs=specs, out_specs=out_spec...  6.88 us
  transfers between devices with their start and end apart: 4, of which 1 were waited for; matrix products, arithmetic and copies ran while one was open for 1% of the time, Pallas kernels for 1%

profile of v13, /device:TPU:1, one launch (start us, length us, event | category | flops | bytes accessed | tf_op | source)
XLA Modules:
  0.0 128.4 jit_solution(12021147167928039402)
XLA Ops:
  0.0 1.5 %shard_map.111 = bf16[16,8,1792]{2,1,0:T(8,128)(2,1)} custom-call(bf16[8,1792]{1,0:T(8,128)(2,1)} %bitcast.17), custom_call_target="tpu_custom_call" | custom-call | tf_op jit(solution)/shard_map/pallas_call | solution.py:230
  1.6 0.0 copy-start.1
  1.6 0.0 copy-start.5
  1.6 15.9 %all-to-all-start = ((bf16[16,8,1792]{2,1,0:T(8,128)(2,1)}), bf16[16,8,1792]{2,1,0:T(8,128)(2,1)S(1)}, u32[]{:S(2)}, u32[]{:S(2)}) async-start(bf16[16,8,1792]{2,1,0:T(8,128)(2,1)} %shard_map.111), calls=%async_computation | async-start | bytes 917504 | tf_op jit(solution)/shard_map/all_to_all | solution.py:264
  17.5 0.0 copy-start.4
  17.5 0.0 copy-done.1
  17.5 0.0 copy-done.5
  17.5 0.7 copy-done.4
  18.2 3.2 %collective-permute-start = (bf16[144,1792]{1,0:T(8,128)(2,1)S(1)}, bf16[144,1792]{1,0:T(8,128)(2,1)S(1)}, u32[]{:S(2)}, u32[]{:S(2)}) collective-permute-start(bf16[144,1792]{1,0:T(8,128)(2,1)S(1)} %shard_map.109.refs_0_), channel_id=1, source_target_pairs={{0,256},{256,0},{1,257},{257,1},{2,258},{258,2},{3,259},{259,3},{4... | collective-permute-start | bytes 1548296 | tf_op jit(solution)/shard_map/ppermute | solution.py:268
  21.4 3.1 %collective-permute-start.1 = (bf16[144,1792]{1,0:T(8,128)(2,1)S(1)}, bf16[144,1792]{1,0:T(8,128)(2,1)S(1)}, u32[]{:S(2)}, u32[]{:S(2)}) collective-permute-start(bf16[144,1792]{1,0:T(8,128)(2,1)S(1)} %shard_map.109.refs_0_), channel_id=1, source_target_pairs={{0,8},{8,0},{1,9},{9,1},{2,10},{10,2},{3,11},{11,3},{4,12},{12,4},... | collective-permute-start | bytes 1548296 | tf_op jit(solution)/shard_map/ppermute | solution.py:269
  24.6 7.8 %collective-permute-done.refs_1_ = bf16[144,1792]{1,0:T(8,128)(2,1)S(1)} collective-permute-done((bf16[144,1792]{1,0:T(8,128)(2,1)S(1)}, bf16[144,1792]{1,0:T(8,128)(2,1)S(1)}, u32[]{:S(2)}, u32[]{:S(2)}) %collective-permute-start) | collective-permute-done | bytes 516128 | tf_op jit(solution)/shard_map/ppermute | solution.py:268
  32.4 3.8 %collective-permute-start.2 = (bf16[144,1792]{1,0:T(8,128)(2,1)S(1)}, bf16[144,1792]{1,0:T(8,128)(2,1)S(1)}, u32[]{:S(2)}, u32[]{:S(2)}) collective-permute-start(bf16[144,1792]{1,0:T(8,128)(2,1)S(1)} %collective-permute-done.refs_1_), channel_id=1, source_target_pairs={{0,8},{8,0},{1,9},{9,1},{2,10},{10,2},{3,11},{11,3},{4,12},{12,4},... | collective-permute-start | bytes 1548296 | tf_op jit(solution)/shard_map/ppermute | solution.py:270
  36.2 0.0 copy-start.6
  36.2 0.0 copy-start.7
  36.2 0.6 copy-done.6
  36.8 0.0 copy-done.7
  36.9 0.1 shard_map.110.powers_ref
  36.9 0.7 dynamic-slice_bitcast_fusion.1.table_ref
  37.6 0.8 dynamic-slice_bitcast_fusion.table_ref
  38.5 0.1 pad_add_fusion.pos
  38.6 0.0 collective-permute-done.1.refs_2_
  38.6 0.0 collective-permute-done.2.refs_3_
  38.6 0.9 shard_map.112.onehot_ref
  39.5 0.0 all-to-all-done.wake_ref
  39.5 1.6 %shard_map.113 = bf16[32,32,128]{2,1,0:T(8,128)(2,1)S(1)} custom-call(bf16[16,8,1792]{2,1,0:T(8,128)(2,1)S(1)} %all-to-all-done.wake_ref, bf16[4,256,128]{2,1,0:T(8,128)(2,1)S(1)} %shard_map.112.onehot_ref, bf16[144,1792]{1,0:T(8,128)(2,1)S(1)} %shard_map.109.refs_0_, bf16[144,1792]{1,0:T(8,128)(2,1)S(1)} %collective-permute-done.refs_1_, ...), custom_call_target="tpu_custom_call" | custom-call | tf_op jit(solution)/shard_map/pallas_call | solution.py:230
  41.1 21.7 %all_to_all.30.in_ref = bf16[32,32,128]{2,1,0:T(8,128)(2,1)S(1)} all-to-all(bf16[32,32,128]{2,1,0:T(8,128)(2,1)S(1)} %shard_map.113), channel_id=1, replica_groups=mesh['yl'=2,'z'=16,'c'=2,'x'=4,'yh'=2] {'yl','c','x','yh'}, dimensions={0} | all-to-all | bytes 524288 | tf_op jit(solution)/shard_map/all_to_all | solution.py:278
  62.8 18.2 %all_to_all.31.in_ref = bf16[16,32,128]{2,1,0:T(8,128)(2,1)S(1)} all-to-all(bf16[16,32,128]{2,1,0:T(8,128)(2,1)S(1)} %shard_map.114), channel_id=1, replica_groups=mesh['yl'=2,'z'=16,'c'=2,'x'=4,'yh'=2] {'z'}, dimensions={0} | all-to-all | bytes 262144 | tf_op jit(solution)/shard_map/all_to_all | solution.py:280
  81.1 0.2 shard_map.115
  81.2 0.0 copy-start.2
  81.2 0.0 copy-start.3
  81.3 13.2 %all_to_all.32.in_ref = bf16[32,8,128]{2,1,0:T(8,128)(2,1)S(1)} all-to-all(bf16[32,8,128]{2,1,0:T(8,128)(2,1)S(1)} %shard_map.115), channel_id=1, replica_groups=mesh['yl'=2,'z'=16,'c'=2,'x'=4,'yh'=2] {'yl','c','x','yh'}, dimensions={0} | all-to-all | bytes 131072 | tf_op jit(solution)/shard_map/all_to_all | solution.py:282
  94.4 0.0 copy-done.2
  94.4 0.0 copy-done.3
  94.4 1.1 shard_map.116
  95.5 15.8 %all_to_all.33.in_ref = bf16[16,32,128]{2,1,0:T(8,128)(2,1)S(1)} all-to-all(bf16[16,32,128]{2,1,0:T(8,128)(2,1)S(1)} %shard_map.116), channel_id=1, replica_groups=mesh['yl'=2,'z'=16,'c'=2,'x'=4,'yh'=2] {'z'}, dimensions={0} | all-to-all | bytes 262144 | tf_op jit(solution)/shard_map/all_to_all | solution.py:294
  111.3 0.0 copy-start
  111.3 0.2 shard_map.117
  111.5 15.6 %all_to_all.34.in_ref = bf16[32,32,128]{2,1,0:T(8,128)(2,1)S(1)} all-to-all(bf16[32,32,128]{2,1,0:T(8,128)(2,1)S(1)} %shard_map.117), channel_id=1, replica_groups=mesh['yl'=2,'z'=16,'c'=2,'x'=4,'yh'=2] {'yl','c','x','yh'}, dimensions={0} | all-to-all | bytes 524288 | tf_op jit(solution)/shard_map/all_to_all | solution.py:296
  127.1 0.0 copy-done
  127.1 1.3 shard_map.118
  (2 shorter events, 0.1 us)
Async XLA Ops:
  1.6 15.9 %copy-start.1 = (bf16[1,128,1792]{2,1,0:T(8,128)(2,1)S(1)}, bf16[1,128,1792]{2,1,0:T(8,128)(2,1)}, u32[]{:S(2)}) copy-start(bf16[1,128,1792]{2,1,0:T(8,128)(2,1)} %param.12) | copy-start | bytes 1376260
  1.6 15.9 %copy-start.5 = (s32[1,256]{1,0:T(1,128)S(1)}, s32[1,256]{1,0:T(1,128)}, u32[]{:S(2)}) copy-start(s32[1,256]{1,0:T(1,128)} %phase_ref.1) | copy-start | bytes 3076
  1.6 37.9 %all-to-all-start = ((bf16[16,8,1792]{2,1,0:T(8,128)(2,1)}), bf16[16,8,1792]{2,1,0:T(8,128)(2,1)S(1)}, u32[]{:S(2)}, u32[]{:S(2)}) async-start(bf16[16,8,1792]{2,1,0:T(8,128)(2,1)} %shard_map.111), calls=%async_computation | async-start | bytes 917504 | tf_op jit(solution)/shard_map/all_to_all | solution.py:264
  17.5 0.7 copy-start.4
  18.2 14.2 %collective-permute-start = (bf16[144,1792]{1,0:T(8,128)(2,1)S(1)}, bf16[144,1792]{1,0:T(8,128)(2,1)S(1)}, u32[]{:S(2)}, u32[]{:S(2)}) collective-permute-start(bf16[144,1792]{1,0:T(8,128)(2,1)S(1)} %shard_map.109.refs_0_), channel_id=1, source_target_pairs={{0,256},{256,0},{1,257},{257,1},{2,258},{258,2},{3,259},{259,3},{4... | collective-permute-start | bytes 1548296 | tf_op jit(solution)/shard_map/ppermute | solution.py:268
  21.4 17.2 %collective-permute-start.1 = (bf16[144,1792]{1,0:T(8,128)(2,1)S(1)}, bf16[144,1792]{1,0:T(8,128)(2,1)S(1)}, u32[]{:S(2)}, u32[]{:S(2)}) collective-permute-start(bf16[144,1792]{1,0:T(8,128)(2,1)S(1)} %shard_map.109.refs_0_), channel_id=1, source_target_pairs={{0,8},{8,0},{1,9},{9,1},{2,10},{10,2},{3,11},{11,3},{4,12},{12,4},... | collective-permute-start | bytes 1548296 | tf_op jit(solution)/shard_map/ppermute | solution.py:269
  32.4 6.2 %collective-permute-start.2 = (bf16[144,1792]{1,0:T(8,128)(2,1)S(1)}, bf16[144,1792]{1,0:T(8,128)(2,1)S(1)}, u32[]{:S(2)}, u32[]{:S(2)}) collective-permute-start(bf16[144,1792]{1,0:T(8,128)(2,1)S(1)} %collective-permute-done.refs_1_), channel_id=1, source_target_pairs={{0,8},{8,0},{1,9},{9,1},{2,10},{10,2},{3,11},{11,3},{4,12},{12,4},... | collective-permute-start | bytes 1548296 | tf_op jit(solution)/shard_map/ppermute | solution.py:270
  36.2 0.7 copy-start.6
  36.2 0.7 copy-start.7
  81.2 13.2 %copy-start.2 = (bf16[1,128,128]{2,1,0:T(8,128)(2,1)S(1)}, bf16[1,128,128]{2,1,0:T(8,128)(2,1)}, u32[]{:S(2)}) copy-start(bf16[1,128,128]{2,1,0:T(8,128)(2,1)} %param.16) | copy-start | bytes 98308
  81.2 13.2 %copy-start.3 = (bf16[1,40,128]{2,1,0:T(8,128)(2,1)S(1)}, bf16[1,40,128]{2,1,0:T(8,128)(2,1)}, u32[]{:S(2)}) copy-start(bf16[1,40,128]{2,1,0:T(8,128)(2,1)} %param.15) | copy-start | bytes 30724
  111.3 15.8 %copy-start = (bf16[1,2048,128]{2,1,0:T(8,128)(2,1)S(1)}, bf16[1,2048,128]{2,1,0:T(8,128)(2,1)}, u32[]{:S(2)}) copy-start(bf16[1,2048,128]{2,1,0:T(8,128)(2,1)} %param.19) | copy-start | bytes 1572868

commit v14 on v13

--- a/solution.py
+++ b/solution.py
@@ -102,10 +102,11 @@
 def project_kernel(wake_ref, onehot_ref, *refs):
     out_ref = refs[4]
     wake = wake_ref[...].reshape(Z * PH, COLS)
+    basis = jnp.concatenate([ref[0:NB] for ref in refs[:4]], axis=0)
+    table = dot_nt(basis, wake).astype(BF)
     picks = []
-    for r, ref in enumerate(refs[:4]):
-        table = dot_nt(wake, ref[0:NB]).astype(BF)
-        part = jnp.dot(onehot_ref[r], table, preferred_element_type=F32)
+    for r in range(4):
+        part = dot_nt(onehot_ref[r], table[r * NB : (r + 1) * NB])
         picks.append(part.reshape(PEERS, TS, NB))
     out_ref[...] = jnp.concatenate(picks, axis=1).astype(BF)
 

time: 129 us -> 128 us (level)
  no operation moved by 1% of the time
where the time goes in v14:
time: 128 us
  blocking collectives  84.5 us (66%)
  starting transfers between devices  26 us (20%)
  waiting for transfers between devices  7.84 us (6%)
  Pallas kernels  6.18 us (5%)
  local copies, waits for them, and re-layouts  2.91 us (2%)
    all_to_all x1, blocking collectives, local(): parts = lax.all_to_all(picked, PLANE, 0, 0, tiled=True)  21.7 us
    all_to_all x1, blocking collectives, local(): forcing = lax.all_to_all(forcing, 'z', 0, 0, tiled=True)  18.2 us
    all_to_all x1, starting transfers between devices, local(): blocks = lax.all_to_all(spread, 'z', 0, 0, tiled=True)  15.9 us
    all_to_all x1, blocking collectives, local(): physical = lax.all_to_all(physical, 'z', 0, 0, tiled=True)  15.8 us
    all_to_all x1, blocking collectives, local(): sectoral = lax.all_to_all(sectoral, PLANE, 0, 0, tiled=True)  15.6 us
    all_to_all x1, blocking collectives, local(): harmonic = lax.all_to_all(harmonic, PLANE, 0, 0, tiled=True)  13.2 us
    ppermute x1, waiting for transfers between devices, local(): by_yl = lax.ppermute(near, 'yl', swap)  7.83 us
    pallas_call x10, Pallas kernels, call(): pl.pallas_call(kernel, out_shape=outs, in_specs=specs, out_specs=out_spec...  6.18 us
  transfers between devices with their start and end apart: 4, of which 1 were waited for; matrix products, arithmetic and copies ran while one was open for 1% of the time, Pallas kernels for 1%

profile of v14, /device:TPU:1, one launch (start us, length us, event | category | flops | bytes accessed | tf_op | source)
XLA Modules:
  0.0 127.7 jit_solution(3299841895448032349)
XLA Ops:
  0.0 1.5 %shard_map.111 = bf16[16,8,1792]{2,1,0:T(8,128)(2,1)} custom-call(bf16[8,1792]{1,0:T(8,128)(2,1)} %bitcast.17), custom_call_target="tpu_custom_call" | custom-call | tf_op jit(solution)/shard_map/pallas_call | solution.py:231
  1.6 0.0 copy-start.1
  1.6 0.0 copy-start.5
  1.6 15.9 %all-to-all-start = ((bf16[16,8,1792]{2,1,0:T(8,128)(2,1)}), bf16[16,8,1792]{2,1,0:T(8,128)(2,1)S(1)}, u32[]{:S(2)}, u32[]{:S(2)}) async-start(bf16[16,8,1792]{2,1,0:T(8,128)(2,1)} %shard_map.111), calls=%async_computation | async-start | bytes 917504 | tf_op jit(solution)/shard_map/all_to_all | solution.py:265
  17.5 0.0 copy-start.4
  17.5 0.0 copy-done.1
  17.5 0.0 copy-done.5
  17.5 0.7 copy-done.4
  18.2 3.2 %collective-permute-start = (bf16[144,1792]{1,0:T(8,128)(2,1)S(1)}, bf16[144,1792]{1,0:T(8,128)(2,1)S(1)}, u32[]{:S(2)}, u32[]{:S(2)}) collective-permute-start(bf16[144,1792]{1,0:T(8,128)(2,1)S(1)} %shard_map.109.refs_0_), channel_id=1, source_target_pairs={{0,256},{256,0},{1,257},{257,1},{2,258},{258,2},{3,259},{259,3},{4... | collective-permute-start | bytes 1548296 | tf_op jit(solution)/shard_map/ppermute | solution.py:269
  21.4 3.1 %collective-permute-start.1 = (bf16[144,1792]{1,0:T(8,128)(2,1)S(1)}, bf16[144,1792]{1,0:T(8,128)(2,1)S(1)}, u32[]{:S(2)}, u32[]{:S(2)}) collective-permute-start(bf16[144,1792]{1,0:T(8,128)(2,1)S(1)} %shard_map.109.refs_0_), channel_id=1, source_target_pairs={{0,8},{8,0},{1,9},{9,1},{2,10},{10,2},{3,11},{11,3},{4,12},{12,4},... | collective-permute-start | bytes 1548296 | tf_op jit(solution)/shard_map/ppermute | solution.py:270
  24.6 7.8 %collective-permute-done.refs_1_ = bf16[144,1792]{1,0:T(8,128)(2,1)S(1)} collective-permute-done((bf16[144,1792]{1,0:T(8,128)(2,1)S(1)}, bf16[144,1792]{1,0:T(8,128)(2,1)S(1)}, u32[]{:S(2)}, u32[]{:S(2)}) %collective-permute-start) | collective-permute-done | bytes 516128 | tf_op jit(solution)/shard_map/ppermute | solution.py:269
  32.4 3.8 %collective-permute-start.2 = (bf16[144,1792]{1,0:T(8,128)(2,1)S(1)}, bf16[144,1792]{1,0:T(8,128)(2,1)S(1)}, u32[]{:S(2)}, u32[]{:S(2)}) collective-permute-start(bf16[144,1792]{1,0:T(8,128)(2,1)S(1)} %collective-permute-done.refs_1_), channel_id=1, source_target_pairs={{0,8},{8,0},{1,9},{9,1},{2,10},{10,2},{3,11},{11,3},{4,12},{12,4},... | collective-permute-start | bytes 1548296 | tf_op jit(solution)/shard_map/ppermute | solution.py:271
  36.2 0.0 copy-start.6
  36.2 0.0 copy-start.7
  36.2 0.6 copy-done.6
  36.8 0.0 copy-done.7
  36.9 0.1 shard_map.110.powers_ref
  36.9 0.7 dynamic-slice_bitcast_fusion.1.table_ref
  37.6 0.8 dynamic-slice_bitcast_fusion.table_ref
  38.5 0.1 pad_add_fusion.pos
  38.6 0.0 collective-permute-done.1.refs_2_
  38.6 0.0 collective-permute-done.2.refs_3_
  38.6 0.9 shard_map.112.onehot_ref
  39.5 0.0 all-to-all-done.wake_ref
  39.5 0.9 shard_map.113
  40.4 21.7 %all_to_all.30.in_ref = bf16[32,32,128]{2,1,0:T(8,128)(2,1)S(1)} all-to-all(bf16[32,32,128]{2,1,0:T(8,128)(2,1)S(1)} %shard_map.113), channel_id=1, replica_groups=mesh['yl'=2,'z'=16,'c'=2,'x'=4,'yh'=2] {'yl','c','x','yh'}, dimensions={0} | all-to-all | bytes 524288 | tf_op jit(solution)/shard_map/all_to_all | solution.py:279
  62.1 18.2 %all_to_all.31.in_ref = bf16[16,32,128]{2,1,0:T(8,128)(2,1)S(1)} all-to-all(bf16[16,32,128]{2,1,0:T(8,128)(2,1)S(1)} %shard_map.114), channel_id=1, replica_groups=mesh['yl'=2,'z'=16,'c'=2,'x'=4,'yh'=2] {'z'}, dimensions={0} | all-to-all | bytes 262144 | tf_op jit(solution)/shard_map/all_to_all | solution.py:281
  80.4 0.2 shard_map.115
  80.5 0.0 copy-start.2
  80.6 0.0 copy-start.3
  80.6 13.2 %all_to_all.32.in_ref = bf16[32,8,128]{2,1,0:T(8,128)(2,1)S(1)} all-to-all(bf16[32,8,128]{2,1,0:T(8,128)(2,1)S(1)} %shard_map.115), channel_id=1, replica_groups=mesh['yl'=2,'z'=16,'c'=2,'x'=4,'yh'=2] {'yl','c','x','yh'}, dimensions={0} | all-to-all | bytes 131072 | tf_op jit(solution)/shard_map/all_to_all | solution.py:283
  93.7 0.0 copy-done.2
  93.7 0.0 copy-done.3
  93.7 1.1 shard_map.116
  94.8 15.8 %all_to_all.33.in_ref = bf16[16,32,128]{2,1,0:T(8,128)(2,1)S(1)} all-to-all(bf16[16,32,128]{2,1,0:T(8,128)(2,1)S(1)} %shard_map.116), channel_id=1, replica_groups=mesh['yl'=2,'z'=16,'c'=2,'x'=4,'yh'=2] {'z'}, dimensions={0} | all-to-all | bytes 262144 | tf_op jit(solution)/shard_map/all_to_all | solution.py:295
  110.6 0.0 copy-start
  110.6 0.2 shard_map.117
  110.8 15.6 %all_to_all.34.in_ref = bf16[32,32,128]{2,1,0:T(8,128)(2,1)S(1)} all-to-all(bf16[32,32,128]{2,1,0:T(8,128)(2,1)S(1)} %shard_map.117), channel_id=1, replica_groups=mesh['yl'=2,'z'=16,'c'=2,'x'=4,'yh'=2] {'yl','c','x','yh'}, dimensions={0} | all-to-all | bytes 524288 | tf_op jit(solution)/shard_map/all_to_all | solution.py:297
  126.4 0.0 copy-done
  126.4 1.3 shard_map.118
  (2 shorter events, 0.1 us)
Async XLA Ops:
  1.6 15.9 %copy-start.1 = (bf16[1,128,1792]{2,1,0:T(8,128)(2,1)S(1)}, bf16[1,128,1792]{2,1,0:T(8,128)(2,1)}, u32[]{:S(2)}) copy-start(bf16[1,128,1792]{2,1,0:T(8,128)(2,1)} %param.12) | copy-start | bytes 1376260
  1.6 15.9 %copy-start.5 = (s32[1,256]{1,0:T(1,128)S(1)}, s32[1,256]{1,0:T(1,128)}, u32[]{:S(2)}) copy-start(s32[1,256]{1,0:T(1,128)} %phase_ref.1) | copy-start | bytes 3076
  1.6 37.9 %all-to-all-start = ((bf16[16,8,1792]{2,1,0:T(8,128)(2,1)}), bf16[16,8,1792]{2,1,0:T(8,128)(2,1)S(1)}, u32[]{:S(2)}, u32[]{:S(2)}) async-start(bf16[16,8,1792]{2,1,0:T(8,128)(2,1)} %shard_map.111), calls=%async_computation | async-start | bytes 917504 | tf_op jit(solution)/shard_map/all_to_all | solution.py:265
  17.5 0.7 copy-start.4
  18.2 14.2 %collective-permute-start = (bf16[144,1792]{1,0:T(8,128)(2,1)S(1)}, bf16[144,1792]{1,0:T(8,128)(2,1)S(1)}, u32[]{:S(2)}, u32[]{:S(2)}) collective-permute-start(bf16[144,1792]{1,0:T(8,128)(2,1)S(1)} %shard_map.109.refs_0_), channel_id=1, source_target_pairs={{0,256},{256,0},{1,257},{257,1},{2,258},{258,2},{3,259},{259,3},{4... | collective-permute-start | bytes 1548296 | tf_op jit(solution)/shard_map/ppermute | solution.py:269
  21.4 17.2 %collective-permute-start.1 = (bf16[144,1792]{1,0:T(8,128)(2,1)S(1)}, bf16[144,1792]{1,0:T(8,128)(2,1)S(1)}, u32[]{:S(2)}, u32[]{:S(2)}) collective-permute-start(bf16[144,1792]{1,0:T(8,128)(2,1)S(1)} %shard_map.109.refs_0_), channel_id=1, source_target_pairs={{0,8},{8,0},{1,9},{9,1},{2,10},{10,2},{3,11},{11,3},{4,12},{12,4},... | collective-permute-start | bytes 1548296 | tf_op jit(solution)/shard_map/ppermute | solution.py:270
  32.4 6.2 %collective-permute-start.2 = (bf16[144,1792]{1,0:T(8,128)(2,1)S(1)}, bf16[144,1792]{1,0:T(8,128)(2,1)S(1)}, u32[]{:S(2)}, u32[]{:S(2)}) collective-permute-start(bf16[144,1792]{1,0:T(8,128)(2,1)S(1)} %collective-permute-done.refs_1_), channel_id=1, source_target_pairs={{0,8},{8,0},{1,9},{9,1},{2,10},{10,2},{3,11},{11,3},{4,12},{12,4},... | collective-permute-start | bytes 1548296 | tf_op jit(solution)/shard_map/ppermute | solution.py:271
  36.2 0.7 copy-start.6
  36.2 0.7 copy-start.7
  80.5 13.2 %copy-start.2 = (bf16[1,128,128]{2,1,0:T(8,128)(2,1)S(1)}, bf16[1,128,128]{2,1,0:T(8,128)(2,1)}, u32[]{:S(2)}) copy-start(bf16[1,128,128]{2,1,0:T(8,128)(2,1)} %param.16) | copy-start | bytes 98308
  80.6 13.2 %copy-start.3 = (bf16[1,40,128]{2,1,0:T(8,128)(2,1)S(1)}, bf16[1,40,128]{2,1,0:T(8,128)(2,1)}, u32[]{:S(2)}) copy-start(bf16[1,40,128]{2,1,0:T(8,128)(2,1)} %param.15) | copy-start | bytes 30724
  110.6 15.8 %copy-start = (bf16[1,2048,128]{2,1,0:T(8,128)(2,1)S(1)}, bf16[1,2048,128]{2,1,0:T(8,128)(2,1)}, u32[]{:S(2)}) copy-start(bf16[1,2048,128]{2,1,0:T(8,128)(2,1)} %param.19) | copy-start | bytes 1572868
